TPU v7x, 32 devices: a whole 2x2x4 slice. The times are simulated.
32 devices in a mesh: grp: 4 (over y, core), emb: 8 (over z, x).
Axes of the slice: x: 2, y: 2, z: 4, core: 2. Of those that a mesh axis runs over, the one named last changes fastest.
Arguments:
- table_window: bfloat16 [16384, 128], P('emb'), may hold values from -3 to 3
- dense_part: bfloat16 [4096, 128], P(('grp', 'emb')), may hold values from -6 to 6
- bag_rows: int32 [4096, 26, 8], P(('grp', 'emb')), may hold values from 0 to 2047
- bag_lengths: int32 [4096, 26], P(('grp', 'emb')), may hold values from 1 to 8
- bag_owner: int32 [4096, 26, 1], P(('grp', 'emb')), may hold values from 0 to 7; in each aligned block of 3328 rows (0 to 3327, 3328 to 6655, ..., all dimensions but the last counted through in order) at most 624 rows name the same one
- labels: int32 [4096], P(('grp', 'emb')), may hold values 0 or 1
- sample_weight: float32 [4096], P(('grp', 'emb')), may hold values from 0.005 to 1.5
- down_w: bfloat16 [3456, 512], replicated, may hold values from -0.109375 to 0.109375
- up_w: bfloat16 [512, 3456], replicated, may hold values from -0.25 to 0.25
- cross_bias: float32 [3456], replicated, may hold values from -3 to 3
- head_w: float32 [3456], replicated, may hold values from -0.109375 to 0.109375
Outputs:
- row_grad: float32 [16384, 128], P('emb')
- head_grad: float32 [3456], replicated
- bias_grad: float32 [3456], replicated
- dense_grad: bfloat16 [4096, 128], P(('grp', 'emb'))
Inputs may be any that keep to these rules, and one draw needn't show every extreme that they name: `bag_owner`: among the bags of the samples of one device (aligned blocks of 128 samples), at most 624 have one owner, and some owner has exactly 624.
All inputs are finite; a program needn't handle non-finite values. No bound on the sum of `labels` on one device may be relied on, other than what follows from the above.
Results may differ from a plain program's by a relative error of at most 0.0045.
The roundings to bfloat16 on the way count: a program that leaves them out, or rounds other values in their place, can miss the bound.
Values may be sent and summed in bfloat16 or wider, within the bound.
No kernel may reach another device: no remote copies, remote signals or barrier semaphores. Data moves between devices by JAX's collectives and lax.ppermute only.
A program may use at most 128 MiB of HBM per device.

v0:
```python
import jax
import jax.numpy as jnp
from jax import lax
from jax.sharding import PartitionSpec as P


def body(
    table_window,
    dense_part,
    bag_rows,
    bag_lengths,
    bag_owner,
    labels,
    sample_weight,
    down_w,
    up_w,
    cross_bias,
    head_w,
):
    owners = lax.axis_size("emb")
    samples = dense_part.shape[0]
    width = dense_part.shape[1]
    tables = bag_rows.shape[1]
    hot = bag_rows.shape[2]
    local_rows = table_window.shape[0]
    bags = samples * tables
    capacity = bags * 3 // (2 * owners)
    owner = bag_owner.reshape(bags)
    owner_hits = (owner[:, None] == jnp.arange(owners, dtype=jnp.int32)[None, :]).astype(jnp.int32)
    ranks = jnp.cumsum(owner_hits, axis=0) - 1
    slot = jnp.sum(ranks * owner_hits, axis=1)
    position = owner * capacity + slot
    live = jnp.arange(hot, dtype=jnp.int32)[None, None, :] < bag_lengths[:, :, None]
    entries = jnp.where(live, bag_rows, -1).reshape(bags, hot)
    requests = jnp.full((owners * capacity, hot), -1, jnp.int32).at[position].set(entries)
    requests = requests.reshape(owners, capacity, hot)
    received = lax.all_to_all(requests, "emb", split_axis=0, concat_axis=0, tiled=True)
    count = received.shape[1]
    flat = received.reshape(owners * count, hot)
    summed = jnp.zeros((owners * count, width), jnp.float32)
    for pool_entry in range(hot):
        pool_index = flat[:, pool_entry]
        pool_valid = pool_index >= 0
        picked = table_window[jnp.where(pool_valid, pool_index, 0)].astype(jnp.float32)
        summed = summed + jnp.where(pool_valid[:, None], picked, 0.0)
    returned = lax.all_to_all(
        summed.astype(jnp.bfloat16).reshape(owners, count, width),
        "emb",
        split_axis=0,
        concat_axis=0,
        tiled=True,
    )
    pooled = returned.reshape(owners * capacity, width)[position].reshape(samples, tables * width)
    x0 = jnp.concatenate([dense_part, pooled], axis=1)
    low = jnp.dot(x0, down_w, preferred_element_type=jnp.float32).astype(jnp.bfloat16)
    cross = jnp.dot(low, up_w, preferred_element_type=jnp.float32) + cross_bias[None, :]
    x0f = x0.astype(jnp.float32)
    x1 = x0f * cross + x0f
    logit = jnp.dot(x1, head_w, precision=lax.Precision.HIGHEST)
    dlogit = sample_weight * (jax.nn.sigmoid(logit) - labels.astype(jnp.float32))
    d_x1 = dlogit[:, None] * head_w[None, :]
    head_part = jnp.dot(dlogit, x1, precision=lax.Precision.HIGHEST)
    bias_part = jnp.sum(d_x1 * x0f, axis=0)
    d_cross = (d_x1 * x0f).astype(jnp.bfloat16)
    d_low = jnp.dot(d_cross, up_w.T, preferred_element_type=jnp.float32).astype(jnp.bfloat16)
    d_x0 = d_x1 * (cross + 1.0) + jnp.dot(d_low, down_w.T, preferred_element_type=jnp.float32)
    dense_grad = d_x0[:, :width].astype(jnp.bfloat16)
    d_pooled = d_x0[:, width:].astype(jnp.bfloat16).reshape(bags, width)
    outgoing = jnp.zeros((owners * capacity, width), jnp.bfloat16).at[position].set(d_pooled)
    incoming = lax.all_to_all(
        outgoing.reshape(owners, capacity, width), "emb", split_axis=0, concat_axis=0, tiled=True
    )
    incoming_f = incoming.reshape(owners * capacity, width).astype(jnp.float32)
    held_flat = received.reshape(owners * capacity, hot)
    row_part = jnp.zeros((local_rows, width), jnp.float32)
    for entry in range(hot):
        index = held_flat[:, entry]
        valid = index >= 0
        row_part = row_part.at[jnp.where(valid, index, 0)].add(
            jnp.where(valid[:, None], incoming_f, 0.0)
        )
    row_grad = lax.psum(row_part, "grp")
    head_grad, bias_grad = lax.psum((head_part, bias_part), ("grp", "emb"))
    return (row_grad, head_grad, bias_grad, dense_grad)


def solution(mesh):
    in_specs = (
        P("emb", None),
        P(("grp", "emb"), None),
        P(("grp", "emb"), None, None),
        P(("grp", "emb"), None),
        P(("grp", "emb"), None, None),
        P(("grp", "emb")),
        P(("grp", "emb")),
        P(),
        P(),
        P(),
        P(),
    )
    out_specs = (P("emb", None), P(), P(), P(("grp", "emb"), None))
    return jax.shard_map(body, mesh=mesh, in_specs=in_specs, out_specs=out_specs, check_vma=False)
```

profile of v0, /device:TPU:0, one launch (start us, length us, event | category | flops | bytes accessed | tf_op | source)
XLA Modules:
  0.0 671.5 jit_solution(3418036900185222025)
XLA Ops:
  7.2 1.6 copy.33
  8.8 1.6 eq.29
  12.7 1.4 fusion.57
  14.0 5.2 reduce-window.6
  19.3 1.8 slice_reduce_fusion
  21.1 1.5 reduce-window.9
  22.5 1.6 add_bitcast_fusion
  24.2 1.4 copy.32
  25.6 1.6 mul.47
  27.2 1.5 fusion.60
  28.7 1.9 copy.35
  30.6 1.9 reshape.243
  32.6 2.6 copy.36
  37.0 15.1 %scatter_custom_fusion = s32[4992,8]{1,0:T(8,128)} fusion(s32[3328]{0:T(1024)S(1)} %fusion.69, s32[3328,8]{1,0:T(8,128)} %copy.36, s32[]{:T(128)} %constant.9.clone.1), kind=kCustom, calls=%fused_computation.67 | custom fusion | bytes 160256 | tf_op jit(solution)/shard_map/scatter | solution.py:35
  52.0 3.1 copy.37
  55.1 14.8 %all_to_all.15 = s32[8,624,8]{1,2,0:T(8,128)S(1)} all-to-all(s32[8,624,8]{1,2,0:T(8,128)} %copy.37), channel_id=1, replica_groups=mesh['grp'=4,'emb'=8] {'emb'}, dimensions={0} | all-to-all | bytes 319488 | tf_op jit(solution)/shard_map/all_to_all | solution.py:37
  70.6 1.7 reshape.153
  72.3 3.0 fusion.62
  75.4 2.9 compare_reduce_fusion.7
  78.9 12.2 %gather_fusion = bf16[4992,128]{1,0:T(8,128)(2,1)} fusion(bf16[2048,128]{1,0:T(8,128)(2,1)} %param.11, s32[5120]{0:T(1024)} %get-tuple-element.29), kind=kCustom, calls=%fused_computation | custom fusion | bytes 2575872 | tf_op jit(solution)/shard_map/gather | solution.py:44
  91.1 12.2 %gather_fusion.1 = bf16[4992,128]{1,0:T(8,128)(2,1)} fusion(bf16[2048,128]{1,0:T(8,128)(2,1)} %param.11, s32[5120]{0:T(1024)} %get-tuple-element.28), kind=kCustom, calls=%fused_computation.1 | custom fusion | bytes 2575872 | tf_op jit(solution)/shard_map/gather | solution.py:44
  103.3 1.4 pad_clamp_fusion.4
  104.6 12.2 %gather_fusion.2 = bf16[4992,128]{1,0:T(8,128)(2,1)} fusion(bf16[2048,128]{1,0:T(8,128)(2,1)} %param.11, s32[5120]{0:T(1024)} %get-tuple-element.27), kind=kCustom, calls=%fused_computation.2 | custom fusion | bytes 2575872 | tf_op jit(solution)/shard_map/gather | solution.py:44
  116.8 12.2 %gather_fusion.3 = bf16[4992,128]{1,0:T(8,128)(2,1)} fusion(bf16[2048,128]{1,0:T(8,128)(2,1)} %param.11, s32[5120]{0:T(1024)} %get-tuple-element.26), kind=kCustom, calls=%fused_computation.3 | custom fusion | bytes 2575872 | tf_op jit(solution)/shard_map/gather | solution.py:44
  129.0 1.4 pad_clamp_fusion.2
  130.4 12.2 %gather_fusion.4 = bf16[4992,128]{1,0:T(8,128)(2,1)} fusion(bf16[2048,128]{1,0:T(8,128)(2,1)} %param.11, s32[5120]{0:T(1024)} %get-tuple-element.25), kind=kCustom, calls=%fused_computation.4 | custom fusion | bytes 2575872 | tf_op jit(solution)/shard_map/gather | solution.py:44
  142.5 12.2 %gather_fusion.5 = bf16[4992,128]{1,0:T(8,128)(2,1)} fusion(bf16[2048,128]{1,0:T(8,128)(2,1)} %param.11, s32[5120]{0:T(1024)} %get-tuple-element.24), kind=kCustom, calls=%fused_computation.5 | custom fusion | bytes 2575872 | tf_op jit(solution)/shard_map/gather | solution.py:44
  154.7 1.4 pad_clamp_fusion
  156.1 12.2 %gather_fusion.6 = bf16[4992,128]{1,0:T(8,128)(2,1)} fusion(bf16[2048,128]{1,0:T(8,128)(2,1)} %param.11, s32[5120]{0:T(1024)} %get-tuple-element.23), kind=kCustom, calls=%fused_computation.6 | custom fusion | bytes 2575872 | tf_op jit(solution)/shard_map/gather | solution.py:44
  168.2 12.2 %gather_fusion.7 = bf16[4992,128]{1,0:T(8,128)(2,1)} fusion(bf16[2048,128]{1,0:T(8,128)(2,1)} %param.11, s32[5120]{0:T(1024)} %get-tuple-element.22), kind=kCustom, calls=%fused_computation.7 | custom fusion | bytes 2575872 | tf_op jit(solution)/shard_map/gather | solution.py:44
  180.4 1.4 broadcast_in_dim.213
  181.8 1.4 broadcast_in_dim.216
  183.1 1.4 broadcast_in_dim.218
  184.5 1.4 broadcast_in_dim.220
  185.9 1.4 broadcast_in_dim.222
  187.3 1.4 broadcast_in_dim.224
  189.4 12.4 %fusion.10 = bf16[8,624,128]{2,1,0:T(8,128)(2,1)} fusion(bf16[8,624,128]{2,1,0:T(8,128)(2,1)} %bitcast.86, bf16[8,624,128]{2,1,0:T(8,128)(2,1)} %bitcast.85, bf16[8,624,128]{2,1,0:T(8,128)(2,1)} %bitcast.84, bf16[8,624,128]{2,1,0:T(8,128)(2,1)} %bitcast.83, bf16[8,624,128]{2,1,0:T(8,128)(2,1)} %bitcast.82, bf16[8,624,128]{2,1,0:T(8,128)(2,1)} %bitcast.81, ...), kind=kLoop, calls=%fused_computation.41 | loop fusion | flops 15335424 | bytes 11541504 | tf_op jit(solution)/shard_map/convert_element_type | solution.py:47
  201.8 4.3 all-to-all-start.1
  206.9 1.3 pad_clamp_fusion.8
  208.3 1.4 constant_dynamic-update-slice_fusion.1
  209.6 26.2 %all-to-all-done.1 = bf16[8,624,128]{2,1,0:T(8,128)(2,1)} async-done(((bf16[8,624,128]{2,1,0:T(8,128)(2,1)}), bf16[8,624,128]{2,1,0:T(8,128)(2,1)}, u32[]{:S(2)}, u32[]{:S(2)}) %all-to-all-start.1) | async-done | bytes 1277984 | tf_op jit(solution)/shard_map/all_to_all | solution.py:46
  235.8 9.2 %gather_fusion.8 = bf16[3328,128]{1,0:T(8,128)(2,1)} fusion(bf16[4992,128]{1,0:T(8,128)(2,1)} %bitcast.10, s32[4096]{0:T(1024)} %pad_clamp_fusion.8), kind=kCustom, calls=%fused_computation.8 | custom fusion | bytes 1717248 | tf_op jit(solution)/shard_map/gather | solution.py:53
  245.1 2.8 reshape.155
  247.8 2.1 constant_dynamic-update-slice_fusion
  250.0 4.7 convolution_add_fusion.1
  254.7 3.9 fusion.46
  258.6 6.1 fusion
  264.7 2.1 slice.85
  266.8 2.9 reshape.251
  269.7 14.9 %scatter_custom_fusion.1 = bf16[4992,128]{1,0:T(8,128)(2,1)} fusion(s32[3328]{0:T(1024)} %copy-done.5, bf16[3328,128]{1,0:T(8,128)(2,1)} %reshape.251, bf16[]{:T(256)} %constant.14.clone.1), kind=kCustom, calls=%fused_computation.91 | custom fusion | bytes 1278464 | tf_op jit(solution)/shard_map/scatter | solution.py:69
  284.5 34.6 %all_to_all.16 = bf16[8,624,128]{2,1,0:T(8,128)(2,1)} all-to-all(bf16[8,624,128]{2,1,0:T(8,128)(2,1)} %bitcast.78), channel_id=1, replica_groups=mesh['grp'=4,'emb'=8] {'emb'}, dimensions={0} | all-to-all | bytes 2555904 | tf_op jit(solution)/shard_map/all_to_all | solution.py:70
  319.1 33.4 %scatter_custom_fusion.2 = f32[2048,128]{1,0:T(8,128)} fusion(s32[4992]{0:T(1024)} %copy-done.3, bf16[4992,128]{1,0:T(8,128)(2,1)} %bitcast.69, f32[]{:T(128)} %constant.8.clone.1, pred[4992]{0:T(1024)(128)(4,1)} %get-tuple-element.4), kind=kCustom, calls=%fused_computation.31 | custom fusion | flops 1916928 | bytes 2332672 | tf_op jit(solution)/shard_map/scatter-add | solution.py:79
  352.5 34.6 %scatter_custom_fusion.3 = f32[2048,128]{1,0:T(8,128)} fusion(f32[2048,128]{1,0:T(8,128)} %scatter_custom_fusion.2, s32[4992]{0:T(1024)} %copy-done.2, bf16[4992,128]{1,0:T(8,128)(2,1)} %bitcast.70, f32[]{:T(128)} %constant.8.clone.1, pred[4992]{0:T(1024)(128)(4,1)} %get-tuple-element.11), kind=kCustom, calls=%fused_computation.32 | custom fusion | flops 1916928 | bytes 2332160 | tf_op jit(solution)/shard_map/scatter-add | solution.py:79
  387.0 34.6 %scatter_custom_fusion.4 = f32[2048,128]{1,0:T(8,128)} fusion(f32[2048,128]{1,0:T(8,128)} %scatter_custom_fusion.3, s32[4992]{0:T(1024)} %get-tuple-element.14, bf16[4992,128]{1,0:T(8,128)(2,1)} %bitcast.71, f32[]{:T(128)} %constant.8.clone.1, pred[4992]{0:T(1024)(128)(4,1)} %get-tuple-element.10), kind=kCustom, calls=%fused_computation.33 | custom fusion | flops 1916928 | bytes 2332160 | tf_op jit(solution)/shard_map/scatter-add | solution.py:79
  421.6 34.8 %scatter_custom_fusion.5 = f32[2048,128]{1,0:T(8,128)} fusion(f32[2048,128]{1,0:T(8,128)} %scatter_custom_fusion.4, s32[4992]{0:T(1024)} %get-tuple-element.15, bf16[4992,128]{1,0:T(8,128)(2,1)} %bitcast.72, f32[]{:T(128)} %constant.8.clone.1, pred[4992]{0:T(1024)(128)(4,1)} %get-tuple-element.9), kind=kCustom, calls=%fused_computation.34 | custom fusion | flops 1916928 | bytes 2332160 | tf_op jit(solution)/shard_map/scatter-add | solution.py:79
  456.4 34.6 %scatter_custom_fusion.6 = f32[2048,128]{1,0:T(8,128)} fusion(f32[2048,128]{1,0:T(8,128)} %scatter_custom_fusion.5, s32[4992]{0:T(1024)} %get-tuple-element.16, bf16[4992,128]{1,0:T(8,128)(2,1)} %bitcast.73, f32[]{:T(128)} %constant.8.clone.1, pred[4992]{0:T(1024)(128)(4,1)} %get-tuple-element.8), kind=kCustom, calls=%fused_computation.35 | custom fusion | flops 1916928 | bytes 2332160 | tf_op jit(solution)/shard_map/scatter-add | solution.py:79
  491.0 34.8 %scatter_custom_fusion.7 = f32[2048,128]{1,0:T(8,128)} fusion(f32[2048,128]{1,0:T(8,128)} %scatter_custom_fusion.6, s32[4992]{0:T(1024)} %get-tuple-element.17, bf16[4992,128]{1,0:T(8,128)(2,1)} %bitcast.74, f32[]{:T(128)} %constant.8.clone.1, pred[4992]{0:T(1024)(128)(4,1)} %get-tuple-element.7), kind=kCustom, calls=%fused_computation.36 | custom fusion | flops 1916928 | bytes 2332160 | tf_op jit(solution)/shard_map/scatter-add | solution.py:79
  525.8 36.2 %scatter_custom_fusion.8 = f32[2048,128]{1,0:T(8,128)} fusion(f32[2048,128]{1,0:T(8,128)} %scatter_custom_fusion.7, s32[4992]{0:T(1024)} %get-tuple-element.18, bf16[4992,128]{1,0:T(8,128)(2,1)} %bitcast.75, f32[]{:T(128)} %constant.8.clone.1, pred[4992]{0:T(1024)(128)(4,1)} %copy-done.7), kind=kCustom, calls=%fused_computation.37 | custom fusion | flops 1916928 | bytes 2332160 | tf_op jit(solution)/shard_map/scatter-add | solution.py:79
  562.0 38.5 %scatter_custom_fusion.9 = f32[2048,128]{1,0:T(8,128)} fusion(f32[2048,128]{1,0:T(8,128)} %scatter_custom_fusion.8, s32[4992]{0:T(1024)} %get-tuple-element.19, bf16[4992,128]{1,0:T(8,128)(2,1)} %bitcast.76, f32[]{:T(128)} %constant.8.clone.1, pred[4992]{0:T(1024)(128)(4,1)} %copy-done.6), kind=kCustom, calls=%fused_computation.38 | custom fusion | flops 1916928 | bytes 2332160 | tf_op jit(solution)/shard_map/scatter-add | solution.py:79
  600.5 1.4 slice.86
  601.9 2.1 fusion.17
  604.0 3.4 fusion.39
  607.5 54.5 %all-reduce = (f32[3456]{0:T(1024)}, f32[3456]{0:T(1024)}) all-reduce(f32[3456]{0:T(1024)} %fusion.39, f32[3456]{0:T(1024)S(1)} %copy-done.4), channel_id=1, replica_groups=mesh['grp'=4,'emb'=8] {'grp','emb'}, use_global_device_ids=true, to_apply=%region_14.15 | all-reduce | flops 6912 | bytes 55296 | tf_op jit(solution)/shard_map/psum | solution.py:83
  661.9 2.3 copy.50
  (28 shorter events, 7.0 us)
Async XLA Ops:
  7.2 242.8 %copy-start = (bf16[3456,512]{1,0:T(8,128)(2,1)S(1)}, bf16[3456,512]{1,0:T(8,128)(2,1)}, u32[]{:S(2)}) copy-start(bf16[3456,512]{1,0:T(8,128)(2,1)} %param.18) | copy-start | bytes 10616836
  36.9 18.2 %copy-start.5 = (s32[3328]{0:T(1024)}, s32[3328]{0:T(1024)S(1)}, u32[]{:S(2)}) copy-start(s32[3328]{0:T(1024)S(1)} %fusion.69) | copy-start | bytes 39940
  75.4 2.9 copy-start.2
  75.4 3.6 copy-start.3
  78.3 110.4 %copy-start.7 = (pred[4992]{0:T(1024)(128)(4,1)}, pred[4992]{0:T(1024)(128)(4,1)S(1)}, u32[]{:S(2)}) copy-start(pred[4992]{0:T(1024)(128)(4,1)S(1)} %get-tuple-element.6) | copy-start | bytes 14980
  78.3 111.1 %copy-start.6 = (pred[4992]{0:T(1024)(128)(4,1)}, pred[4992]{0:T(1024)(128)(4,1)S(1)}, u32[]{:S(2)}) copy-start(pred[4992]{0:T(1024)(128)(4,1)S(1)} %get-tuple-element.5) | copy-start | bytes 14980
  201.8 4.5 copy-start.1
  201.8 34.0 %all-to-all-start.1 = ((bf16[8,624,128]{2,1,0:T(8,128)(2,1)}), bf16[8,624,128]{2,1,0:T(8,128)(2,1)}, u32[]{:S(2)}, u32[]{:S(2)}) async-start(bf16[8,624,128]{2,1,0:T(8,128)(2,1)} %fusion.10), calls=%async_computation.1 | async-start | bytes 2555904 | tf_op jit(solution)/shard_map/all_to_all | solution.py:46
  206.1 455.9 %all-reduce.3.cloned.1.call-start = ((), (), s32[]{:S(2)}) async-start(), calls=%async_computation.3 | async-start | bytes 2097152 | tf_op jit(solution)/shard_map/psum | solution.py:82
  604.0 3.4 copy-start.4
Sparse Core Ops, SparseCore 0:
  600.7 50.8 all-reduce.2
where the time goes:
time: 684 us; the launch traced here: 671 us
  other arithmetic  322 us (47%)
  local copies, waits for them, and re-layouts  182 us (27%)
  blocking collectives  104 us (15%)
  waiting for transfers between devices  26.2 us (4%)
  matrix products  18.1 us (3%)
  between operations  14.6 us (2%)
    scatter-add x8, other arithmetic, body(): row_part.at[jnp.where(valid, index, 0)]  281 us
    gather x8, local copies, waits for them, and re-layouts, body(): table_window[jnp.where(pool_valid, pool_index, 0)].astype(jnp.float32)  97.4 us
    psum x1, blocking collectives, body(): head_grad, bias_grad = lax.psum((head_part, bias_part), ('grp', 'emb'))  54.5 us
    all_to_all x1, blocking collectives, body(): lax.all_to_all(outgoing.reshape(owners, capacity, width), 'emb', split_ax...  34.6 us
    all_to_all x1, waiting for transfers between devices, body(): lax.all_to_all(summed.astype(jnp.bfloat16).reshape(owners, count, width),...  26.2 us
    scatter x1, local copies, waits for them, and re-layouts, body(): jnp.full((owners * capacity, hot), -1, jnp.int32).at[position].set(entries)  15.1 us
    scatter x1, local copies, waits for them, and re-layouts, body(): jnp.zeros((owners * capacity, width), jnp.bfloat16).at[position]  14.9 us
    all_to_all x1, blocking collectives, body(): lax.all_to_all(requests, 'emb', split_axis=0, concat_axis=0, tiled=True)  14.8 us
  transfers between devices with their start and end apart: 2, of which 1 were waited for; matrix products, arithmetic and copies ran while one was open for 2% of the time, Pallas kernels for 0%

commit v1 on v0

v1 whole, which is shorter than its diff:
```python
import functools

import jax
import jax.numpy as jnp
from jax import lax
from jax.experimental import pallas as pl
from jax.experimental.pallas import tpu as pltpu
from jax.sharding import PartitionSpec as P

BF16 = jnp.bfloat16
F32 = jnp.float32
LANES = 128
CHUNK = 32
VMEM_BYTES = 16 * 1024 * 1024


def params():
    return pltpu.CompilerParams(vmem_limit_bytes=VMEM_BYTES)


VMEM = pl.BlockSpec(memory_space=pltpu.VMEM)


def cost(flops, moved):
    return pl.CostEstimate(flops=flops, bytes_accessed=moved, transcendentals=0)


def ring_place(owner):
    return jnp.where(owner % 2 == 1, owner // 2, 7 - owner // 2)


def diagonal():
    return lax.broadcasted_iota(jnp.int32, (LANES, LANES), 0) == lax.broadcasted_iota(
        jnp.int32, (LANES, LANES), 1
    )


def count_kernel(owners, local_rows, where_ref, place_ref, counts_ref, turn_ref, column_ref):
    tables, hot, _ = place_ref.shape
    rows = counts_ref.shape[0]
    high = rows // LANES
    half, index = where_ref[0], where_ref[1]
    shift = local_rows.bit_length() - 1
    eye = diagonal()
    ones = jnp.ones((LANES, LANES), BF16)
    ids = lax.broadcasted_iota(jnp.int32, (LANES, LANES), 0)

    def table(at, carry):
        place = place_ref[at]
        owner = place[0:1, :] >> shift
        if owners == 8:
            turn = (ring_place(owner) - ring_place(index) + owners) & (owners - 1)
        else:
            turn = owner
        turn = turn.astype(F32)
        turn_ref[pl.ds(at, 1), :] = turn
        lanes = pl.ds(pl.multiple_of(at * LANES, LANES), LANES)
        column_ref[lanes, :] = jnp.dot(
            jnp.where(eye, turn, 0.0).astype(BF16), ones, preferred_element_type=F32
        ).astype(BF16)
        here = (place & (local_rows - 1)) - half * rows
        inside = (place >= 0) & (here >= 0) & (here < rows)
        low = jnp.where(inside, here & (LANES - 1), -1)
        code = jnp.where(inside, jnp.left_shift(1, 4 * (here >> (LANES.bit_length() - 1))), 0)
        for first in range(0, LANES, CHUNK):
            total = 0
            for h in range(hot):
                total = total + jnp.where(
                    ids[first : first + CHUNK] == low[h : h + 1, :], code[h : h + 1, :], 0
                )
            for part in range(high):
                count = lax.shift_right_logical(total, 4 * part) & 15
                start = part * LANES + first
                counts_ref[start : start + CHUNK, lanes] = count.astype(F32).astype(BF16)
        return carry

    lax.fori_loop(0, tables, table, 0, unroll=2)


def bag_counts(where, place, owners, local_rows):
    tables, hot, samples = place.shape
    bags = tables * samples
    rows = local_rows // 2
    return pl.pallas_call(
        functools.partial(count_kernel, owners, local_rows),
        out_shape=(
            jax.ShapeDtypeStruct((rows, bags), BF16),
            jax.ShapeDtypeStruct((tables, samples), F32),
            jax.ShapeDtypeStruct((bags, LANES), BF16),
        ),
        in_specs=[pl.BlockSpec(memory_space=pltpu.SMEM), VMEM],
        out_specs=(VMEM, VMEM, VMEM),
        compiler_params=params(),
        cost_estimate=cost(5 * 10**9, 0),
        name="bag_counts",
    )(where, place)


def pool_kernel(shards, turns, tables, added, turn_ref, counts_ref, *refs):
    sum_ref = refs[-1]
    blocks = refs[: sum(shards)]
    before = refs[sum(shards) : sum(shards) + added]
    left, at = [], 0
    for parts in shards:
        tiles = [
            ref[row : row + LANES, :]
            for ref in blocks[at : at + parts]
            for row in range(0, ref.shape[0], LANES)
        ]
        left.append(jnp.concatenate(tiles, axis=1))
        at += parts
    left = jnp.concatenate(left, axis=0)
    for start in range(0, turn_ref.shape[0], tables):
        bags = slice(start * LANES, (start + tables) * LANES)
        product = jnp.dot(left, counts_ref[:, bags], preferred_element_type=F32)
        for table in range(tables):
            turn = turn_ref[start + table : start + table + 1, :]
            here = slice((start + table) * LANES, (start + table + 1) * LANES)
            total = before[0][:, here] if before else 0.0
            for i, one in enumerate(turns):
                mine = product[i * LANES : (i + 1) * LANES, table * LANES : (table + 1) * LANES]
                total = jnp.where(turn == one, mine, total)
            sum_ref[:, here] = total


def pool(turns, turn, counts, shards, before, ahead=()):
    rows, bags = counts.shape
    blocks = [block for shard in shards for block in shard]
    width = blocks[0].shape[1]
    tables = turn.shape[0]
    extra = ([] if before is None else [before]) + list(ahead)
    return pl.pallas_call(
        functools.partial(
            pool_kernel,
            [len(shard) for shard in shards],
            turns,
            tables if len(turns) <= 4 else tables // 2,
            0 if before is None else 1,
        ),
        out_shape=jax.ShapeDtypeStruct((width, bags), F32),
        in_specs=[VMEM] * (2 + len(blocks) + len(extra)),
        out_specs=VMEM,
        compiler_params=params(),
        cost_estimate=cost(0, 0),
        name="pool",
    )(turn, counts, *blocks, *extra)


def cross_kernel(
    tables,
    dense_ref,
    own_ref,
    other_ref,
    label_ref,
    weight_ref,
    down_ref,
    up_ref,
    bias_ref,
    head_ref,
    d_pooled_ref,
    dense_grad_ref,
    grads_ref,
    x0_ref,
    cross_ref,
    d_cross_ref,
):
    samples = dense_ref.shape[0]
    blocks = tables + 1
    eye = diagonal()
    column = lambda ref: jnp.sum(jnp.where(eye, ref[...], 0.0), axis=1, keepdims=True)
    x0_ref[:, :LANES] = dense_ref[...]
    for table in range(tables):
        here = slice(table * LANES, (table + 1) * LANES)
        x0_ref[:, (table + 1) * LANES : (table + 2) * LANES] = (
            (own_ref[:, here] + other_ref[:, here]).T.astype(BF16)
        )
    low = jnp.dot(x0_ref[...], down_ref[...], preferred_element_type=F32).astype(BF16)
    logit = jnp.zeros((samples, LANES), F32)
    for block in range(blocks):
        here = slice(block * LANES, (block + 1) * LANES)
        cross = jnp.dot(low, up_ref[:, here], preferred_element_type=F32) + bias_ref[block : block + 1, :]
        cross_ref[:, here] = cross
        x0f = x0_ref[:, here].astype(F32)
        logit = logit + (x0f * cross + x0f) * head_ref[block : block + 1, :]
    logit = jnp.sum(logit, axis=1, keepdims=True)
    d_logit = column(weight_ref) * (jax.nn.sigmoid(logit) - column(label_ref))
    for block in range(blocks):
        here = slice(block * LANES, (block + 1) * LANES)
        x0f = x0_ref[:, here].astype(F32)
        x1 = x0f * cross_ref[:, here] + x0f
        grads_ref[0, block : block + 1, :] = jnp.sum(d_logit * x1, axis=0, keepdims=True)
        d_cross = d_logit * head_ref[block : block + 1, :] * x0f
        grads_ref[1, block : block + 1, :] = jnp.sum(d_cross, axis=0, keepdims=True)
        d_cross_ref[:, here] = d_cross.astype(BF16)
    d_low = lax.dot_general(
        d_cross_ref[...], up_ref[...], (((1,), (1,)), ((), ())), preferred_element_type=F32
    ).astype(BF16)
    for block in range(blocks):
        here = slice(block * LANES, (block + 1) * LANES)
        d_x1 = d_logit * head_ref[block : block + 1, :]
        d_x0 = d_x1 * (cross_ref[:, here] + 1.0) + lax.dot_general(
            d_low, down_ref[here, :], (((1,), (1,)), ((), ())), preferred_element_type=F32
        )
        if block == 0:
            dense_grad_ref[...] = d_x0.astype(BF16)
        else:
            place = slice((block - 1) * samples, block * samples)
            d_pooled_ref[place, :] = d_x0.astype(BF16)


def cross_layer(dense, own, other, labels, weights, down_w, up_w, bias, head):
    samples, width = dense.shape
    tables = own.shape[1] // samples
    cross = down_w.shape[0]
    return pl.pallas_call(
        functools.partial(cross_kernel, tables),
        out_shape=(
            jax.ShapeDtypeStruct((tables * samples, width), BF16),
            jax.ShapeDtypeStruct((samples, width), BF16),
            jax.ShapeDtypeStruct((2, cross // LANES, LANES), F32),
        ),
        scratch_shapes=[
            pltpu.VMEM((samples, cross), BF16),
            pltpu.VMEM((samples, cross), F32),
            pltpu.VMEM((samples, cross), BF16),
        ],
        compiler_params=params(),
        cost_estimate=cost(8 * 10**9, 12 * 10**6),
        name="cross_layer",
    )(dense, own, other, labels, weights, down_w, up_w, bias, head)


def spread_kernel(turns, count, at, *refs):
    sides = [refs[3 * i : 3 * i + 3] for i in range(count)]
    before = refs[3 * count : -1 - count]
    rows_ref, masked = refs[-1 - count], refs[-count:]
    zero = jnp.array(0, BF16)
    for (column_ref, gradient_ref, _), masked_ref in zip(sides, masked):
        for i, one in enumerate(turns):
            masked_ref[:, i * LANES : (i + 1) * LANES] = jnp.where(
                column_ref[...] == jnp.array(one, BF16), gradient_ref[...], zero
            )
    total = before[0][:, at * LANES : (at + len(turns)) * LANES] if before else None
    for (_, _, counts_ref), masked_ref in zip(sides, masked):
        part = jnp.dot(counts_ref[...], masked_ref[...], preferred_element_type=F32)
        total = part if total is None else total + part
    rows_ref[...] = total


def spread(turns, sides, before=None, at=0):
    bags, width = sides[0][1].shape
    rows = sides[0][2].shape[0]
    wide = len(turns) * width
    operands = [one for side in sides for one in side] + ([] if before is None else [before])
    return pl.pallas_call(
        functools.partial(spread_kernel, turns, len(sides), at),
        out_shape=jax.ShapeDtypeStruct((rows, wide), F32),
        in_specs=[VMEM] * len(operands),
        out_specs=VMEM,
        scratch_shapes=[pltpu.VMEM((bags, wide), BF16)] * len(sides),
        compiler_params=params(),
        cost_estimate=cost(0, 0),
        name="spread",
    )(*operands)


def place_kernel(at_ref, part_ref, *refs):
    rows_ref, sem = refs[-2], refs[-1]
    rows = part_ref.shape[0]
    start = pl.multiple_of(at_ref[0] * rows, rows)
    copy = pltpu.make_async_copy(part_ref, rows_ref.at[pl.ds(start, rows), :], sem)
    copy.start()
    copy.wait()


def place_half(at, part, before=None):
    rows, width = part.shape
    either = pl.BlockSpec(memory_space=pl.ANY)
    return pl.pallas_call(
        place_kernel,
        out_shape=jax.ShapeDtypeStruct((2 * rows, width), F32),
        in_specs=[pl.BlockSpec(memory_space=pltpu.SMEM), VMEM] + [either] * (before is not None),
        out_specs=either,
        scratch_shapes=[pltpu.SemaphoreType.DMA],
        input_output_aliases={} if before is None else {2: 0},
        compiler_params=params(),
        cost_estimate=cost(0, 0),
        name="place_half",
    )(at, part, *([] if before is None else [before]))


def swap(value, axis, stride):
    size = lax.axis_size(axis)
    return lax.ppermute(value, axis, [(i, i ^ stride) for i in range(size)])


def sum_pairs(value, axis, stride, wire):
    while stride < lax.axis_size(axis):
        value = value.astype(wire)
        value = value.astype(F32) + swap(value, axis, stride).astype(F32)
        stride *= 2
    return value


def ring_order(size):
    inner = 1 << ((size.bit_length() - 1) // 2)
    outer = size // inner
    cycle = []
    for far in range(outer):
        columns = range(1, inner) if far % 2 == 0 else range(inner - 1, 0, -1)
        cycle += [far * inner + column for column in columns]
    return cycle + [far * inner for far in range(outer - 1, -1, -1)]


def ring_turns(owners):
    order = ring_order(owners)
    right = [(order[i], order[(i + 1) % owners]) for i in range(owners)]
    return right, [(there, here) for here, there in right]


def count_and_pool(where, place, shard, local_rows, ahead):
    owners = lax.axis_size("emb")
    count = lambda own: bag_counts(where, own, owners, local_rows)
    places = [place, swap(place, "grp", 1)]
    sums = [None, None]

    def add(side, turns, shards, ahead=()):
        sums[side] = pool(turns, sides[side][1], sides[side][0], shards, sums[side], ahead)

    if owners != 8:
        sides = [count(one) for one in places]
        table = lax.all_gather(shard, "emb", axis=0, tiled=False)
        for start in range(0, owners, 8):
            here = tuple(range(start, start + 8))
            for side in (1, 0):
                add(side, here, [[table[one]] for one in here])
        return sides, sums
    right, left = ring_turns(owners)
    lefts, rights = [shard], [shard]

    def step(beside):
        before = lefts[-1], rights[-1], beside
        a, b, beside = before if beside is None else lax.optimization_barrier(before)
        lefts.append(lax.ppermute(a, "emb", right))
        rights.append(lax.ppermute(b, "emb", left))
        return beside

    step(None)
    own, places[1] = step((count(places[0]), places[1]))
    sides = list(step([own, count(places[1])]))
    near = (0, 1, 7), [[shard], [rights[1]], [lefts[1]]]
    add(1, *near)
    add(1, (2, 6), [[rights[2]], [lefts[2]]], ahead)
    add(0, *near)
    middle = shard.shape[0] // 2
    a, b, sums[0], sums[1] = lax.optimization_barrier(
        (lefts[3][:middle], rights[3][middle:], sums[0], sums[1])
    )
    far = [lax.ppermute(a, "emb", right), lax.ppermute(b, "emb", left)]
    add(0, (2, 6), [[rights[2]], [lefts[2]]])
    add(1, (3, 5), [[rights[3]], [lefts[3]]])
    add(1, (4,), [far])
    sums[0], sums[1] = lax.optimization_barrier((sums[0], sums[1]))
    add(0, (3, 5), [[rights[3]], [lefts[3]]])
    add(0, (4,), [far])
    return sides, sums


def spread_and_sum(sides, grads):
    owners = lax.axis_size("emb")
    width = sides[0][1].shape[1]
    exchanges = [
        (axis, 1 << bit)
        for axis in ("grp", "emb")
        for bit in range(lax.axis_size(axis).bit_length() - 1)
    ][1:]
    if owners != 8 or len(exchanges) != 4:
        parts = [
            spread(tuple(range(start, start + 4)), sides).astype(BF16)
            for start in range(0, owners, 4)
        ]
        for axis, stride in exchanges:
            grads = grads + swap(grads, axis, stride)
        part = lax.psum_scatter(
            jnp.concatenate(parts, axis=1), "emb", scatter_dimension=1, tiled=True
        )
        return sum_pairs(part, "grp", 2, BF16), grads
    right, left = ring_turns(owners)

    def exchange(grads):
        return grads + swap(grads, *exchanges.pop(0))

    def send(to_right, to_left):
        return lax.ppermute(to_right, "emb", right), lax.ppermute(to_left, "emb", left)

    def messages(part, went_right, went_left):
        to_right, to_left = part[:, :width], part[:, width:]
        return (to_right + went_right).astype(BF16), (to_left + went_left).astype(BF16)

    own = spread((4, 0), sides[:1])
    part = spread((4, 0), sides[1:], own)
    far, mine = part[:, :width].astype(BF16), part[:, width:]
    middle = far.shape[0] // 2
    far, sides, grads = lax.optimization_barrier((far, sides, grads))
    went_right, went_left = send(far[:middle], far[middle:])
    went_right = jnp.pad(went_right.astype(F32), ((0, middle), (0, 0)))
    went_left = jnp.pad(went_left.astype(F32), ((middle, 0), (0, 0)))
    for step in (3, 2, 1):
        part = spread((step, owners - step), sides)
        to_right, to_left = messages(part, went_right, went_left)
        to_right, to_left, sides, grads = lax.optimization_barrier((to_right, to_left, sides, grads))
        went_right, went_left = send(to_right, to_left)
        grads = exchange(grads)
        went_right, went_left = went_right.astype(F32), went_left.astype(F32)
    total = (mine + went_right + went_left).astype(BF16)
    total, grads = lax.optimization_barrier((total, grads))
    other, grads = lax.optimization_barrier((swap(total, "grp", 2), exchange(grads)))
    return total.astype(F32) + other.astype(F32), grads


def body(
    table_window,
    dense_part,
    bag_rows,
    bag_lengths,
    bag_owner,
    labels,
    sample_weight,
    down_w,
    up_w,
    cross_bias,
    head_w,
):
    samples, tables, hot = bag_rows.shape
    local_rows, width = table_window.shape
    rows = local_rows // 2
    half = (lax.axis_index("grp") % 2).astype(jnp.int32)
    where = jnp.stack([half, lax.axis_index("emb").astype(jnp.int32)])
    shard = lax.dynamic_slice_in_dim(table_window, half * rows, rows, 0)
    shard = shard.reshape(-1, LANES, width).transpose(0, 2, 1).reshape(rows, LANES)
    live = jnp.arange(hot, dtype=jnp.int32)[None, :, None] < bag_lengths.T[:, None, :]
    place = bag_owner.transpose(1, 2, 0) * local_rows + bag_rows.transpose(1, 2, 0)
    place = jnp.where(live, place, -1)
    sides, (own, lent) = count_and_pool(where, place, shard, local_rows, (down_w, up_w))
    other = swap(lent, "grp", 1)
    d_pooled, dense_grad, grads = cross_layer(
        dense_part,
        own,
        other,
        labels.astype(F32).reshape(1, samples),
        sample_weight.reshape(1, samples),
        down_w,
        up_w,
        cross_bias.reshape(-1, LANES),
        head_w.reshape(-1, LANES),
    )
    grads = grads + swap(grads, "grp", 1)
    sides = [
        (sides[0][2], d_pooled, sides[0][0]),
        (sides[1][2], swap(d_pooled, "grp", 1), sides[1][0]),
    ]
    row_half, grads = spread_and_sum(sides, grads)
    at = half.reshape(1)
    row_grad = place_half(1 - at, swap(row_half, "grp", 1), place_half(at, row_half))
    return (row_grad, grads[0].reshape(-1), grads[1].reshape(-1), dense_grad)


def solution(mesh):
    in_specs = (
        P("emb", None),
        P(("grp", "emb"), None),
        P(("grp", "emb"), None, None),
        P(("grp", "emb"), None),
        P(("grp", "emb"), None, None),
        P(("grp", "emb")),
        P(("grp", "emb")),
        P(),
        P(),
        P(),
        P(),
    )
    out_specs = (P("emb", None), P(), P(), P(("grp", "emb"), None))
    return jax.shard_map(body, mesh=mesh, in_specs=in_specs, out_specs=out_specs, check_vma=False)
```

time: 684 us -> 94.2 us (0.14); the launches traced: 671 us -> 93.9 us
  other arithmetic: 322 us -> 2.2 us
  local copies, waits for them, and re-layouts: 182 us -> 2.19 us
  blocking collectives: 104 us -> 0 us
  Pallas kernels: 0 us -> 48.1 us
  starting transfers between devices: 4.48 us -> 24.5 us
  matrix products: 18.1 us -> 0 us
  between operations: 14.6 us -> 1.28 us
  waiting for transfers between devices: 26.2 us -> 15.6 us
    scatter-add x8 -> x0, other arithmetic: 281 us -> none  [body(): row_part.at[jnp.where(valid, index, 0)]]
    gather x9 -> x0, local copies, waits for them, and re-layouts: 107 us -> none  [the longest x8 97.4 us: body(): table_window[jnp.where(pool_valid, pool_index, 0)].astype(jnp.float32)]
    psum x1 -> x0, blocking collectives: 54.5 us -> none  [body(): head_grad, bias_grad = lax.psum((head_part, bias_part), ('grp', 'emb'))]
    all_to_all x2 -> x0, blocking collectives: 49.4 us -> none  [the longest x1 34.6 us: body(): lax.all_to_all(outgoing.reshape(owners, capacity, width), 'emb', split_ax...]
    pallas_call x0 -> x18, Pallas kernels: none -> 48.1 us  [the longest x5 16.2 us: spread(): pl.pallas_call(functools.partial(spread_kernel, turns, len(sides), at), o...]
    scatter x2 -> x0, local copies, waits for them, and re-layouts: 29.9 us -> none  [the longest x1 15.1 us: body(): jnp.full((owners * capacity, hot), -1, jnp.int32).at[position].set(entries)]
    all_to_all x1 -> x0, waiting for transfers between devices: 26.2 us -> none  [body(): lax.all_to_all(summed.astype(jnp.bfloat16).reshape(owners, count, width),...]
    ppermute x0 -> x26, starting transfers between devices: none -> 24.5 us  [the longest x10 6.89 us: swap(): return lax.ppermute(value, axis, [(i, i ^ stride) for i in range(size)])]
  transfers between devices with their start and end apart: 2 -> 26, of which waited for: 1 -> 12; matrix products, arithmetic and copies ran while one was open for 2% -> 3% of each run, Pallas kernels for 0% -> 42%
where the time goes in v1:
time: 94.2 us; the launch traced here: 93.9 us
  Pallas kernels  48.1 us (51%)
  starting transfers between devices  24.5 us (26%)
  waiting for transfers between devices  15.6 us (17%)
  other arithmetic  2.2 us (2%)
  local copies, waits for them, and re-layouts  2.19 us (2%)
  between operations  1.28 us (1%)
    pallas_call x5, Pallas kernels, spread(): pl.pallas_call(functools.partial(spread_kernel, turns, len(sides), at), o...  16.2 us
    pallas_call x8, Pallas kernels, pool(): pl.pallas_call(functools.partial(pool_kernel, [len(shard) for shard in sh...  15.5 us
    pallas_call x2, Pallas kernels, bag_counts(): pl.pallas_call(functools.partial(count_kernel, owners, local_rows), out_s...  10.4 us
    ppermute x10, waiting for transfers between devices, swap(): return lax.ppermute(value, axis, [(i, i ^ stride) for i in range(size)])  9.82 us
    ppermute x10, starting transfers between devices, swap(): return lax.ppermute(value, axis, [(i, i ^ stride) for i in range(size)])  6.89 us
    ppermute x3, starting transfers between devices, step(): lefts.append(lax.ppermute(a, 'emb', right))  6.14 us
    ppermute x4, starting transfers between devices, send(): lax.ppermute(to_right, 'emb', right)  5.22 us
    pallas_call x1, Pallas kernels, cross_layer(): pl.pallas_call(functools.partial(cross_kernel, tables), out_shape=(jax.Sh...  4.51 us
  transfers between devices with their start and end apart: 26, of which 12 were waited for; matrix products, arithmetic and copies ran while one was open for 3% of the time, Pallas kernels for 42%

profile of v1, /device:TPU:0, one launch (start us, length us, event | category | flops | bytes accessed | tf_op | source)
XLA Modules:
  0.0 93.9 jit_solution(13701607081589557614)
XLA Ops:
  0.7 1.0 %copy-done = bf16[2048,128]{1,0:T(8,128)(2,1)S(1)} copy-done((bf16[2048,128]{1,0:T(8,128)(2,1)S(1)}, bf16[2048,128]{1,0:T(8,128)(2,1)}, u32[]{:S(2)}) %copy-start) | copy-done | bytes 524312
  1.7 0.2 copy.16
  1.9 3.0 %collective-permute-start = (bf16[1024,128]{1,0:T(8,128)(2,1)S(1)}, bf16[1024,128]{1,0:T(8,128)(2,1)S(1)}, u32[]{:S(2)}, u32[]{:S(2)}) collective-permute-start(bf16[1024,128]{1,0:T(8,128)(2,1)S(1)} %bitcast.25), channel_id=1, source_target_pairs={{1,3},{3,5},{5,7},{7,6},{6,4},{4,2},{2,0},{0,1},{9,11},{11,13},{13... | collective-permute-start | bytes 786440 | tf_op jit(solution)/shard_map/ppermute | solution.py:344
  4.9 0.2 collective-permute-start.1
  5.0 0.7 multiply_bitcast_fusion
  5.8 0.9 fusion.8.place_ref
  6.8 0.1 pad_add_fusion.where_ref
  6.8 5.2 %bag_counts.2 = (bf16[1024,3328]{1,0:T(8,128)(2,1)S(1)}, f32[26,128]{1,0:T(8,128)S(1)}, bf16[3328,128]{1,0:T(8,128)(2,1)S(1)}) custom-call(s32[2]{0:T(128)S(1)} %pad_add_fusion.where_ref, s32[26,8,128]{2,1,0:T(8,128)S(1)} %fusion.8.place_ref), custom_call_target="tpu_custom_call" | custom-call | flops 5000000000 | tf_op jit(solution)/shard_map/bag_counts/pallas_call | solution.py:84
  12.1 0.6 collective-permute-done.1.refs_1_
  12.6 1.6 %collective-permute-start.3 = (bf16[1024,128]{1,0:T(8,128)(2,1)S(1)}, bf16[1024,128]{1,0:T(8,128)(2,1)S(1)}, u32[]{:S(2)}, u32[]{:S(2)}) collective-permute-start(bf16[1024,128]{1,0:T(8,128)(2,1)S(1)} %collective-permute-done.refs_2_), channel_id=1, source_target_pairs={{1,3},{3,5},{5,7},{7,6},{6,4},{4,2},{2,0},{0,1},{9,11},{11,13},{13... | collective-permute-start | bytes 786440 | tf_op jit(solution)/shard_map/ppermute | solution.py:344
  14.2 0.4 collective-permute-start.4
  14.7 5.2 %bag_counts.3 = (bf16[1024,3328]{1,0:T(8,128)(2,1)S(1)}, f32[26,128]{1,0:T(8,128)S(1)}, bf16[3328,128]{1,0:T(8,128)(2,1)S(1)}) custom-call(s32[2]{0:T(128)S(1)} %pad_add_fusion.where_ref, s32[26,8,128]{2,1,0:T(8,128)S(1)} %collective-permute-done.2.place_ref), custom_call_target="tpu_custom_call" | custom-call | flops 5000000000 | tf_op jit(solution)/shard_map/bag_counts/pallas_call | solution.py:84
  19.9 1.2 %collective-permute-done.3.refs_1_ = bf16[1024,128]{1,0:T(8,128)(2,1)S(1)} collective-permute-done((bf16[1024,128]{1,0:T(8,128)(2,1)S(1)}, bf16[1024,128]{1,0:T(8,128)(2,1)S(1)}, u32[]{:S(2)}, u32[]{:S(2)}) %collective-permute-start.3) | collective-permute-done | bytes 262176 | tf_op jit(solution)/shard_map/ppermute | solution.py:344
  21.0 1.4 %collective-permute-done.4.refs_0_ = bf16[1024,128]{1,0:T(8,128)(2,1)S(1)} collective-permute-done((bf16[1024,128]{1,0:T(8,128)(2,1)S(1)}, bf16[1024,128]{1,0:T(8,128)(2,1)S(1)}, u32[]{:S(2)}, u32[]{:S(2)}) %collective-permute-start.4) | collective-permute-done | bytes 262176 | tf_op jit(solution)/shard_map/ppermute | solution.py:345
  22.4 1.6 %collective-permute-start.5 = (bf16[1024,128]{1,0:T(8,128)(2,1)S(1)}, bf16[1024,128]{1,0:T(8,128)(2,1)S(1)}, u32[]{:S(2)}, u32[]{:S(2)}) collective-permute-start(bf16[1024,128]{1,0:T(8,128)(2,1)S(1)} %collective-permute-done.3.refs_1_), channel_id=1, source_target_pairs={{1,3},{3,5},{5,7},{7,6},{6,4},{4,2},{2,0},{0,1},{9,11},{11,13},{13... | collective-permute-start | bytes 786440 | tf_op jit(solution)/shard_map/ppermute | solution.py:344
  24.0 0.4 collective-permute-start.6
  24.4 2.8 %pool.9.refs_2_ = f32[128,3328]{1,0:T(8,128)S(1)} custom-call(f32[26,128]{1,0:T(8,128)S(1)} %get-tuple-element.83.turn_ref, bf16[1024,3328]{1,0:T(8,128)(2,1)S(1)} %get-tuple-element.116.counts_ref.refs_2_.refs_5_, bf16[1024,128]{1,0:T(8,128)(2,1)S(1)} %bitcast.27, bf16[1024,128]{1,0:T(8,128)(2,1)S(1)} %collective-permute-done.1.refs_1_, ...), custom_call_target="tpu_custom_call" | custom-call | tf_op jit(solution)/shard_map/pool/pallas_call | solution.py:132
  27.3 2.8 %pool.8.refs_2_ = f32[128,3328]{1,0:T(8,128)S(1)} custom-call(f32[26,128]{1,0:T(8,128)S(1)} %get-tuple-element.79.turn_ref, bf16[1024,3328]{1,0:T(8,128)(2,1)S(1)} %get-tuple-element.113.counts_ref.refs_2_, bf16[1024,128]{1,0:T(8,128)(2,1)S(1)} %bitcast.28, bf16[1024,128]{1,0:T(8,128)(2,1)S(1)} %collective-permute-done.1.refs_1_, ...), custom_call_target="tpu_custom_call" | custom-call | tf_op jit(solution)/shard_map/pool/pallas_call | solution.py:132
  30.1 0.2 copy-done.2
  30.4 1.9 %pool.10.refs_2_ = f32[128,3328]{1,0:T(8,128)S(1)} custom-call(f32[26,128]{1,0:T(8,128)S(1)} %get-tuple-element.83.turn_ref, bf16[1024,3328]{1,0:T(8,128)(2,1)S(1)} %get-tuple-element.116.counts_ref.refs_2_.refs_5_, bf16[1024,128]{1,0:T(8,128)(2,1)S(1)} %collective-permute-done.4.refs_0_, bf16[1024,128]{1,0:T(8,128)(2,1)S(1)} %collective-permute-done.3.refs_1_, ...), custom_call_target="tpu_custom_call" | custom-call | tf_op jit(solution)/shard_map/pool/pallas_call | solution.py:132
  32.3 1.6 %collective-permute-start.7 = (bf16[512,128]{1,0:T(8,128)(2,1)S(1)}, bf16[512,128]{1,0:T(8,128)(2,1)S(1)}, u32[]{:S(2)}, u32[]{:S(2)}) collective-permute-start(bf16[512,128]{1,0:T(8,128)(2,1)S(1)} %slice.57), channel_id=1, source_target_pairs={{1,3},{3,5},{5,7},{7,6},{6,4},{4,2},{2,0},{0,1},{9,11},{11,13},{13... | collective-permute-start | bytes 393224 | tf_op jit(solution)/shard_map/ppermute | solution.py:359
  34.0 0.4 collective-permute-start.8
  34.4 1.9 %pool.12.refs_2_ = f32[128,3328]{1,0:T(8,128)S(1)} custom-call(f32[26,128]{1,0:T(8,128)S(1)} %get-tuple-element.83.turn_ref, bf16[1024,3328]{1,0:T(8,128)(2,1)S(1)} %get-tuple-element.116.counts_ref.refs_2_.refs_5_, bf16[1024,128]{1,0:T(8,128)(2,1)S(1)} %collective-permute-done.6.refs_0_, bf16[1024,128]{1,0:T(8,128)(2,1)S(1)} %collective-permute-done.5.refs_1_, ...), custom_call_target="tpu_custom_call" | custom-call | tf_op jit(solution)/shard_map/pool/pallas_call | solution.py:132
  36.4 1.9 %pool.11.refs_2_ = f32[128,3328]{1,0:T(8,128)S(1)} custom-call(f32[26,128]{1,0:T(8,128)S(1)} %get-tuple-element.79.turn_ref, bf16[1024,3328]{1,0:T(8,128)(2,1)S(1)} %get-tuple-element.113.counts_ref.refs_2_, bf16[1024,128]{1,0:T(8,128)(2,1)S(1)} %collective-permute-done.4.refs_0_, bf16[1024,128]{1,0:T(8,128)(2,1)S(1)} %collective-permute-done.3.refs_1_, ...), custom_call_target="tpu_custom_call" | custom-call | tf_op jit(solution)/shard_map/pool/pallas_call | solution.py:132
  38.3 0.6 collective-permute-done.8.refs_1_
  38.9 1.1 %pool.13 = f32[128,3328]{1,0:T(8,128)S(1)} custom-call(f32[26,128]{1,0:T(8,128)S(1)} %get-tuple-element.83.turn_ref, bf16[1024,3328]{1,0:T(8,128)(2,1)S(1)} %get-tuple-element.116.counts_ref.refs_2_.refs_5_, bf16[512,128]{1,0:T(8,128)(2,1)S(1)} %collective-permute-done.7.refs_0_, bf16[512,128]{1,0:T(8,128)(2,1)S(1)} %collective-permute-done.8.refs_1_, ...), custom_call_target="tpu_custom_call" | custom-call | tf_op jit(solution)/shard_map/pool/pallas_call | solution.py:132
  40.1 1.9 %pool.14.refs_2_ = f32[128,3328]{1,0:T(8,128)S(1)} custom-call(f32[26,128]{1,0:T(8,128)S(1)} %get-tuple-element.79.turn_ref, bf16[1024,3328]{1,0:T(8,128)(2,1)S(1)} %get-tuple-element.113.counts_ref.refs_2_, bf16[1024,128]{1,0:T(8,128)(2,1)S(1)} %collective-permute-done.6.refs_0_, bf16[1024,128]{1,0:T(8,128)(2,1)S(1)} %collective-permute-done.5.refs_1_, ...), custom_call_target="tpu_custom_call" | custom-call | tf_op jit(solution)/shard_map/pool/pallas_call | solution.py:132
  42.1 1.1 %pool.15.own_ref = f32[128,3328]{1,0:T(8,128)S(1)} custom-call(f32[26,128]{1,0:T(8,128)S(1)} %get-tuple-element.79.turn_ref, bf16[1024,3328]{1,0:T(8,128)(2,1)S(1)} %get-tuple-element.113.counts_ref.refs_2_, bf16[512,128]{1,0:T(8,128)(2,1)S(1)} %collective-permute-done.7.refs_0_, bf16[512,128]{1,0:T(8,128)(2,1)S(1)} %collective-permute-done.8.refs_1_, ...), custom_call_target="tpu_custom_call" | custom-call | tf_op jit(solution)/shard_map/pool/pallas_call | solution.py:132
  43.2 0.5 collective-permute-done.9.other_ref
  43.7 4.5 %cross_layer.1 = (bf16[3328,128]{1,0:T(8,128)(2,1)S(1)}, bf16[128,128]{1,0:T(8,128)(2,1)}, f32[2,27,128]{2,1,0:T(8,128)S(1)}) custom-call(bf16[128,128]{1,0:T(8,128)(2,1)S(1)} %copy-done.3, f32[128,3328]{1,0:T(8,128)S(1)} %pool.15.own_ref, f32[128,3328]{1,0:T(8,128)S(1)} %collective-permute-done.9.other_ref, f32[1,128]{1,0:T(1,128)S(1)} %convert_bitcast_fusion.label_ref, ...), custom_call_target="tpu_custom_call" | custom-call | flops 8000000000 | bytes 12000000 | tf_op jit(solution)/shard_map/cross_layer/pallas_call | solution.py:215
  48.2 0.2 collective-permute-start.10
  48.4 0.4 collective-permute-start.11
  48.8 2.1 %spread.5.refs_3_ = f32[1024,256]{1,0:T(8,128)S(1)} custom-call(bf16[3328,128]{1,0:T(8,128)(2,1)S(1)} %get-tuple-element.111.refs_0_, bf16[3328,128]{1,0:T(8,128)(2,1)S(1)} %get-tuple-element.112.refs_1_, bf16[1024,3328]{1,0:T(8,128)(2,1)S(1)} %get-tuple-element.113.counts_ref.refs_2_), custom_call_target="tpu_custom_call" | custom-call | tf_op jit(solution)/shard_map/spread/pallas_call | solution.py:255
  50.9 2.3 %spread.6 = f32[1024,256]{1,0:T(8,128)S(1)} custom-call(bf16[3328,128]{1,0:T(8,128)(2,1)S(1)} %get-tuple-element.114.refs_0_.refs_3_, bf16[3328,128]{1,0:T(8,128)(2,1)S(1)} %collective-permute-done.10.refs_1_.refs_4_, bf16[1024,3328]{1,0:T(8,128)(2,1)S(1)} %get-tuple-element.116.counts_ref.refs_2_.refs_5_, f32[1024,256]{1,0:T(8,128)S(1)} %spread.5.refs_3_), custom_call_target="tpu_custom_call" | custom-call | tf_op jit(solution)/shard_map/spread/pallas_call | solution.py:255
  53.4 1.6 %collective-permute-start.12 = (bf16[512,128]{1,0:T(8,128)(2,1)S(1)}, bf16[512,128]{1,0:T(8,128)(2,1)S(1)}, u32[]{:S(2)}, u32[]{:S(2)}) collective-permute-start(bf16[512,128]{1,0:T(8,128)(2,1)S(1)} %get-tuple-element.135), channel_id=1, source_target_pairs={{1,3},{3,5},{5,7},{7,6},{6,4},{4,2},{2,0},{0,1},{9,11},{11,13},{13... | collective-permute-start | bytes 393224 | tf_op jit(solution)/shard_map/ppermute | solution.py:394
  55.0 0.5 collective-permute-start.13
  55.4 3.9 %spread.7 = f32[1024,256]{1,0:T(8,128)S(1)} custom-call(bf16[3328,128]{1,0:T(8,128)(2,1)S(1)} %get-tuple-element.111.refs_0_, bf16[3328,128]{1,0:T(8,128)(2,1)S(1)} %get-tuple-element.112.refs_1_, bf16[1024,3328]{1,0:T(8,128)(2,1)S(1)} %get-tuple-element.113.counts_ref.refs_2_, bf16[3328,128]{1,0:T(8,128)(2,1)S(1)} %get-tuple-element.114.refs_0_.refs_3_, ...), custom_call_target="tpu_custom_call" | custom-call | tf_op jit(solution)/shard_map/spread/pallas_call | solution.py:255
  59.4 0.8 collective-permute-done.13
  60.2 0.1 fusion.4
  60.3 1.6 %collective-permute-start.14 = (bf16[1024,128]{1,0:T(8,128)(2,1)S(1)}, bf16[1024,128]{1,0:T(8,128)(2,1)S(1)}, u32[]{:S(2)}, u32[]{:S(2)}) collective-permute-start(bf16[1024,128]{1,0:T(8,128)(2,1)S(1)} %get-tuple-element.108), channel_id=1, source_target_pairs={{1,3},{3,5},{5,7},{7,6},{6,4},{4,2},{2,0},{0,1},{9,11},{11,13},{13... | collective-permute-start | bytes 786440 | tf_op jit(solution)/shard_map/ppermute | solution.py:394
  61.9 0.4 collective-permute-start.15
  62.4 1.5 %collective-permute-start.16 = (f32[2,27,128]{2,1,0:T(8,128)S(1)}, f32[2,27,128]{2,1,0:T(8,128)S(1)}, u32[]{:S(2)}, u32[]{:S(2)}) collective-permute-start(f32[2,27,128]{2,1,0:T(8,128)S(1)} %add.68), channel_id=1, source_target_pairs={{0,16},{8,24},{16,0},{24,8},{1,17},{9,25},{17,1},{25,9},{2,18},{10... | collective-permute-start | bytes 82952 | tf_op jit(solution)/shard_map/ppermute | solution.py:294
  63.9 3.9 %spread.8 = f32[1024,256]{1,0:T(8,128)S(1)} custom-call(bf16[3328,128]{1,0:T(8,128)(2,1)S(1)} %get-tuple-element.111.refs_0_, bf16[3328,128]{1,0:T(8,128)(2,1)S(1)} %get-tuple-element.112.refs_1_, bf16[1024,3328]{1,0:T(8,128)(2,1)S(1)} %get-tuple-element.113.counts_ref.refs_2_, bf16[3328,128]{1,0:T(8,128)(2,1)S(1)} %get-tuple-element.114.refs_0_.refs_3_, ...), custom_call_target="tpu_custom_call" | custom-call | tf_op jit(solution)/shard_map/spread/pallas_call | solution.py:255
  67.8 1.0 %collective-permute-done.15 = bf16[1024,128]{1,0:T(8,128)(2,1)S(1)} collective-permute-done((bf16[1024,128]{1,0:T(8,128)(2,1)S(1)}, bf16[1024,128]{1,0:T(8,128)(2,1)S(1)}, u32[]{:S(2)}, u32[]{:S(2)}) %collective-permute-start.15) | collective-permute-done | bytes 262176 | tf_op jit(solution)/shard_map/ppermute | solution.py:394
  68.8 0.1 fusion.2
  68.9 1.4 %collective-permute-start.17 = (bf16[1024,128]{1,0:T(8,128)(2,1)S(1)}, bf16[1024,128]{1,0:T(8,128)(2,1)S(1)}, u32[]{:S(2)}, u32[]{:S(2)}) collective-permute-start(bf16[1024,128]{1,0:T(8,128)(2,1)S(1)} %get-tuple-element.117), channel_id=1, source_target_pairs={{1,3},{3,5},{5,7},{7,6},{6,4},{4,2},{2,0},{0,1},{9,11},{11,13},{13... | collective-permute-start | bytes 786440 | tf_op jit(solution)/shard_map/ppermute | solution.py:394
  70.3 0.7 collective-permute-start.18
  71.0 1.3 %collective-permute-start.19 = (f32[2,27,128]{2,1,0:T(8,128)S(1)}, f32[2,27,128]{2,1,0:T(8,128)S(1)}, u32[]{:S(2)}, u32[]{:S(2)}) collective-permute-start(f32[2,27,128]{2,1,0:T(8,128)S(1)} %add.73), channel_id=1, source_target_pairs={{0,1},{1,0},{2,3},{3,2},{4,5},{5,4},{6,7},{7,6},{8,9},{9,8},{10,11... | collective-permute-start | bytes 82952 | tf_op jit(solution)/shard_map/ppermute | solution.py:294
  72.4 3.9 %spread.9 = f32[1024,256]{1,0:T(8,128)S(1)} custom-call(bf16[3328,128]{1,0:T(8,128)(2,1)S(1)} %get-tuple-element.111.refs_0_, bf16[3328,128]{1,0:T(8,128)(2,1)S(1)} %get-tuple-element.112.refs_1_, bf16[1024,3328]{1,0:T(8,128)(2,1)S(1)} %get-tuple-element.113.counts_ref.refs_2_, bf16[3328,128]{1,0:T(8,128)(2,1)S(1)} %get-tuple-element.114.refs_0_.refs_3_, ...), custom_call_target="tpu_custom_call" | custom-call | tf_op jit(solution)/shard_map/spread/pallas_call | solution.py:255
  76.3 0.8 collective-permute-done.19
  77.1 0.1 fusion
  77.2 0.6 collective-permute-start.20
  77.8 1.5 %collective-permute-start.21 = (bf16[1024,128]{1,0:T(8,128)(2,1)S(1)}, bf16[1024,128]{1,0:T(8,128)(2,1)S(1)}, u32[]{:S(2)}, u32[]{:S(2)}) collective-permute-start(bf16[1024,128]{1,0:T(8,128)(2,1)S(1)} %get-tuple-element.121), channel_id=1, source_target_pairs={{3,1},{5,3},{7,5},{6,7},{4,6},{2,4},{0,2},{1,0},{11,9},{13,11},{15... | collective-permute-start | bytes 786440 | tf_op jit(solution)/shard_map/ppermute | solution.py:394
  79.3 0.3 collective-permute-start.22
  79.6 4.4 %collective-permute-done.22 = f32[2,27,128]{2,1,0:T(8,128)S(1)} collective-permute-done((f32[2,27,128]{2,1,0:T(8,128)S(1)}, f32[2,27,128]{2,1,0:T(8,128)S(1)}, u32[]{:S(2)}, u32[]{:S(2)}) %collective-permute-start.22) | collective-permute-done | bytes 27680 | tf_op jit(solution)/shard_map/ppermute | solution.py:294
  84.0 0.2 collective-permute-done.21
  84.2 0.1 fusion.7
  84.3 1.8 %collective-permute-start.23 = (bf16[1024,128]{1,0:T(8,128)(2,1)S(1)}, bf16[1024,128]{1,0:T(8,128)(2,1)S(1)}, u32[]{:S(2)}, u32[]{:S(2)}) collective-permute-start(bf16[1024,128]{1,0:T(8,128)(2,1)S(1)} %fusion.7), channel_id=1, source_target_pairs={{0,16},{8,24},{16,0},{24,8},{1,17},{9,25},{17,1},{25,9},{2,18},{10... | collective-permute-start | bytes 786440 | tf_op jit(solution)/shard_map/ppermute | solution.py:294
  86.1 1.2 %collective-permute-start.24 = (f32[2,27,128]{2,1,0:T(8,128)S(1)}, f32[2,27,128]{2,1,0:T(8,128)S(1)}, u32[]{:S(2)}, u32[]{:S(2)}) collective-permute-start(f32[2,27,128]{2,1,0:T(8,128)S(1)} %add.79), channel_id=1, source_target_pairs={{0,4},{1,5},{2,6},{3,7},{4,0},{5,1},{6,2},{7,3},{8,12},{9,13},{10,... | collective-permute-start | bytes 82952 | tf_op jit(solution)/shard_map/ppermute | solution.py:294
  87.3 3.6 %collective-permute-done.24 = f32[2,27,128]{2,1,0:T(8,128)S(1)} collective-permute-done((f32[2,27,128]{2,1,0:T(8,128)S(1)}, f32[2,27,128]{2,1,0:T(8,128)S(1)}, u32[]{:S(2)}, u32[]{:S(2)}) %collective-permute-start.24) | collective-permute-done | bytes 27680 | tf_op jit(solution)/shard_map/ppermute | solution.py:294
  91.1 0.8 place_half.2.refs_0_
  91.9 0.6 slice_bitcast_fusion
  92.5 0.5 collective-permute-done.25.part_ref
  93.0 0.8 place_half.3
  (44 shorter events, 0.5 us)
Async XLA Ops:
  0.6 1.0 %copy-start = (bf16[2048,128]{1,0:T(8,128)(2,1)S(1)}, bf16[2048,128]{1,0:T(8,128)(2,1)}, u32[]{:S(2)}) copy-start(bf16[2048,128]{1,0:T(8,128)(2,1)} %param.11) | copy-start | bytes 1572868
  1.9 10.2 %collective-permute-start = (bf16[1024,128]{1,0:T(8,128)(2,1)S(1)}, bf16[1024,128]{1,0:T(8,128)(2,1)S(1)}, u32[]{:S(2)}, u32[]{:S(2)}) collective-permute-start(bf16[1024,128]{1,0:T(8,128)(2,1)S(1)} %bitcast.25), channel_id=1, source_target_pairs={{1,3},{3,5},{5,7},{7,6},{6,4},{4,2},{2,0},{0,1},{9,11},{11,13},{13... | collective-permute-start | bytes 786440 | tf_op jit(solution)/shard_map/ppermute | solution.py:344
  4.9 7.8 %collective-permute-start.1 = (bf16[1024,128]{1,0:T(8,128)(2,1)S(1)}, bf16[1024,128]{1,0:T(8,128)(2,1)S(1)}, u32[]{:S(2)}, u32[]{:S(2)}) collective-permute-start(bf16[1024,128]{1,0:T(8,128)(2,1)S(1)} %bitcast.26), channel_id=1, source_target_pairs={{3,1},{5,3},{7,5},{6,7},{4,6},{2,4},{0,2},{1,0},{11,9},{13,11},{15... | collective-permute-start | bytes 786440 | tf_op jit(solution)/shard_map/ppermute | solution.py:345
  6.7 5.4 %collective-permute-start.2 = (s32[26,8,128]{2,1,0:T(8,128)S(1)}, s32[26,8,128]{2,1,0:T(8,128)S(1)}, u32[]{:S(2)}, u32[]{:S(2)}) collective-permute-start(s32[26,8,128]{2,1,0:T(8,128)S(1)} %fusion.8.place_ref), channel_id=1, source_target_pairs={{0,8},{8,0},{16,24},{24,16},{1,9},{9,1},{17,25},{25,17},{2,10},{10... | collective-permute-start | bytes 319496 | tf_op jit(solution)/shard_map/ppermute | solution.py:294
  12.6 8.4 %collective-permute-start.3 = (bf16[1024,128]{1,0:T(8,128)(2,1)S(1)}, bf16[1024,128]{1,0:T(8,128)(2,1)S(1)}, u32[]{:S(2)}, u32[]{:S(2)}) collective-permute-start(bf16[1024,128]{1,0:T(8,128)(2,1)S(1)} %collective-permute-done.refs_2_), channel_id=1, source_target_pairs={{1,3},{3,5},{5,7},{7,6},{6,4},{4,2},{2,0},{0,1},{9,11},{11,13},{13... | collective-permute-start | bytes 786440 | tf_op jit(solution)/shard_map/ppermute | solution.py:344
  14.2 8.2 %collective-permute-start.4 = (bf16[1024,128]{1,0:T(8,128)(2,1)S(1)}, bf16[1024,128]{1,0:T(8,128)(2,1)S(1)}, u32[]{:S(2)}, u32[]{:S(2)}) collective-permute-start(bf16[1024,128]{1,0:T(8,128)(2,1)S(1)} %collective-permute-done.1.refs_1_), channel_id=1, source_target_pairs={{3,1},{5,3},{7,5},{6,7},{4,6},{2,4},{0,2},{1,0},{11,9},{13,11},{15... | collective-permute-start | bytes 786440 | tf_op jit(solution)/shard_map/ppermute | solution.py:345
  22.4 9.9 %collective-permute-start.5 = (bf16[1024,128]{1,0:T(8,128)(2,1)S(1)}, bf16[1024,128]{1,0:T(8,128)(2,1)S(1)}, u32[]{:S(2)}, u32[]{:S(2)}) collective-permute-start(bf16[1024,128]{1,0:T(8,128)(2,1)S(1)} %collective-permute-done.3.refs_1_), channel_id=1, source_target_pairs={{1,3},{3,5},{5,7},{7,6},{6,4},{4,2},{2,0},{0,1},{9,11},{11,13},{13... | collective-permute-start | bytes 786440 | tf_op jit(solution)/shard_map/ppermute | solution.py:344
  24.0 8.3 %collective-permute-start.6 = (bf16[1024,128]{1,0:T(8,128)(2,1)S(1)}, bf16[1024,128]{1,0:T(8,128)(2,1)S(1)}, u32[]{:S(2)}, u32[]{:S(2)}) collective-permute-start(bf16[1024,128]{1,0:T(8,128)(2,1)S(1)} %collective-permute-done.4.refs_0_), channel_id=1, source_target_pairs={{3,1},{5,3},{7,5},{6,7},{4,6},{2,4},{0,2},{1,0},{11,9},{13,11},{15... | collective-permute-start | bytes 786440 | tf_op jit(solution)/shard_map/ppermute | solution.py:345
  27.3 2.8 %copy-start.1 = (bf16[3456,512]{1,0:T(8,128)(2,1)S(1)}, bf16[3456,512]{1,0:T(8,128)(2,1)}, u32[]{:S(2)}) copy-start(bf16[3456,512]{1,0:T(8,128)(2,1)} %down_ref.1) | copy-start | bytes 10616836
  27.3 3.1 %copy-start.2 = (bf16[512,3456]{1,0:T(8,128)(2,1)S(1)}, bf16[512,3456]{1,0:T(8,128)(2,1)}, u32[]{:S(2)}) copy-start(bf16[512,3456]{1,0:T(8,128)(2,1)} %up_ref.1) | copy-start | bytes 10616836
  32.3 6.0 %collective-permute-start.7 = (bf16[512,128]{1,0:T(8,128)(2,1)S(1)}, bf16[512,128]{1,0:T(8,128)(2,1)S(1)}, u32[]{:S(2)}, u32[]{:S(2)}) collective-permute-start(bf16[512,128]{1,0:T(8,128)(2,1)S(1)} %slice.57), channel_id=1, source_target_pairs={{1,3},{3,5},{5,7},{7,6},{6,4},{4,2},{2,0},{0,1},{9,11},{11,13},{13... | collective-permute-start | bytes 393224 | tf_op jit(solution)/shard_map/ppermute | solution.py:359
  34.0 5.0 %collective-permute-start.8 = (bf16[512,128]{1,0:T(8,128)(2,1)S(1)}, bf16[512,128]{1,0:T(8,128)(2,1)S(1)}, u32[]{:S(2)}, u32[]{:S(2)}) collective-permute-start(bf16[512,128]{1,0:T(8,128)(2,1)S(1)} %slice.58), channel_id=1, source_target_pairs={{3,1},{5,3},{7,5},{6,7},{4,6},{2,4},{0,2},{1,0},{11,9},{13,11},{15... | collective-permute-start | bytes 393224 | tf_op jit(solution)/shard_map/ppermute | solution.py:359
  38.3 1.8 %copy-start.7 = (s32[128]{0:T(128)S(1)}, s32[128]{0:T(128)}, u32[]{:S(2)}) copy-start(s32[128]{0:T(128)} %param.16) | copy-start | bytes 1540
  40.0 3.7 %collective-permute-start.9 = (f32[128,3328]{1,0:T(8,128)S(1)}, f32[128,3328]{1,0:T(8,128)S(1)}, u32[]{:S(2)}, u32[]{:S(2)}) collective-permute-start(f32[128,3328]{1,0:T(8,128)S(1)} %pool.13), channel_id=1, source_target_pairs={{0,8},{8,0},{16,24},{24,16},{1,9},{9,1},{17,25},{25,17},{2,10},{10... | collective-permute-start | bytes 5111816 | tf_op jit(solution)/shard_map/ppermute | solution.py:294
  42.0 1.6 %copy-start.3 = (bf16[128,128]{1,0:T(8,128)(2,1)S(1)}, bf16[128,128]{1,0:T(8,128)(2,1)}, u32[]{:S(2)}) copy-start(bf16[128,128]{1,0:T(8,128)(2,1)} %dense_ref.1) | copy-start | bytes 98308
  42.1 1.6 %copy-start.4 = (f32[3456]{0:T(1024)S(1)}, f32[3456]{0:T(1024)}, u32[]{:S(2)}) copy-start(f32[3456]{0:T(1024)} %param.20) | copy-start | bytes 41476
  42.1 1.6 %copy-start.5 = (f32[3456]{0:T(1024)S(1)}, f32[3456]{0:T(1024)}, u32[]{:S(2)}) copy-start(f32[3456]{0:T(1024)} %param.21) | copy-start | bytes 41476
  42.1 1.6 %copy-start.6 = (f32[128]{0:T(128)S(1)}, f32[128]{0:T(128)}, u32[]{:S(2)}) copy-start(f32[128]{0:T(128)} %param.17) | copy-start | bytes 1540
  48.2 2.7 %collective-permute-start.10 = (bf16[3328,128]{1,0:T(8,128)(2,1)S(1)}, bf16[3328,128]{1,0:T(8,128)(2,1)S(1)}, u32[]{:S(2)}, u32[]{:S(2)}) collective-permute-start(bf16[3328,128]{1,0:T(8,128)(2,1)S(1)} %get-tuple-element.112.refs_1_), channel_id=1, source_target_pairs={{0,8},{8,0},{16,24},{24,16},{1,9},{9,1},{17,25},{25,17},{2,10},{10... | collective-permute-start | bytes 2555912 | tf_op jit(solution)/shard_map/ppermute | solution.py:294
  48.4 2.5 %collective-permute-start.11 = (f32[2,27,128]{2,1,0:T(8,128)S(1)}, f32[2,27,128]{2,1,0:T(8,128)S(1)}, u32[]{:S(2)}, u32[]{:S(2)}) collective-permute-start(f32[2,27,128]{2,1,0:T(8,128)S(1)} %get-tuple-element.93), channel_id=1, source_target_pairs={{0,8},{8,0},{16,24},{24,16},{1,9},{9,1},{17,25},{25,17},{2,10},{10... | collective-permute-start | bytes 82952 | tf_op jit(solution)/shard_map/ppermute | solution.py:294
  53.4 6.0 %collective-permute-start.12 = (bf16[512,128]{1,0:T(8,128)(2,1)S(1)}, bf16[512,128]{1,0:T(8,128)(2,1)S(1)}, u32[]{:S(2)}, u32[]{:S(2)}) collective-permute-start(bf16[512,128]{1,0:T(8,128)(2,1)S(1)} %get-tuple-element.135), channel_id=1, source_target_pairs={{1,3},{3,5},{5,7},{7,6},{6,4},{4,2},{2,0},{0,1},{9,11},{11,13},{13... | collective-permute-start | bytes 393224 | tf_op jit(solution)/shard_map/ppermute | solution.py:394
  55.0 5.3 %collective-permute-start.13 = (bf16[512,128]{1,0:T(8,128)(2,1)S(1)}, bf16[512,128]{1,0:T(8,128)(2,1)S(1)}, u32[]{:S(2)}, u32[]{:S(2)}) collective-permute-start(bf16[512,128]{1,0:T(8,128)(2,1)S(1)} %get-tuple-element.134), channel_id=1, source_target_pairs={{3,1},{5,3},{7,5},{6,7},{4,6},{2,4},{0,2},{1,0},{11,9},{13,11},{15... | collective-permute-start | bytes 393224 | tf_op jit(solution)/shard_map/ppermute | solution.py:394
  60.3 7.5 %collective-permute-start.14 = (bf16[1024,128]{1,0:T(8,128)(2,1)S(1)}, bf16[1024,128]{1,0:T(8,128)(2,1)S(1)}, u32[]{:S(2)}, u32[]{:S(2)}) collective-permute-start(bf16[1024,128]{1,0:T(8,128)(2,1)S(1)} %get-tuple-element.108), channel_id=1, source_target_pairs={{1,3},{3,5},{5,7},{7,6},{6,4},{4,2},{2,0},{0,1},{9,11},{11,13},{13... | collective-permute-start | bytes 786440 | tf_op jit(solution)/shard_map/ppermute | solution.py:394
  61.9 6.9 %collective-permute-start.15 = (bf16[1024,128]{1,0:T(8,128)(2,1)S(1)}, bf16[1024,128]{1,0:T(8,128)(2,1)S(1)}, u32[]{:S(2)}, u32[]{:S(2)}) collective-permute-start(bf16[1024,128]{1,0:T(8,128)(2,1)S(1)} %get-tuple-element.109), channel_id=1, source_target_pairs={{3,1},{5,3},{7,5},{6,7},{4,6},{2,4},{0,2},{1,0},{11,9},{13,11},{15... | collective-permute-start | bytes 786440 | tf_op jit(solution)/shard_map/ppermute | solution.py:394
  62.4 5.4 %collective-permute-start.16 = (f32[2,27,128]{2,1,0:T(8,128)S(1)}, f32[2,27,128]{2,1,0:T(8,128)S(1)}, u32[]{:S(2)}, u32[]{:S(2)}) collective-permute-start(f32[2,27,128]{2,1,0:T(8,128)S(1)} %add.68), channel_id=1, source_target_pairs={{0,16},{8,24},{16,0},{24,8},{1,17},{9,25},{17,1},{25,9},{2,18},{10... | collective-permute-start | bytes 82952 | tf_op jit(solution)/shard_map/ppermute | solution.py:294
  68.9 8.2 %collective-permute-start.17 = (bf16[1024,128]{1,0:T(8,128)(2,1)S(1)}, bf16[1024,128]{1,0:T(8,128)(2,1)S(1)}, u32[]{:S(2)}, u32[]{:S(2)}) collective-permute-start(bf16[1024,128]{1,0:T(8,128)(2,1)S(1)} %get-tuple-element.117), channel_id=1, source_target_pairs={{1,3},{3,5},{5,7},{7,6},{6,4},{4,2},{2,0},{0,1},{9,11},{11,13},{13... | collective-permute-start | bytes 786440 | tf_op jit(solution)/shard_map/ppermute | solution.py:394
  70.3 6.8 %collective-permute-start.18 = (bf16[1024,128]{1,0:T(8,128)(2,1)S(1)}, bf16[1024,128]{1,0:T(8,128)(2,1)S(1)}, u32[]{:S(2)}, u32[]{:S(2)}) collective-permute-start(bf16[1024,128]{1,0:T(8,128)(2,1)S(1)} %get-tuple-element.118), channel_id=1, source_target_pairs={{3,1},{5,3},{7,5},{6,7},{4,6},{2,4},{0,2},{1,0},{11,9},{13,11},{15... | collective-permute-start | bytes 786440 | tf_op jit(solution)/shard_map/ppermute | solution.py:394
  71.0 6.1 %collective-permute-start.19 = (f32[2,27,128]{2,1,0:T(8,128)S(1)}, f32[2,27,128]{2,1,0:T(8,128)S(1)}, u32[]{:S(2)}, u32[]{:S(2)}) collective-permute-start(f32[2,27,128]{2,1,0:T(8,128)S(1)} %add.73), channel_id=1, source_target_pairs={{0,1},{1,0},{2,3},{3,2},{4,5},{5,4},{6,7},{7,6},{8,9},{9,8},{10,11... | collective-permute-start | bytes 82952 | tf_op jit(solution)/shard_map/ppermute | solution.py:294
  77.2 6.8 %collective-permute-start.20 = (bf16[1024,128]{1,0:T(8,128)(2,1)S(1)}, bf16[1024,128]{1,0:T(8,128)(2,1)S(1)}, u32[]{:S(2)}, u32[]{:S(2)}) collective-permute-start(bf16[1024,128]{1,0:T(8,128)(2,1)S(1)} %get-tuple-element.120), channel_id=1, source_target_pairs={{1,3},{3,5},{5,7},{7,6},{6,4},{4,2},{2,0},{0,1},{9,11},{11,13},{13... | collective-permute-start | bytes 786440 | tf_op jit(solution)/shard_map/ppermute | solution.py:394
  77.8 6.4 %collective-permute-start.21 = (bf16[1024,128]{1,0:T(8,128)(2,1)S(1)}, bf16[1024,128]{1,0:T(8,128)(2,1)S(1)}, u32[]{:S(2)}, u32[]{:S(2)}) collective-permute-start(bf16[1024,128]{1,0:T(8,128)(2,1)S(1)} %get-tuple-element.121), channel_id=1, source_target_pairs={{3,1},{5,3},{7,5},{6,7},{4,6},{2,4},{0,2},{1,0},{11,9},{13,11},{15... | collective-permute-start | bytes 786440 | tf_op jit(solution)/shard_map/ppermute | solution.py:394
  79.3 4.7 %collective-permute-start.22 = (f32[2,27,128]{2,1,0:T(8,128)S(1)}, f32[2,27,128]{2,1,0:T(8,128)S(1)}, u32[]{:S(2)}, u32[]{:S(2)}) collective-permute-start(f32[2,27,128]{2,1,0:T(8,128)S(1)} %add.76), channel_id=1, source_target_pairs={{0,2},{1,3},{2,0},{3,1},{4,6},{5,7},{6,4},{7,5},{8,10},{9,11},{10,... | collective-permute-start | bytes 82952 | tf_op jit(solution)/shard_map/ppermute | solution.py:294
  84.3 6.6 %collective-permute-start.23 = (bf16[1024,128]{1,0:T(8,128)(2,1)S(1)}, bf16[1024,128]{1,0:T(8,128)(2,1)S(1)}, u32[]{:S(2)}, u32[]{:S(2)}) collective-permute-start(bf16[1024,128]{1,0:T(8,128)(2,1)S(1)} %fusion.7), channel_id=1, source_target_pairs={{0,16},{8,24},{16,0},{24,8},{1,17},{9,25},{17,1},{25,9},{2,18},{10... | collective-permute-start | bytes 786440 | tf_op jit(solution)/shard_map/ppermute | solution.py:294
  86.1 4.8 %collective-permute-start.24 = (f32[2,27,128]{2,1,0:T(8,128)S(1)}, f32[2,27,128]{2,1,0:T(8,128)S(1)}, u32[]{:S(2)}, u32[]{:S(2)}) collective-permute-start(f32[2,27,128]{2,1,0:T(8,128)S(1)} %add.79), channel_id=1, source_target_pairs={{0,4},{1,5},{2,6},{3,7},{4,0},{5,1},{6,2},{7,3},{8,12},{9,13},{10,... | collective-permute-start | bytes 82952 | tf_op jit(solution)/shard_map/ppermute | solution.py:294
  91.0 2.0 %collective-permute-start.25 = (f32[1024,128]{1,0:T(8,128)S(1)}, f32[1024,128]{1,0:T(8,128)S(1)}, u32[]{:S(2)}, u32[]{:S(2)}) collective-permute-start(f32[1024,128]{1,0:T(8,128)S(1)} %convert_add_fusion.part_ref), channel_id=1, source_target_pairs={{0,8},{8,0},{16,24},{24,16},{1,9},{9,1},{17,25},{25,17},{2,10},{10... | collective-permute-start | bytes 1572872 | tf_op jit(solution)/shard_map/ppermute | solution.py:294

commit v2 on v1

--- a/solution.py
+++ b/solution.py
@@ -35,7 +35,17 @@
     )
 
 
-def count_kernel(owners, local_rows, where_ref, place_ref, counts_ref, turn_ref, column_ref):
+def side_by_side(blocks):
+    tiles = [ref[row : row + LANES, :] for ref in blocks for row in range(0, ref.shape[0], LANES)]
+    return jnp.concatenate(tiles, axis=1)
+
+
+def count_kernel(owners, local_rows, turns, where_ref, place_ref, *refs):
+    if turns:
+        counts_ref, turn_ref, column_ref, sum_ref = refs[-4:]
+        own_turn_ref, own_counts_ref, blocks = refs[0], refs[1], refs[2:-4]
+    else:
+        counts_ref, turn_ref, column_ref = refs
     tables, hot, _ = place_ref.shape
     rows = counts_ref.shape[0]
     high = rows // LANES
@@ -74,26 +84,48 @@
                 counts_ref[start : start + CHUNK, lanes] = count.astype(F32).astype(BF16)
         return carry
 
-    lax.fori_loop(0, tables, table, 0, unroll=2)
-
-
-def bag_counts(where, place, owners, local_rows):
+    def pair(at, carry):
+        lanes = pl.ds(pl.multiple_of(at * 2 * LANES, 2 * LANES), 2 * LANES)
+        left = jnp.concatenate([side_by_side([block]) for block in blocks], axis=0)
+        product = jnp.dot(left, own_counts_ref[:, lanes], preferred_element_type=F32)
+        for one in range(2):
+            table(2 * at + one, 0)
+        total = []
+        for one in range(2):
+            turn = own_turn_ref[pl.ds(2 * at + one, 1), :]
+            part = 0.0
+            for i, each in enumerate(turns):
+                mine = product[i * LANES : (i + 1) * LANES, one * LANES : (one + 1) * LANES]
+                part = jnp.where(turn == each, mine, part)
+            total.append(part)
+        sum_ref[:, lanes] = jnp.concatenate(total, axis=1)
+        return carry
+
+    if turns:
+        lax.fori_loop(0, tables // 2, pair, 0)
+    else:
+        lax.fori_loop(0, tables, table, 0, unroll=2)
+
+
+def bag_counts(where, place, owners, local_rows, turns=(), own=(), shards=()):
     tables, hot, samples = place.shape
     bags = tables * samples
     rows = local_rows // 2
+    operands = [*own, *shards] if turns else []
+    out_shape = (
+        jax.ShapeDtypeStruct((rows, bags), BF16),
+        jax.ShapeDtypeStruct((tables, samples), F32),
+        jax.ShapeDtypeStruct((bags, LANES), BF16),
+    ) + ((jax.ShapeDtypeStruct((LANES, bags), F32),) if turns else ())
     return pl.pallas_call(
-        functools.partial(count_kernel, owners, local_rows),
-        out_shape=(
-            jax.ShapeDtypeStruct((rows, bags), BF16),
-            jax.ShapeDtypeStruct((tables, samples), F32),
-            jax.ShapeDtypeStruct((bags, LANES), BF16),
-        ),
-        in_specs=[pl.BlockSpec(memory_space=pltpu.SMEM), VMEM],
-        out_specs=(VMEM, VMEM, VMEM),
+        functools.partial(count_kernel, owners, local_rows, turns),
+        out_shape=out_shape,
+        in_specs=[pl.BlockSpec(memory_space=pltpu.SMEM)] + [VMEM] * (1 + len(operands)),
+        out_specs=(VMEM,) * len(out_shape),
         compiler_params=params(),
         cost_estimate=cost(5 * 10**9, 0),
         name="bag_counts",
-    )(where, place)
+    )(where, place, *operands)
 
 
 def pool_kernel(shards, turns, tables, added, turn_ref, counts_ref, *refs):
@@ -102,12 +134,7 @@
     before = refs[sum(shards) : sum(shards) + added]
     left, at = [], 0
     for parts in shards:
-        tiles = [
-            ref[row : row + LANES, :]
-            for ref in blocks[at : at + parts]
-            for row in range(0, ref.shape[0], LANES)
-        ]
-        left.append(jnp.concatenate(tiles, axis=1))
+        left.append(side_by_side(blocks[at : at + parts]))
         at += parts
     left = jnp.concatenate(left, axis=0)
     for start in range(0, turn_ref.shape[0], tables):
@@ -347,22 +374,24 @@
 
     step(None)
     own, places[1] = step((count(places[0]), places[1]))
-    sides = list(step([own, count(places[1])]))
     near = (0, 1, 7), [[shard], [rights[1]], [lefts[1]]]
+    *lent, sums[0] = bag_counts(
+        where, places[1], owners, local_rows, near[0], (own[1], own[0]), [one for one, in near[1]]
+    )
+    *sides, sums[0] = step([own, lent, sums[0]])
     add(1, *near)
     add(1, (2, 6), [[rights[2]], [lefts[2]]], ahead)
-    add(0, *near)
+    add(0, (2, 6), [[rights[2]], [lefts[2]]])
     middle = shard.shape[0] // 2
     a, b, sums[0], sums[1] = lax.optimization_barrier(
         (lefts[3][:middle], rights[3][middle:], sums[0], sums[1])
     )
     far = [lax.ppermute(a, "emb", right), lax.ppermute(b, "emb", left)]
-    add(0, (2, 6), [[rights[2]], [lefts[2]]])
-    add(1, (3, 5), [[rights[3]], [lefts[3]]])
-    add(1, (4,), [far])
+    for side in (1, 0):
+        add(side, (3, 5), [[rights[3]], [lefts[3]]])
     sums[0], sums[1] = lax.optimization_barrier((sums[0], sums[1]))
-    add(0, (3, 5), [[rights[3]], [lefts[3]]])
-    add(0, (4,), [far])
+    for side in (1, 0):
+        add(side, (4,), [far])
     return sides, sums
 
 

time: 94.2 us -> 93.3 us (level)
    pallas_call x8 -> x7, Pallas kernels: 15.5 us -> 12.7 us  [pool(): pl.pallas_call(functools.partial(pool_kernel, [len(shard) for shard in sh...]
    pallas_call x2, Pallas kernels: 10.4 us -> 12.6 us  [bag_counts(): pl.pallas_call(functools.partial(count_kernel, owners, local_rows, turns)...]
    ppermute x10, waiting for transfers between devices: 9.82 us -> 11.5 us  [swap(): return lax.ppermute(value, axis, [(i, i ^ stride) for i in range(size)])]
    ppermute x3, waiting for transfers between devices: 1.19 us -> 0.01 us  [step(): lefts.append(lax.ppermute(a, 'emb', right))]
    ppermute x3, waiting for transfers between devices: 1.96 us -> 0.86 us  [step(): rights.append(lax.ppermute(b, 'emb', left))]
  transfers between devices with their start and end apart: 26 -> 26, of which waited for: 12 -> 11; matrix products, arithmetic and copies ran while one was open for 3% -> 3% of each run, Pallas kernels for 42% -> 42%
where the time goes in v2:
time: 93.3 us; the launch traced here: 93 us
  Pallas kernels  47.3 us (51%)
  starting transfers between devices  24.5 us (26%)
  waiting for transfers between devices  15.3 us (16%)
  local copies, waits for them, and re-layouts  2.42 us (3%)
  other arithmetic  2.2 us (2%)
  between operations  1.27 us (1%)
    pallas_call x5, Pallas kernels, spread(): pl.pallas_call(functools.partial(spread_kernel, turns, len(sides), at), o...  16 us
    pallas_call x7, Pallas kernels, pool(): pl.pallas_call(functools.partial(pool_kernel, [len(shard) for shard in sh...  12.7 us
    pallas_call x2, Pallas kernels, bag_counts(): pl.pallas_call(functools.partial(count_kernel, owners, local_rows, turns)...  12.6 us
    ppermute x10, waiting for transfers between devices, swap(): return lax.ppermute(value, axis, [(i, i ^ stride) for i in range(size)])  11.5 us
    ppermute x10, starting transfers between devices, swap(): return lax.ppermute(value, axis, [(i, i ^ stride) for i in range(size)])  6.96 us
    ppermute x3, starting transfers between devices, step(): lefts.append(lax.ppermute(a, 'emb', right))  6.14 us
    ppermute x4, starting transfers between devices, send(): lax.ppermute(to_right, 'emb', right)  5.46 us
    pallas_call x1, Pallas kernels, cross_layer(): pl.pallas_call(functools.partial(cross_kernel, tables), out_shape=(jax.Sh...  4.45 us
  transfers between devices with their start and end apart: 26, of which 11 were waited for; matrix products, arithmetic and copies ran while one was open for 3% of the time, Pallas kernels for 42%

profile of v2, /device:TPU:0, one launch (start us, length us, event | category | flops | bytes accessed | tf_op | source)
XLA Modules:
  0.0 93.0 jit_solution(10852834132949574850)
XLA Ops:
  0.7 1.0 %copy-done = bf16[2048,128]{1,0:T(8,128)(2,1)S(1)} copy-done((bf16[2048,128]{1,0:T(8,128)(2,1)S(1)}, bf16[2048,128]{1,0:T(8,128)(2,1)}, u32[]{:S(2)}) %copy-start) | copy-done | bytes 524312
  1.7 0.2 copy.16
  1.9 3.0 %collective-permute-start = (bf16[1024,128]{1,0:T(8,128)(2,1)S(1)}, bf16[1024,128]{1,0:T(8,128)(2,1)S(1)}, u32[]{:S(2)}, u32[]{:S(2)}) collective-permute-start(bf16[1024,128]{1,0:T(8,128)(2,1)S(1)} %bitcast.25), channel_id=1, source_target_pairs={{1,3},{3,5},{5,7},{7,6},{6,4},{4,2},{2,0},{0,1},{9,11},{11,13},{13... | collective-permute-start | bytes 786440 | tf_op jit(solution)/shard_map/ppermute | solution.py:371
  4.9 0.2 collective-permute-start.1
  5.0 0.7 multiply_bitcast_fusion
  5.8 0.9 fusion.8.place_ref
  6.7 0.1 collective-permute-start.2
  6.8 0.1 pad_add_fusion.where_ref
  6.8 5.2 %bag_counts.2 = (bf16[1024,3328]{1,0:T(8,128)(2,1)S(1)}, f32[26,128]{1,0:T(8,128)S(1)}, bf16[3328,128]{1,0:T(8,128)(2,1)S(1)}) custom-call(s32[2]{0:T(128)S(1)} %pad_add_fusion.where_ref, s32[26,8,128]{2,1,0:T(8,128)S(1)} %fusion.8.place_ref), custom_call_target="tpu_custom_call" | custom-call | flops 5000000000 | tf_op jit(solution)/shard_map/bag_counts/pallas_call | solution.py:120
  12.1 0.6 collective-permute-done.1.refs_3_.refs_1_
  12.6 1.6 %collective-permute-start.3 = (bf16[1024,128]{1,0:T(8,128)(2,1)S(1)}, bf16[1024,128]{1,0:T(8,128)(2,1)S(1)}, u32[]{:S(2)}, u32[]{:S(2)}) collective-permute-start(bf16[1024,128]{1,0:T(8,128)(2,1)S(1)} %collective-permute-done.refs_4_.refs_2_), channel_id=1, source_target_pairs={{1,3},{3,5},{5,7},{7,6},{6,4},{4,2},{2,0},{0,1},{9,11},{11,13},{13... | collective-permute-start | bytes 786440 | tf_op jit(solution)/shard_map/ppermute | solution.py:371
  14.2 0.4 collective-permute-start.4
  14.7 7.5 %bag_counts.3 = (bf16[1024,3328]{1,0:T(8,128)(2,1)S(1)}, f32[26,128]{1,0:T(8,128)S(1)}, bf16[3328,128]{1,0:T(8,128)(2,1)S(1)}, f32[128,3328]{1,0:T(8,128)S(1)}) custom-call(s32[2]{0:T(128)S(1)} %pad_add_fusion.where_ref, s32[26,8,128]{2,1,0:T(8,128)S(1)} %collective-permute-done.2.place_ref, f32[26,128]{1,0:T(8,128)S(1)} %get-tuple-element.82.refs_0_.turn_ref, ...), custom_call_target="tpu_custom_call" | custom-call | flops 5000000000 | tf_op jit(solution)/shard_map/bag_counts/pallas_call | solution.py:120
  22.1 0.3 collective-permute-done.4.refs_0_
  22.4 1.6 %collective-permute-start.5 = (bf16[1024,128]{1,0:T(8,128)(2,1)S(1)}, bf16[1024,128]{1,0:T(8,128)(2,1)S(1)}, u32[]{:S(2)}, u32[]{:S(2)}) collective-permute-start(bf16[1024,128]{1,0:T(8,128)(2,1)S(1)} %collective-permute-done.3.refs_1_), channel_id=1, source_target_pairs={{1,3},{3,5},{5,7},{7,6},{6,4},{4,2},{2,0},{0,1},{9,11},{11,13},{13... | collective-permute-start | bytes 786440 | tf_op jit(solution)/shard_map/ppermute | solution.py:371
  24.0 0.4 collective-permute-start.6
  24.5 2.8 %pool.8.refs_2_ = f32[128,3328]{1,0:T(8,128)S(1)} custom-call(f32[26,128]{1,0:T(8,128)S(1)} %get-tuple-element.87.turn_ref, bf16[1024,3328]{1,0:T(8,128)(2,1)S(1)} %get-tuple-element.120.counts_ref.refs_2_.refs_5_, bf16[1024,128]{1,0:T(8,128)(2,1)S(1)} %bitcast.28, bf16[1024,128]{1,0:T(8,128)(2,1)S(1)} %collective-permute-done.1.refs_3_.refs_1_, ...), custom_call_target="tpu_custom_call" | custom-call | tf_op jit(solution)/shard_map/pool/pallas_call | solution.py:159
  27.3 0.3 copy-done.2
  27.5 1.9 %pool.9.refs_2_ = f32[128,3328]{1,0:T(8,128)S(1)} custom-call(f32[26,128]{1,0:T(8,128)S(1)} %get-tuple-element.87.turn_ref, bf16[1024,3328]{1,0:T(8,128)(2,1)S(1)} %get-tuple-element.120.counts_ref.refs_2_.refs_5_, bf16[1024,128]{1,0:T(8,128)(2,1)S(1)} %collective-permute-done.4.refs_0_, bf16[1024,128]{1,0:T(8,128)(2,1)S(1)} %collective-permute-done.3.refs_1_, ...), custom_call_target="tpu_custom_call" | custom-call | tf_op jit(solution)/shard_map/pool/pallas_call | solution.py:159
  29.5 1.9 %pool.7.refs_2_ = f32[128,3328]{1,0:T(8,128)S(1)} custom-call(f32[26,128]{1,0:T(8,128)S(1)} %get-tuple-element.82.refs_0_.turn_ref, bf16[1024,3328]{1,0:T(8,128)(2,1)S(1)} %get-tuple-element.117.refs_1_.counts_ref.refs_2_, bf16[1024,128]{1,0:T(8,128)(2,1)S(1)} %collective-permute-done.4.refs_0_, bf16[1024,128]{1,0:T(8,128)(2,1)S(1)} %collective-permute-done.3.refs_1_, ...), custom_call_target="tpu_custom_call" | custom-call | tf_op jit(solution)/shard_map/pool/pallas_call | solution.py:159
  31.5 1.6 %collective-permute-start.7 = (bf16[512,128]{1,0:T(8,128)(2,1)S(1)}, bf16[512,128]{1,0:T(8,128)(2,1)S(1)}, u32[]{:S(2)}, u32[]{:S(2)}) collective-permute-start(bf16[512,128]{1,0:T(8,128)(2,1)S(1)} %slice.57), channel_id=1, source_target_pairs={{1,3},{3,5},{5,7},{7,6},{6,4},{4,2},{2,0},{0,1},{9,11},{11,13},{13... | collective-permute-start | bytes 393224 | tf_op jit(solution)/shard_map/ppermute | solution.py:389
  33.1 0.4 collective-permute-start.8
  33.5 1.9 %pool.11.refs_2_ = f32[128,3328]{1,0:T(8,128)S(1)} custom-call(f32[26,128]{1,0:T(8,128)S(1)} %get-tuple-element.87.turn_ref, bf16[1024,3328]{1,0:T(8,128)(2,1)S(1)} %get-tuple-element.120.counts_ref.refs_2_.refs_5_, bf16[1024,128]{1,0:T(8,128)(2,1)S(1)} %collective-permute-done.6.refs_0_, bf16[1024,128]{1,0:T(8,128)(2,1)S(1)} %collective-permute-done.5.refs_1_, ...), custom_call_target="tpu_custom_call" | custom-call | tf_op jit(solution)/shard_map/pool/pallas_call | solution.py:159
  35.5 2.0 %pool.10.refs_2_ = f32[128,3328]{1,0:T(8,128)S(1)} custom-call(f32[26,128]{1,0:T(8,128)S(1)} %get-tuple-element.82.refs_0_.turn_ref, bf16[1024,3328]{1,0:T(8,128)(2,1)S(1)} %get-tuple-element.117.refs_1_.counts_ref.refs_2_, bf16[1024,128]{1,0:T(8,128)(2,1)S(1)} %collective-permute-done.6.refs_0_, bf16[1024,128]{1,0:T(8,128)(2,1)S(1)} %collective-permute-done.5.refs_1_, ...), custom_call_target="tpu_custom_call" | custom-call | tf_op jit(solution)/shard_map/pool/pallas_call | solution.py:159
  37.5 0.6 collective-permute-done.8.refs_1_
  38.1 1.1 %pool.13 = f32[128,3328]{1,0:T(8,128)S(1)} custom-call(f32[26,128]{1,0:T(8,128)S(1)} %get-tuple-element.87.turn_ref, bf16[1024,3328]{1,0:T(8,128)(2,1)S(1)} %get-tuple-element.120.counts_ref.refs_2_.refs_5_, bf16[512,128]{1,0:T(8,128)(2,1)S(1)} %collective-permute-done.7.refs_0_, bf16[512,128]{1,0:T(8,128)(2,1)S(1)} %collective-permute-done.8.refs_1_, ...), custom_call_target="tpu_custom_call" | custom-call | tf_op jit(solution)/shard_map/pool/pallas_call | solution.py:159
  39.3 1.1 %pool.12.own_ref = f32[128,3328]{1,0:T(8,128)S(1)} custom-call(f32[26,128]{1,0:T(8,128)S(1)} %get-tuple-element.82.refs_0_.turn_ref, bf16[1024,3328]{1,0:T(8,128)(2,1)S(1)} %get-tuple-element.117.refs_1_.counts_ref.refs_2_, bf16[512,128]{1,0:T(8,128)(2,1)S(1)} %collective-permute-done.7.refs_0_, bf16[512,128]{1,0:T(8,128)(2,1)S(1)} %collective-permute-done.8.refs_1_, ...), custom_call_target="tpu_custom_call" | custom-call | tf_op jit(solution)/shard_map/pool/pallas_call | solution.py:159
  40.3 2.5 %collective-permute-done.9.other_ref = f32[128,3328]{1,0:T(8,128)S(1)} collective-permute-done((f32[128,3328]{1,0:T(8,128)S(1)}, f32[128,3328]{1,0:T(8,128)S(1)}, u32[]{:S(2)}, u32[]{:S(2)}) %collective-permute-start.9) | collective-permute-done | bytes 1703968 | tf_op jit(solution)/shard_map/ppermute | solution.py:321
  42.8 4.4 %cross_layer.1 = (bf16[3328,128]{1,0:T(8,128)(2,1)S(1)}, bf16[128,128]{1,0:T(8,128)(2,1)}, f32[2,27,128]{2,1,0:T(8,128)S(1)}) custom-call(bf16[128,128]{1,0:T(8,128)(2,1)S(1)} %copy-done.3, f32[128,3328]{1,0:T(8,128)S(1)} %pool.12.own_ref, f32[128,3328]{1,0:T(8,128)S(1)} %collective-permute-done.9.other_ref, f32[1,128]{1,0:T(1,128)S(1)} %convert_bitcast_fusion.label_ref, ...), custom_call_target="tpu_custom_call" | custom-call | flops 8000000000 | bytes 12000000 | tf_op jit(solution)/shard_map/cross_layer/pallas_call | solution.py:242
  47.3 0.2 collective-permute-start.10
  47.5 0.4 collective-permute-start.11
  47.8 2.1 %spread.5.refs_3_ = f32[1024,256]{1,0:T(8,128)S(1)} custom-call(bf16[3328,128]{1,0:T(8,128)(2,1)S(1)} %get-tuple-element.115.refs_0_, bf16[3328,128]{1,0:T(8,128)(2,1)S(1)} %get-tuple-element.116.refs_1_, bf16[1024,3328]{1,0:T(8,128)(2,1)S(1)} %get-tuple-element.117.refs_1_.counts_ref.refs_2_), custom_call_target="tpu_custom_call" | custom-call | tf_op jit(solution)/shard_map/spread/pallas_call | solution.py:282
  50.0 2.1 %spread.6 = f32[1024,256]{1,0:T(8,128)S(1)} custom-call(bf16[3328,128]{1,0:T(8,128)(2,1)S(1)} %get-tuple-element.118.refs_0_.refs_3_, bf16[3328,128]{1,0:T(8,128)(2,1)S(1)} %collective-permute-done.10.refs_1_.refs_4_, bf16[1024,3328]{1,0:T(8,128)(2,1)S(1)} %get-tuple-element.120.counts_ref.refs_2_.refs_5_, f32[1024,256]{1,0:T(8,128)S(1)} %spread.5.refs_3_), custom_call_target="tpu_custom_call" | custom-call | tf_op jit(solution)/shard_map/spread/pallas_call | solution.py:282
  52.2 0.2 fusion.9
  52.4 1.6 %collective-permute-start.12 = (bf16[512,128]{1,0:T(8,128)(2,1)S(1)}, bf16[512,128]{1,0:T(8,128)(2,1)S(1)}, u32[]{:S(2)}, u32[]{:S(2)}) collective-permute-start(bf16[512,128]{1,0:T(8,128)(2,1)S(1)} %get-tuple-element.139), channel_id=1, source_target_pairs={{1,3},{3,5},{5,7},{7,6},{6,4},{4,2},{2,0},{0,1},{9,11},{11,13},{13... | collective-permute-start | bytes 393224 | tf_op jit(solution)/shard_map/ppermute | solution.py:423
  54.0 0.5 collective-permute-start.13
  54.5 3.9 %spread.7 = f32[1024,256]{1,0:T(8,128)S(1)} custom-call(bf16[3328,128]{1,0:T(8,128)(2,1)S(1)} %get-tuple-element.115.refs_0_, bf16[3328,128]{1,0:T(8,128)(2,1)S(1)} %get-tuple-element.116.refs_1_, bf16[1024,3328]{1,0:T(8,128)(2,1)S(1)} %get-tuple-element.117.refs_1_.counts_ref.refs_2_, bf16[3328,128]{1,0:T(8,128)(2,1)S(1)} %get-tuple-element.118.refs_0_.refs_3_, ...), custom_call_target="tpu_custom_call" | custom-call | tf_op jit(solution)/shard_map/spread/pallas_call | solution.py:282
  58.4 0.8 collective-permute-done.13
  59.3 0.1 fusion.4
  59.4 1.6 %collective-permute-start.14 = (bf16[1024,128]{1,0:T(8,128)(2,1)S(1)}, bf16[1024,128]{1,0:T(8,128)(2,1)S(1)}, u32[]{:S(2)}, u32[]{:S(2)}) collective-permute-start(bf16[1024,128]{1,0:T(8,128)(2,1)S(1)} %get-tuple-element.112), channel_id=1, source_target_pairs={{1,3},{3,5},{5,7},{7,6},{6,4},{4,2},{2,0},{0,1},{9,11},{11,13},{13... | collective-permute-start | bytes 786440 | tf_op jit(solution)/shard_map/ppermute | solution.py:423
  61.0 0.4 collective-permute-start.15
  61.5 1.5 %collective-permute-start.16 = (f32[2,27,128]{2,1,0:T(8,128)S(1)}, f32[2,27,128]{2,1,0:T(8,128)S(1)}, u32[]{:S(2)}, u32[]{:S(2)}) collective-permute-start(f32[2,27,128]{2,1,0:T(8,128)S(1)} %add.68), channel_id=1, source_target_pairs={{0,16},{8,24},{16,0},{24,8},{1,17},{9,25},{17,1},{25,9},{2,18},{10... | collective-permute-start | bytes 82952 | tf_op jit(solution)/shard_map/ppermute | solution.py:321
  63.0 3.9 %spread.8 = f32[1024,256]{1,0:T(8,128)S(1)} custom-call(bf16[3328,128]{1,0:T(8,128)(2,1)S(1)} %get-tuple-element.115.refs_0_, bf16[3328,128]{1,0:T(8,128)(2,1)S(1)} %get-tuple-element.116.refs_1_, bf16[1024,3328]{1,0:T(8,128)(2,1)S(1)} %get-tuple-element.117.refs_1_.counts_ref.refs_2_, bf16[3328,128]{1,0:T(8,128)(2,1)S(1)} %get-tuple-element.118.refs_0_.refs_3_, ...), custom_call_target="tpu_custom_call" | custom-call | tf_op jit(solution)/shard_map/spread/pallas_call | solution.py:282
  66.9 1.0 %collective-permute-done.15 = bf16[1024,128]{1,0:T(8,128)(2,1)S(1)} collective-permute-done((bf16[1024,128]{1,0:T(8,128)(2,1)S(1)}, bf16[1024,128]{1,0:T(8,128)(2,1)S(1)}, u32[]{:S(2)}, u32[]{:S(2)}) %collective-permute-start.15) | collective-permute-done | bytes 262176 | tf_op jit(solution)/shard_map/ppermute | solution.py:423
  67.9 0.1 fusion.2
  68.0 1.4 %collective-permute-start.17 = (bf16[1024,128]{1,0:T(8,128)(2,1)S(1)}, bf16[1024,128]{1,0:T(8,128)(2,1)S(1)}, u32[]{:S(2)}, u32[]{:S(2)}) collective-permute-start(bf16[1024,128]{1,0:T(8,128)(2,1)S(1)} %get-tuple-element.121), channel_id=1, source_target_pairs={{1,3},{3,5},{5,7},{7,6},{6,4},{4,2},{2,0},{0,1},{9,11},{11,13},{13... | collective-permute-start | bytes 786440 | tf_op jit(solution)/shard_map/ppermute | solution.py:423
  69.4 0.7 collective-permute-start.18
  70.1 1.3 %collective-permute-start.19 = (f32[2,27,128]{2,1,0:T(8,128)S(1)}, f32[2,27,128]{2,1,0:T(8,128)S(1)}, u32[]{:S(2)}, u32[]{:S(2)}) collective-permute-start(f32[2,27,128]{2,1,0:T(8,128)S(1)} %add.73), channel_id=1, source_target_pairs={{0,1},{1,0},{2,3},{3,2},{4,5},{5,4},{6,7},{7,6},{8,9},{9,8},{10,11... | collective-permute-start | bytes 82952 | tf_op jit(solution)/shard_map/ppermute | solution.py:321
  71.4 3.9 %spread.9 = f32[1024,256]{1,0:T(8,128)S(1)} custom-call(bf16[3328,128]{1,0:T(8,128)(2,1)S(1)} %get-tuple-element.115.refs_0_, bf16[3328,128]{1,0:T(8,128)(2,1)S(1)} %get-tuple-element.116.refs_1_, bf16[1024,3328]{1,0:T(8,128)(2,1)S(1)} %get-tuple-element.117.refs_1_.counts_ref.refs_2_, bf16[3328,128]{1,0:T(8,128)(2,1)S(1)} %get-tuple-element.118.refs_0_.refs_3_, ...), custom_call_target="tpu_custom_call" | custom-call | tf_op jit(solution)/shard_map/spread/pallas_call | solution.py:282
  75.4 0.8 collective-permute-done.19
  76.2 0.1 fusion
  76.3 0.8 collective-permute-start.20
  77.1 1.2 %collective-permute-start.21 = (bf16[1024,128]{1,0:T(8,128)(2,1)S(1)}, bf16[1024,128]{1,0:T(8,128)(2,1)S(1)}, u32[]{:S(2)}, u32[]{:S(2)}) collective-permute-start(bf16[1024,128]{1,0:T(8,128)(2,1)S(1)} %get-tuple-element.125), channel_id=1, source_target_pairs={{3,1},{5,3},{7,5},{6,7},{4,6},{2,4},{0,2},{1,0},{11,9},{13,11},{15... | collective-permute-start | bytes 786440 | tf_op jit(solution)/shard_map/ppermute | solution.py:423
  78.4 0.4 collective-permute-start.22
  78.8 4.3 %collective-permute-done.22 = f32[2,27,128]{2,1,0:T(8,128)S(1)} collective-permute-done((f32[2,27,128]{2,1,0:T(8,128)S(1)}, f32[2,27,128]{2,1,0:T(8,128)S(1)}, u32[]{:S(2)}, u32[]{:S(2)}) %collective-permute-start.22) | collective-permute-done | bytes 27680 | tf_op jit(solution)/shard_map/ppermute | solution.py:321
  83.1 0.4 collective-permute-done.21
  83.5 0.1 fusion.7
  83.6 1.6 %collective-permute-start.23 = (bf16[1024,128]{1,0:T(8,128)(2,1)S(1)}, bf16[1024,128]{1,0:T(8,128)(2,1)S(1)}, u32[]{:S(2)}, u32[]{:S(2)}) collective-permute-start(bf16[1024,128]{1,0:T(8,128)(2,1)S(1)} %fusion.7), channel_id=1, source_target_pairs={{0,16},{8,24},{16,0},{24,8},{1,17},{9,25},{17,1},{25,9},{2,18},{10... | collective-permute-start | bytes 786440 | tf_op jit(solution)/shard_map/ppermute | solution.py:321
  85.2 1.3 %collective-permute-start.24 = (f32[2,27,128]{2,1,0:T(8,128)S(1)}, f32[2,27,128]{2,1,0:T(8,128)S(1)}, u32[]{:S(2)}, u32[]{:S(2)}) collective-permute-start(f32[2,27,128]{2,1,0:T(8,128)S(1)} %add.79), channel_id=1, source_target_pairs={{0,4},{1,5},{2,6},{3,7},{4,0},{5,1},{6,2},{7,3},{8,12},{9,13},{10,... | collective-permute-start | bytes 82952 | tf_op jit(solution)/shard_map/ppermute | solution.py:321
  86.5 3.5 %collective-permute-done.24 = f32[2,27,128]{2,1,0:T(8,128)S(1)} collective-permute-done((f32[2,27,128]{2,1,0:T(8,128)S(1)}, f32[2,27,128]{2,1,0:T(8,128)S(1)}, u32[]{:S(2)}, u32[]{:S(2)}) %collective-permute-start.24) | collective-permute-done | bytes 27680 | tf_op jit(solution)/shard_map/ppermute | solution.py:321
  90.2 0.8 place_half.2.refs_0_
  91.0 0.6 slice_bitcast_fusion
  91.6 0.5 collective-permute-done.25.part_ref
  92.0 0.8 place_half.3
  (43 shorter events, 0.4 us)
Async XLA Ops:
  0.6 1.0 %copy-start = (bf16[2048,128]{1,0:T(8,128)(2,1)S(1)}, bf16[2048,128]{1,0:T(8,128)(2,1)}, u32[]{:S(2)}) copy-start(bf16[2048,128]{1,0:T(8,128)(2,1)} %param.11) | copy-start | bytes 1572868
  1.9 10.2 %collective-permute-start = (bf16[1024,128]{1,0:T(8,128)(2,1)S(1)}, bf16[1024,128]{1,0:T(8,128)(2,1)S(1)}, u32[]{:S(2)}, u32[]{:S(2)}) collective-permute-start(bf16[1024,128]{1,0:T(8,128)(2,1)S(1)} %bitcast.25), channel_id=1, source_target_pairs={{1,3},{3,5},{5,7},{7,6},{6,4},{4,2},{2,0},{0,1},{9,11},{11,13},{13... | collective-permute-start | bytes 786440 | tf_op jit(solution)/shard_map/ppermute | solution.py:371
  4.9 7.8 %collective-permute-start.1 = (bf16[1024,128]{1,0:T(8,128)(2,1)S(1)}, bf16[1024,128]{1,0:T(8,128)(2,1)S(1)}, u32[]{:S(2)}, u32[]{:S(2)}) collective-permute-start(bf16[1024,128]{1,0:T(8,128)(2,1)S(1)} %bitcast.26), channel_id=1, source_target_pairs={{3,1},{5,3},{7,5},{6,7},{4,6},{2,4},{0,2},{1,0},{11,9},{13,11},{15... | collective-permute-start | bytes 786440 | tf_op jit(solution)/shard_map/ppermute | solution.py:372
  6.7 5.4 %collective-permute-start.2 = (s32[26,8,128]{2,1,0:T(8,128)S(1)}, s32[26,8,128]{2,1,0:T(8,128)S(1)}, u32[]{:S(2)}, u32[]{:S(2)}) collective-permute-start(s32[26,8,128]{2,1,0:T(8,128)S(1)} %fusion.8.place_ref), channel_id=1, source_target_pairs={{0,8},{8,0},{16,24},{24,16},{1,9},{9,1},{17,25},{25,17},{2,10},{10... | collective-permute-start | bytes 319496 | tf_op jit(solution)/shard_map/ppermute | solution.py:321
  12.6 9.5 %collective-permute-start.3 = (bf16[1024,128]{1,0:T(8,128)(2,1)S(1)}, bf16[1024,128]{1,0:T(8,128)(2,1)S(1)}, u32[]{:S(2)}, u32[]{:S(2)}) collective-permute-start(bf16[1024,128]{1,0:T(8,128)(2,1)S(1)} %collective-permute-done.refs_4_.refs_2_), channel_id=1, source_target_pairs={{1,3},{3,5},{5,7},{7,6},{6,4},{4,2},{2,0},{0,1},{9,11},{11,13},{13... | collective-permute-start | bytes 786440 | tf_op jit(solution)/shard_map/ppermute | solution.py:371
  14.2 8.2 %collective-permute-start.4 = (bf16[1024,128]{1,0:T(8,128)(2,1)S(1)}, bf16[1024,128]{1,0:T(8,128)(2,1)S(1)}, u32[]{:S(2)}, u32[]{:S(2)}) collective-permute-start(bf16[1024,128]{1,0:T(8,128)(2,1)S(1)} %collective-permute-done.1.refs_3_.refs_1_), channel_id=1, source_target_pairs={{3,1},{5,3},{7,5},{6,7},{4,6},{2,4},{0,2},{1,0},{11,9},{13,11},{15... | collective-permute-start | bytes 786440 | tf_op jit(solution)/shard_map/ppermute | solution.py:372
  22.4 9.0 %collective-permute-start.5 = (bf16[1024,128]{1,0:T(8,128)(2,1)S(1)}, bf16[1024,128]{1,0:T(8,128)(2,1)S(1)}, u32[]{:S(2)}, u32[]{:S(2)}) collective-permute-start(bf16[1024,128]{1,0:T(8,128)(2,1)S(1)} %collective-permute-done.3.refs_1_), channel_id=1, source_target_pairs={{1,3},{3,5},{5,7},{7,6},{6,4},{4,2},{2,0},{0,1},{9,11},{11,13},{13... | collective-permute-start | bytes 786440 | tf_op jit(solution)/shard_map/ppermute | solution.py:371
  24.0 7.4 %collective-permute-start.6 = (bf16[1024,128]{1,0:T(8,128)(2,1)S(1)}, bf16[1024,128]{1,0:T(8,128)(2,1)S(1)}, u32[]{:S(2)}, u32[]{:S(2)}) collective-permute-start(bf16[1024,128]{1,0:T(8,128)(2,1)S(1)} %collective-permute-done.4.refs_0_), channel_id=1, source_target_pairs={{3,1},{5,3},{7,5},{6,7},{4,6},{2,4},{0,2},{1,0},{11,9},{13,11},{15... | collective-permute-start | bytes 786440 | tf_op jit(solution)/shard_map/ppermute | solution.py:372
  24.4 2.8 %copy-start.1 = (bf16[3456,512]{1,0:T(8,128)(2,1)S(1)}, bf16[3456,512]{1,0:T(8,128)(2,1)}, u32[]{:S(2)}) copy-start(bf16[3456,512]{1,0:T(8,128)(2,1)} %down_ref.1) | copy-start | bytes 10616836
  24.5 3.1 %copy-start.2 = (bf16[512,3456]{1,0:T(8,128)(2,1)S(1)}, bf16[512,3456]{1,0:T(8,128)(2,1)}, u32[]{:S(2)}) copy-start(bf16[512,3456]{1,0:T(8,128)(2,1)} %up_ref.1) | copy-start | bytes 10616836
  31.5 6.0 %collective-permute-start.7 = (bf16[512,128]{1,0:T(8,128)(2,1)S(1)}, bf16[512,128]{1,0:T(8,128)(2,1)S(1)}, u32[]{:S(2)}, u32[]{:S(2)}) collective-permute-start(bf16[512,128]{1,0:T(8,128)(2,1)S(1)} %slice.57), channel_id=1, source_target_pairs={{1,3},{3,5},{5,7},{7,6},{6,4},{4,2},{2,0},{0,1},{9,11},{11,13},{13... | collective-permute-start | bytes 393224 | tf_op jit(solution)/shard_map/ppermute | solution.py:389
  33.1 5.0 %collective-permute-start.8 = (bf16[512,128]{1,0:T(8,128)(2,1)S(1)}, bf16[512,128]{1,0:T(8,128)(2,1)S(1)}, u32[]{:S(2)}, u32[]{:S(2)}) collective-permute-start(bf16[512,128]{1,0:T(8,128)(2,1)S(1)} %slice.58), channel_id=1, source_target_pairs={{3,1},{5,3},{7,5},{6,7},{4,6},{2,4},{0,2},{1,0},{11,9},{13,11},{15... | collective-permute-start | bytes 393224 | tf_op jit(solution)/shard_map/ppermute | solution.py:389
  37.5 1.8 %copy-start.7 = (s32[128]{0:T(128)S(1)}, s32[128]{0:T(128)}, u32[]{:S(2)}) copy-start(s32[128]{0:T(128)} %param.16) | copy-start | bytes 1540
  39.1 3.7 %collective-permute-start.9 = (f32[128,3328]{1,0:T(8,128)S(1)}, f32[128,3328]{1,0:T(8,128)S(1)}, u32[]{:S(2)}, u32[]{:S(2)}) collective-permute-start(f32[128,3328]{1,0:T(8,128)S(1)} %pool.13), channel_id=1, source_target_pairs={{0,8},{8,0},{16,24},{24,16},{1,9},{9,1},{17,25},{25,17},{2,10},{10... | collective-permute-start | bytes 5111816 | tf_op jit(solution)/shard_map/ppermute | solution.py:321
  39.2 3.6 %copy-start.3 = (bf16[128,128]{1,0:T(8,128)(2,1)S(1)}, bf16[128,128]{1,0:T(8,128)(2,1)}, u32[]{:S(2)}) copy-start(bf16[128,128]{1,0:T(8,128)(2,1)} %dense_ref.1) | copy-start | bytes 98308
  39.2 3.6 %copy-start.4 = (f32[3456]{0:T(1024)S(1)}, f32[3456]{0:T(1024)}, u32[]{:S(2)}) copy-start(f32[3456]{0:T(1024)} %param.20) | copy-start | bytes 41476
  39.3 3.5 %copy-start.5 = (f32[3456]{0:T(1024)S(1)}, f32[3456]{0:T(1024)}, u32[]{:S(2)}) copy-start(f32[3456]{0:T(1024)} %param.21) | copy-start | bytes 41476
  39.3 3.5 %copy-start.6 = (f32[128]{0:T(128)S(1)}, f32[128]{0:T(128)}, u32[]{:S(2)}) copy-start(f32[128]{0:T(128)} %param.17) | copy-start | bytes 1540
  47.3 2.7 %collective-permute-start.10 = (bf16[3328,128]{1,0:T(8,128)(2,1)S(1)}, bf16[3328,128]{1,0:T(8,128)(2,1)S(1)}, u32[]{:S(2)}, u32[]{:S(2)}) collective-permute-start(bf16[3328,128]{1,0:T(8,128)(2,1)S(1)} %get-tuple-element.116.refs_1_), channel_id=1, source_target_pairs={{0,8},{8,0},{16,24},{24,16},{1,9},{9,1},{17,25},{25,17},{2,10},{10... | collective-permute-start | bytes 2555912 | tf_op jit(solution)/shard_map/ppermute | solution.py:321
  47.5 2.5 %collective-permute-start.11 = (f32[2,27,128]{2,1,0:T(8,128)S(1)}, f32[2,27,128]{2,1,0:T(8,128)S(1)}, u32[]{:S(2)}, u32[]{:S(2)}) collective-permute-start(f32[2,27,128]{2,1,0:T(8,128)S(1)} %get-tuple-element.97), channel_id=1, source_target_pairs={{0,8},{8,0},{16,24},{24,16},{1,9},{9,1},{17,25},{25,17},{2,10},{10... | collective-permute-start | bytes 82952 | tf_op jit(solution)/shard_map/ppermute | solution.py:321
  52.4 6.0 %collective-permute-start.12 = (bf16[512,128]{1,0:T(8,128)(2,1)S(1)}, bf16[512,128]{1,0:T(8,128)(2,1)S(1)}, u32[]{:S(2)}, u32[]{:S(2)}) collective-permute-start(bf16[512,128]{1,0:T(8,128)(2,1)S(1)} %get-tuple-element.139), channel_id=1, source_target_pairs={{1,3},{3,5},{5,7},{7,6},{6,4},{4,2},{2,0},{0,1},{9,11},{11,13},{13... | collective-permute-start | bytes 393224 | tf_op jit(solution)/shard_map/ppermute | solution.py:423
  54.0 5.3 %collective-permute-start.13 = (bf16[512,128]{1,0:T(8,128)(2,1)S(1)}, bf16[512,128]{1,0:T(8,128)(2,1)S(1)}, u32[]{:S(2)}, u32[]{:S(2)}) collective-permute-start(bf16[512,128]{1,0:T(8,128)(2,1)S(1)} %get-tuple-element.138), channel_id=1, source_target_pairs={{3,1},{5,3},{7,5},{6,7},{4,6},{2,4},{0,2},{1,0},{11,9},{13,11},{15... | collective-permute-start | bytes 393224 | tf_op jit(solution)/shard_map/ppermute | solution.py:423
  59.4 7.5 %collective-permute-start.14 = (bf16[1024,128]{1,0:T(8,128)(2,1)S(1)}, bf16[1024,128]{1,0:T(8,128)(2,1)S(1)}, u32[]{:S(2)}, u32[]{:S(2)}) collective-permute-start(bf16[1024,128]{1,0:T(8,128)(2,1)S(1)} %get-tuple-element.112), channel_id=1, source_target_pairs={{1,3},{3,5},{5,7},{7,6},{6,4},{4,2},{2,0},{0,1},{9,11},{11,13},{13... | collective-permute-start | bytes 786440 | tf_op jit(solution)/shard_map/ppermute | solution.py:423
  61.0 6.9 %collective-permute-start.15 = (bf16[1024,128]{1,0:T(8,128)(2,1)S(1)}, bf16[1024,128]{1,0:T(8,128)(2,1)S(1)}, u32[]{:S(2)}, u32[]{:S(2)}) collective-permute-start(bf16[1024,128]{1,0:T(8,128)(2,1)S(1)} %get-tuple-element.113), channel_id=1, source_target_pairs={{3,1},{5,3},{7,5},{6,7},{4,6},{2,4},{0,2},{1,0},{11,9},{13,11},{15... | collective-permute-start | bytes 786440 | tf_op jit(solution)/shard_map/ppermute | solution.py:423
  61.5 5.4 %collective-permute-start.16 = (f32[2,27,128]{2,1,0:T(8,128)S(1)}, f32[2,27,128]{2,1,0:T(8,128)S(1)}, u32[]{:S(2)}, u32[]{:S(2)}) collective-permute-start(f32[2,27,128]{2,1,0:T(8,128)S(1)} %add.68), channel_id=1, source_target_pairs={{0,16},{8,24},{16,0},{24,8},{1,17},{9,25},{17,1},{25,9},{2,18},{10... | collective-permute-start | bytes 82952 | tf_op jit(solution)/shard_map/ppermute | solution.py:321
  68.0 8.1 %collective-permute-start.17 = (bf16[1024,128]{1,0:T(8,128)(2,1)S(1)}, bf16[1024,128]{1,0:T(8,128)(2,1)S(1)}, u32[]{:S(2)}, u32[]{:S(2)}) collective-permute-start(bf16[1024,128]{1,0:T(8,128)(2,1)S(1)} %get-tuple-element.121), channel_id=1, source_target_pairs={{1,3},{3,5},{5,7},{7,6},{6,4},{4,2},{2,0},{0,1},{9,11},{11,13},{13... | collective-permute-start | bytes 786440 | tf_op jit(solution)/shard_map/ppermute | solution.py:423
  69.4 6.7 %collective-permute-start.18 = (bf16[1024,128]{1,0:T(8,128)(2,1)S(1)}, bf16[1024,128]{1,0:T(8,128)(2,1)S(1)}, u32[]{:S(2)}, u32[]{:S(2)}) collective-permute-start(bf16[1024,128]{1,0:T(8,128)(2,1)S(1)} %get-tuple-element.122), channel_id=1, source_target_pairs={{3,1},{5,3},{7,5},{6,7},{4,6},{2,4},{0,2},{1,0},{11,9},{13,11},{15... | collective-permute-start | bytes 786440 | tf_op jit(solution)/shard_map/ppermute | solution.py:423
  70.1 6.0 %collective-permute-start.19 = (f32[2,27,128]{2,1,0:T(8,128)S(1)}, f32[2,27,128]{2,1,0:T(8,128)S(1)}, u32[]{:S(2)}, u32[]{:S(2)}) collective-permute-start(f32[2,27,128]{2,1,0:T(8,128)S(1)} %add.73), channel_id=1, source_target_pairs={{0,1},{1,0},{2,3},{3,2},{4,5},{5,4},{6,7},{7,6},{8,9},{9,8},{10,11... | collective-permute-start | bytes 82952 | tf_op jit(solution)/shard_map/ppermute | solution.py:321
  76.3 6.8 %collective-permute-start.20 = (bf16[1024,128]{1,0:T(8,128)(2,1)S(1)}, bf16[1024,128]{1,0:T(8,128)(2,1)S(1)}, u32[]{:S(2)}, u32[]{:S(2)}) collective-permute-start(bf16[1024,128]{1,0:T(8,128)(2,1)S(1)} %get-tuple-element.124), channel_id=1, source_target_pairs={{1,3},{3,5},{5,7},{7,6},{6,4},{4,2},{2,0},{0,1},{9,11},{11,13},{13... | collective-permute-start | bytes 786440 | tf_op jit(solution)/shard_map/ppermute | solution.py:423
  77.1 6.4 %collective-permute-start.21 = (bf16[1024,128]{1,0:T(8,128)(2,1)S(1)}, bf16[1024,128]{1,0:T(8,128)(2,1)S(1)}, u32[]{:S(2)}, u32[]{:S(2)}) collective-permute-start(bf16[1024,128]{1,0:T(8,128)(2,1)S(1)} %get-tuple-element.125), channel_id=1, source_target_pairs={{3,1},{5,3},{7,5},{6,7},{4,6},{2,4},{0,2},{1,0},{11,9},{13,11},{15... | collective-permute-start | bytes 786440 | tf_op jit(solution)/shard_map/ppermute | solution.py:423
  78.4 4.7 %collective-permute-start.22 = (f32[2,27,128]{2,1,0:T(8,128)S(1)}, f32[2,27,128]{2,1,0:T(8,128)S(1)}, u32[]{:S(2)}, u32[]{:S(2)}) collective-permute-start(f32[2,27,128]{2,1,0:T(8,128)S(1)} %add.76), channel_id=1, source_target_pairs={{0,2},{1,3},{2,0},{3,1},{4,6},{5,7},{6,4},{7,5},{8,10},{9,11},{10,... | collective-permute-start | bytes 82952 | tf_op jit(solution)/shard_map/ppermute | solution.py:321
  83.6 6.4 %collective-permute-start.23 = (bf16[1024,128]{1,0:T(8,128)(2,1)S(1)}, bf16[1024,128]{1,0:T(8,128)(2,1)S(1)}, u32[]{:S(2)}, u32[]{:S(2)}) collective-permute-start(bf16[1024,128]{1,0:T(8,128)(2,1)S(1)} %fusion.7), channel_id=1, source_target_pairs={{0,16},{8,24},{16,0},{24,8},{1,17},{9,25},{17,1},{25,9},{2,18},{10... | collective-permute-start | bytes 786440 | tf_op jit(solution)/shard_map/ppermute | solution.py:321
  85.2 4.8 %collective-permute-start.24 = (f32[2,27,128]{2,1,0:T(8,128)S(1)}, f32[2,27,128]{2,1,0:T(8,128)S(1)}, u32[]{:S(2)}, u32[]{:S(2)}) collective-permute-start(f32[2,27,128]{2,1,0:T(8,128)S(1)} %add.79), channel_id=1, source_target_pairs={{0,4},{1,5},{2,6},{3,7},{4,0},{5,1},{6,2},{7,3},{8,12},{9,13},{10,... | collective-permute-start | bytes 82952 | tf_op jit(solution)/shard_map/ppermute | solution.py:321
  90.1 2.0 %collective-permute-start.25 = (f32[1024,128]{1,0:T(8,128)S(1)}, f32[1024,128]{1,0:T(8,128)S(1)}, u32[]{:S(2)}, u32[]{:S(2)}) collective-permute-start(f32[1024,128]{1,0:T(8,128)S(1)} %convert_add_fusion.part_ref), channel_id=1, source_target_pairs={{0,8},{8,0},{16,24},{24,16},{1,9},{9,1},{17,25},{25,17},{2,10},{10... | collective-permute-start | bytes 1572872 | tf_op jit(solution)/shard_map/ppermute | solution.py:321

commit v3 on v2

--- a/solution.py
+++ b/solution.py
@@ -143,14 +143,14 @@
         for table in range(tables):
             turn = turn_ref[start + table : start + table + 1, :]
             here = slice((start + table) * LANES, (start + table + 1) * LANES)
-            total = before[0][:, here] if before else 0.0
+            total = before[0][:, here] if before else jnp.zeros((LANES, LANES), F32)
             for i, one in enumerate(turns):
                 mine = product[i * LANES : (i + 1) * LANES, table * LANES : (table + 1) * LANES]
                 total = jnp.where(turn == one, mine, total)
-            sum_ref[:, here] = total
-
-
-def pool(turns, turn, counts, shards, before, ahead=()):
+            sum_ref[:, here] = total.astype(sum_ref.dtype)
+
+
+def pool(turns, turn, counts, shards, before, ahead=(), dtype=F32):
     rows, bags = counts.shape
     blocks = [block for shard in shards for block in shard]
     width = blocks[0].shape[1]
@@ -164,7 +164,7 @@
             tables if len(turns) <= 4 else tables // 2,
             0 if before is None else 1,
         ),
-        out_shape=jax.ShapeDtypeStruct((width, bags), F32),
+        out_shape=jax.ShapeDtypeStruct((width, bags), dtype),
         in_specs=[VMEM] * (2 + len(blocks) + len(extra)),
         out_specs=VMEM,
         compiler_params=params(),
@@ -178,6 +178,7 @@
     dense_ref,
     own_ref,
     other_ref,
+    far_ref,
     label_ref,
     weight_ref,
     down_ref,
@@ -199,7 +200,9 @@
     for table in range(tables):
         here = slice(table * LANES, (table + 1) * LANES)
         x0_ref[:, (table + 1) * LANES : (table + 2) * LANES] = (
-            (own_ref[:, here] + other_ref[:, here]).T.astype(BF16)
+            (own_ref[:, here] + (other_ref[:, here] + far_ref[:, here].astype(F32)))
+            .astype(BF16)
+            .T
         )
     low = jnp.dot(x0_ref[...], down_ref[...], preferred_element_type=F32).astype(BF16)
     logit = jnp.zeros((samples, LANES), F32)
@@ -235,7 +238,7 @@
             d_pooled_ref[place, :] = d_x0.astype(BF16)
 
 
-def cross_layer(dense, own, other, labels, weights, down_w, up_w, bias, head):
+def cross_layer(dense, own, other, far, labels, weights, down_w, up_w, bias, head):
     samples, width = dense.shape
     tables = own.shape[1] // samples
     cross = down_w.shape[0]
@@ -254,7 +257,7 @@
         compiler_params=params(),
         cost_estimate=cost(8 * 10**9, 12 * 10**6),
         name="cross_layer",
-    )(dense, own, other, labels, weights, down_w, up_w, bias, head)
+    )(dense, own, other, far, labels, weights, down_w, up_w, bias, head)
 
 
 def spread_kernel(turns, count, at, *refs):
@@ -361,7 +364,8 @@
             here = tuple(range(start, start + 8))
             for side in (1, 0):
                 add(side, here, [[table[one]] for one in here])
-        return sides, sums
+        sums[1] = swap(sums[1], "grp", 1)
+        return sides, sums + [jnp.zeros_like(sums[1], BF16)]
     right, left = ring_turns(owners)
     lefts, rights = [shard], [shard]
 
@@ -387,11 +391,13 @@
         (lefts[3][:middle], rights[3][middle:], sums[0], sums[1])
     )
     far = [lax.ppermute(a, "emb", right), lax.ppermute(b, "emb", left)]
+    other, sums[1] = swap(sums[1], "grp", 1), None
     for side in (1, 0):
         add(side, (3, 5), [[rights[3]], [lefts[3]]])
     sums[0], sums[1] = lax.optimization_barrier((sums[0], sums[1]))
-    for side in (1, 0):
-        add(side, (4,), [far])
+    lent = pool((4,), sides[1][1], sides[1][0], [far], sums[1], dtype=BF16)
+    sums[1:] = other, swap(lent, "grp", 1)
+    add(0, (4,), [far])
     return sides, sums
 
 
@@ -470,12 +476,12 @@
     live = jnp.arange(hot, dtype=jnp.int32)[None, :, None] < bag_lengths.T[:, None, :]
     place = bag_owner.transpose(1, 2, 0) * local_rows + bag_rows.transpose(1, 2, 0)
     place = jnp.where(live, place, -1)
-    sides, (own, lent) = count_and_pool(where, place, shard, local_rows, (down_w, up_w))
-    other = swap(lent, "grp", 1)
+    sides, (own, other, far) = count_and_pool(where, place, shard, local_rows, (down_w, up_w))
     d_pooled, dense_grad, grads = cross_layer(
         dense_part,
         own,
         other,
+        far,
         labels.astype(F32).reshape(1, samples),
         sample_weight.reshape(1, samples),
         down_w,

time: 93.3 us -> 93.4 us (level)
  waiting for transfers between devices: 15.3 us -> 11.2 us
  starting transfers between devices: 24.5 us -> 28.1 us
    ppermute x10 -> x11, starting transfers between devices: 6.96 us -> 10.2 us  [swap(): return lax.ppermute(value, axis, [(i, i ^ stride) for i in range(size)])]
    ppermute x10 -> x11, waiting for transfers between devices: 11.5 us -> 8.26 us  [swap(): return lax.ppermute(value, axis, [(i, i ^ stride) for i in range(size)])]
    ppermute x4, starting transfers between devices: 2.85 us -> 4.87 us  [send(): lax.ppermute(to_left, 'emb', left)]
    ppermute x4, waiting for transfers between devices: 2.31 us -> 0.34 us  [send(): lax.ppermute(to_left, 'emb', left)]
    ppermute x4, starting transfers between devices: 5.46 us -> 3.66 us  [send(): lax.ppermute(to_right, 'emb', right)]
  transfers between devices with their start and end apart: 26 -> 27, of which waited for: 11 -> 10; matrix products, arithmetic and copies ran while one was open for 3% -> 3% of each run, Pallas kernels for 42% -> 43%
where the time goes in v3:
time: 93.4 us; the launch traced here: 93.2 us
  Pallas kernels  47.4 us (51%)
  starting transfers between devices  28.1 us (30%)
  waiting for transfers between devices  11.2 us (12%)
  local copies, waits for them, and re-layouts  3.08 us (3%)
  other arithmetic  2.21 us (2%)
  between operations  1.31 us (1%)
    pallas_call x5, Pallas kernels, spread(): pl.pallas_call(functools.partial(spread_kernel, turns, len(sides), at), o...  16 us
    pallas_call x7, Pallas kernels, pool(): pl.pallas_call(functools.partial(pool_kernel, [len(shard) for shard in sh...  12.7 us
    pallas_call x2, Pallas kernels, bag_counts(): pl.pallas_call(functools.partial(count_kernel, owners, local_rows, turns)...  12.6 us
    ppermute x11, starting transfers between devices, swap(): return lax.ppermute(value, axis, [(i, i ^ stride) for i in range(size)])  10.2 us
    ppermute x11, waiting for transfers between devices, swap(): return lax.ppermute(value, axis, [(i, i ^ stride) for i in range(size)])  8.26 us
    ppermute x3, starting transfers between devices, step(): lefts.append(lax.ppermute(a, 'emb', right))  6.14 us
    ppermute x4, starting transfers between devices, send(): lax.ppermute(to_left, 'emb', left)  4.87 us
    pallas_call x1, Pallas kernels, cross_layer(): pl.pallas_call(functools.partial(cross_kernel, tables), out_shape=(jax.Sh...  4.46 us
  transfers between devices with their start and end apart: 27, of which 10 were waited for; matrix products, arithmetic and copies ran while one was open for 3% of the time, Pallas kernels for 43%

profile of v3, /device:TPU:0, one launch (start us, length us, event | category | flops | bytes accessed | tf_op | source)
XLA Modules:
  0.0 93.2 jit_solution(7078645898437907584)
XLA Ops:
  0.7 1.0 %copy-done = bf16[2048,128]{1,0:T(8,128)(2,1)S(1)} copy-done((bf16[2048,128]{1,0:T(8,128)(2,1)S(1)}, bf16[2048,128]{1,0:T(8,128)(2,1)}, u32[]{:S(2)}) %copy-start) | copy-done | bytes 524312
  1.7 0.2 copy.16
  1.9 3.0 %collective-permute-start = (bf16[1024,128]{1,0:T(8,128)(2,1)S(1)}, bf16[1024,128]{1,0:T(8,128)(2,1)S(1)}, u32[]{:S(2)}, u32[]{:S(2)}) collective-permute-start(bf16[1024,128]{1,0:T(8,128)(2,1)S(1)} %bitcast.25), channel_id=1, source_target_pairs={{1,3},{3,5},{5,7},{7,6},{6,4},{4,2},{2,0},{0,1},{9,11},{11,13},{13... | collective-permute-start | bytes 786440 | tf_op jit(solution)/shard_map/ppermute | solution.py:375
  4.9 0.2 collective-permute-start.1
  5.0 0.7 multiply_bitcast_fusion
  5.8 0.9 fusion.8.place_ref
  6.7 0.1 collective-permute-start.2
  6.8 0.1 pad_add_fusion.where_ref
  6.8 5.2 %bag_counts.2 = (bf16[1024,3328]{1,0:T(8,128)(2,1)S(1)}, f32[26,128]{1,0:T(8,128)S(1)}, bf16[3328,128]{1,0:T(8,128)(2,1)S(1)}) custom-call(s32[2]{0:T(128)S(1)} %pad_add_fusion.where_ref, s32[26,8,128]{2,1,0:T(8,128)S(1)} %fusion.8.place_ref), custom_call_target="tpu_custom_call" | custom-call | flops 5000000000 | tf_op jit(solution)/shard_map/bag_counts/pallas_call | solution.py:120
  12.1 0.6 collective-permute-done.1.refs_3_.refs_1_
  12.6 1.6 %collective-permute-start.3 = (bf16[1024,128]{1,0:T(8,128)(2,1)S(1)}, bf16[1024,128]{1,0:T(8,128)(2,1)S(1)}, u32[]{:S(2)}, u32[]{:S(2)}) collective-permute-start(bf16[1024,128]{1,0:T(8,128)(2,1)S(1)} %collective-permute-done.refs_4_.refs_2_), channel_id=1, source_target_pairs={{1,3},{3,5},{5,7},{7,6},{6,4},{4,2},{2,0},{0,1},{9,11},{11,13},{13... | collective-permute-start | bytes 786440 | tf_op jit(solution)/shard_map/ppermute | solution.py:375
  14.2 0.4 collective-permute-start.4
  14.7 7.5 %bag_counts.3 = (bf16[1024,3328]{1,0:T(8,128)(2,1)S(1)}, f32[26,128]{1,0:T(8,128)S(1)}, bf16[3328,128]{1,0:T(8,128)(2,1)S(1)}, f32[128,3328]{1,0:T(8,128)S(1)}) custom-call(s32[2]{0:T(128)S(1)} %pad_add_fusion.where_ref, s32[26,8,128]{2,1,0:T(8,128)S(1)} %collective-permute-done.2.place_ref, f32[26,128]{1,0:T(8,128)S(1)} %get-tuple-element.82.refs_0_.turn_ref, ...), custom_call_target="tpu_custom_call" | custom-call | flops 5000000000 | tf_op jit(solution)/shard_map/bag_counts/pallas_call | solution.py:120
  22.1 0.3 collective-permute-done.4.refs_0_
  22.4 1.6 %collective-permute-start.5 = (bf16[1024,128]{1,0:T(8,128)(2,1)S(1)}, bf16[1024,128]{1,0:T(8,128)(2,1)S(1)}, u32[]{:S(2)}, u32[]{:S(2)}) collective-permute-start(bf16[1024,128]{1,0:T(8,128)(2,1)S(1)} %collective-permute-done.3.refs_1_), channel_id=1, source_target_pairs={{1,3},{3,5},{5,7},{7,6},{6,4},{4,2},{2,0},{0,1},{9,11},{11,13},{13... | collective-permute-start | bytes 786440 | tf_op jit(solution)/shard_map/ppermute | solution.py:375
  24.0 0.4 collective-permute-start.6
  24.4 2.8 %pool.8.refs_2_ = f32[128,3328]{1,0:T(8,128)S(1)} custom-call(f32[26,128]{1,0:T(8,128)S(1)} %get-tuple-element.87.turn_ref, bf16[1024,3328]{1,0:T(8,128)(2,1)S(1)} %get-tuple-element.120.counts_ref.refs_2_.refs_5_, bf16[1024,128]{1,0:T(8,128)(2,1)S(1)} %bitcast.28, bf16[1024,128]{1,0:T(8,128)(2,1)S(1)} %collective-permute-done.1.refs_3_.refs_1_, ...), custom_call_target="tpu_custom_call" | custom-call | tf_op jit(solution)/shard_map/pool/pallas_call | solution.py:159
  27.3 1.9 %pool.7.refs_2_ = f32[128,3328]{1,0:T(8,128)S(1)} custom-call(f32[26,128]{1,0:T(8,128)S(1)} %get-tuple-element.82.refs_0_.turn_ref, bf16[1024,3328]{1,0:T(8,128)(2,1)S(1)} %get-tuple-element.117.refs_1_.counts_ref.refs_2_, bf16[1024,128]{1,0:T(8,128)(2,1)S(1)} %collective-permute-done.4.refs_0_, bf16[1024,128]{1,0:T(8,128)(2,1)S(1)} %collective-permute-done.3.refs_1_, ...), custom_call_target="tpu_custom_call" | custom-call | tf_op jit(solution)/shard_map/pool/pallas_call | solution.py:159
  29.3 1.1 %copy-done.2 = bf16[512,3456]{1,0:T(8,128)(2,1)S(1)} copy-done((bf16[512,3456]{1,0:T(8,128)(2,1)S(1)}, bf16[512,3456]{1,0:T(8,128)(2,1)}, u32[]{:S(2)}) %copy-start.2) | copy-done | bytes 3538968
  30.4 1.9 %pool.9 = f32[128,3328]{1,0:T(8,128)S(1)} custom-call(f32[26,128]{1,0:T(8,128)S(1)} %get-tuple-element.87.turn_ref, bf16[1024,3328]{1,0:T(8,128)(2,1)S(1)} %get-tuple-element.120.counts_ref.refs_2_.refs_5_, bf16[1024,128]{1,0:T(8,128)(2,1)S(1)} %collective-permute-done.4.refs_0_, bf16[1024,128]{1,0:T(8,128)(2,1)S(1)} %collective-permute-done.3.refs_1_, ...), custom_call_target="tpu_custom_call" | custom-call | tf_op jit(solution)/shard_map/pool/pallas_call | solution.py:159
  32.4 1.6 %collective-permute-start.7 = (bf16[512,128]{1,0:T(8,128)(2,1)S(1)}, bf16[512,128]{1,0:T(8,128)(2,1)S(1)}, u32[]{:S(2)}, u32[]{:S(2)}) collective-permute-start(bf16[512,128]{1,0:T(8,128)(2,1)S(1)} %slice.57), channel_id=1, source_target_pairs={{1,3},{3,5},{5,7},{7,6},{6,4},{4,2},{2,0},{0,1},{9,11},{11,13},{13... | collective-permute-start | bytes 393224 | tf_op jit(solution)/shard_map/ppermute | solution.py:393
  34.1 0.4 collective-permute-start.8
  34.5 1.9 %pool.11.refs_2_ = f32[128,3328]{1,0:T(8,128)S(1)} custom-call(f32[26,128]{1,0:T(8,128)S(1)} %get-tuple-element.87.turn_ref, bf16[1024,3328]{1,0:T(8,128)(2,1)S(1)} %get-tuple-element.120.counts_ref.refs_2_.refs_5_, bf16[1024,128]{1,0:T(8,128)(2,1)S(1)} %collective-permute-done.6.refs_0_, bf16[1024,128]{1,0:T(8,128)(2,1)S(1)} %collective-permute-done.5.refs_1_), custom_call_target="tpu_custom_call" | custom-call | tf_op jit(solution)/shard_map/pool/pallas_call | solution.py:159
  36.4 1.9 %pool.10.refs_2_ = f32[128,3328]{1,0:T(8,128)S(1)} custom-call(f32[26,128]{1,0:T(8,128)S(1)} %get-tuple-element.82.refs_0_.turn_ref, bf16[1024,3328]{1,0:T(8,128)(2,1)S(1)} %get-tuple-element.117.refs_1_.counts_ref.refs_2_, bf16[1024,128]{1,0:T(8,128)(2,1)S(1)} %collective-permute-done.6.refs_0_, bf16[1024,128]{1,0:T(8,128)(2,1)S(1)} %collective-permute-done.5.refs_1_, ...), custom_call_target="tpu_custom_call" | custom-call | tf_op jit(solution)/shard_map/pool/pallas_call | solution.py:159
  38.4 1.2 %collective-permute-done.8.refs_1_ = bf16[512,128]{1,0:T(8,128)(2,1)S(1)} collective-permute-done((bf16[512,128]{1,0:T(8,128)(2,1)S(1)}, bf16[512,128]{1,0:T(8,128)(2,1)S(1)}, u32[]{:S(2)}, u32[]{:S(2)}) %collective-permute-start.8) | collective-permute-done | bytes 131104 | tf_op jit(solution)/shard_map/ppermute | solution.py:393
  39.6 1.1 %pool.13 = bf16[128,3328]{1,0:T(8,128)(2,1)S(1)} custom-call(f32[26,128]{1,0:T(8,128)S(1)} %get-tuple-element.87.turn_ref, bf16[1024,3328]{1,0:T(8,128)(2,1)S(1)} %get-tuple-element.120.counts_ref.refs_2_.refs_5_, bf16[512,128]{1,0:T(8,128)(2,1)S(1)} %collective-permute-done.7.refs_0_, bf16[512,128]{1,0:T(8,128)(2,1)S(1)} %collective-permute-done.8.refs_1_, ...), custom_call_target="tpu_custom_call" | custom-call | tf_op jit(solution)/shard_map/pool/pallas_call | solution.py:159
  40.7 0.1 collective-permute-start.10
  40.9 1.1 %pool.12.own_ref = f32[128,3328]{1,0:T(8,128)S(1)} custom-call(f32[26,128]{1,0:T(8,128)S(1)} %get-tuple-element.82.refs_0_.turn_ref, bf16[1024,3328]{1,0:T(8,128)(2,1)S(1)} %get-tuple-element.117.refs_1_.counts_ref.refs_2_, bf16[512,128]{1,0:T(8,128)(2,1)S(1)} %collective-permute-done.7.refs_0_, bf16[512,128]{1,0:T(8,128)(2,1)S(1)} %collective-permute-done.8.refs_1_, ...), custom_call_target="tpu_custom_call" | custom-call | tf_op jit(solution)/shard_map/pool/pallas_call | solution.py:159
  42.0 1.2 %collective-permute-done.10.far_ref = bf16[128,3328]{1,0:T(8,128)(2,1)S(1)} collective-permute-done((bf16[128,3328]{1,0:T(8,128)(2,1)S(1)}, bf16[128,3328]{1,0:T(8,128)(2,1)S(1)}, u32[]{:S(2)}, u32[]{:S(2)}) %collective-permute-start.10) | collective-permute-done | bytes 852000 | tf_op jit(solution)/shard_map/ppermute | solution.py:324
  43.2 4.5 %cross_layer.1 = (bf16[3328,128]{1,0:T(8,128)(2,1)S(1)}, bf16[128,128]{1,0:T(8,128)(2,1)}, f32[2,27,128]{2,1,0:T(8,128)S(1)}) custom-call(bf16[128,128]{1,0:T(8,128)(2,1)S(1)} %copy-done.3, f32[128,3328]{1,0:T(8,128)S(1)} %pool.12.own_ref, f32[128,3328]{1,0:T(8,128)S(1)} %collective-permute-done.9.other_ref, ...), custom_call_target="tpu_custom_call" | custom-call | flops 8000000000 | bytes 12000000 | tf_op jit(solution)/shard_map/cross_layer/pallas_call | solution.py:245
  47.7 0.2 collective-permute-start.11
  47.9 0.4 collective-permute-start.12
  48.2 2.1 %spread.5.refs_3_ = f32[1024,256]{1,0:T(8,128)S(1)} custom-call(bf16[3328,128]{1,0:T(8,128)(2,1)S(1)} %get-tuple-element.115.refs_0_, bf16[3328,128]{1,0:T(8,128)(2,1)S(1)} %get-tuple-element.116.refs_1_, bf16[1024,3328]{1,0:T(8,128)(2,1)S(1)} %get-tuple-element.117.refs_1_.counts_ref.refs_2_), custom_call_target="tpu_custom_call" | custom-call | tf_op jit(solution)/shard_map/spread/pallas_call | solution.py:285
  50.4 2.1 %spread.6 = f32[1024,256]{1,0:T(8,128)S(1)} custom-call(bf16[3328,128]{1,0:T(8,128)(2,1)S(1)} %get-tuple-element.118.refs_0_.refs_3_, bf16[3328,128]{1,0:T(8,128)(2,1)S(1)} %collective-permute-done.11.refs_1_.refs_4_, bf16[1024,3328]{1,0:T(8,128)(2,1)S(1)} %get-tuple-element.120.counts_ref.refs_2_.refs_5_, f32[1024,256]{1,0:T(8,128)S(1)} %spread.5.refs_3_), custom_call_target="tpu_custom_call" | custom-call | tf_op jit(solution)/shard_map/spread/pallas_call | solution.py:285
  52.6 0.7 collective-permute-start.14
  53.3 1.6 %collective-permute-start.13 = (bf16[512,128]{1,0:T(8,128)(2,1)S(1)}, bf16[512,128]{1,0:T(8,128)(2,1)S(1)}, u32[]{:S(2)}, u32[]{:S(2)}) collective-permute-start(bf16[512,128]{1,0:T(8,128)(2,1)S(1)} %get-tuple-element.139), channel_id=1, source_target_pairs={{1,3},{3,5},{5,7},{7,6},{6,4},{4,2},{2,0},{0,1},{9,11},{11,13},{13... | collective-permute-start | bytes 393224 | tf_op jit(solution)/shard_map/ppermute | solution.py:429
  54.9 3.9 %spread.7 = f32[1024,256]{1,0:T(8,128)S(1)} custom-call(bf16[3328,128]{1,0:T(8,128)(2,1)S(1)} %get-tuple-element.115.refs_0_, bf16[3328,128]{1,0:T(8,128)(2,1)S(1)} %get-tuple-element.116.refs_1_, bf16[1024,3328]{1,0:T(8,128)(2,1)S(1)} %get-tuple-element.117.refs_1_.counts_ref.refs_2_, bf16[3328,128]{1,0:T(8,128)(2,1)S(1)} %get-tuple-element.118.refs_0_.refs_3_, ...), custom_call_target="tpu_custom_call" | custom-call | tf_op jit(solution)/shard_map/spread/pallas_call | solution.py:285
  58.9 0.1 fusion.4
  58.9 1.0 %collective-permute-start.16 = (bf16[1024,128]{1,0:T(8,128)(2,1)S(1)}, bf16[1024,128]{1,0:T(8,128)(2,1)S(1)}, u32[]{:S(2)}, u32[]{:S(2)}) collective-permute-start(bf16[1024,128]{1,0:T(8,128)(2,1)S(1)} %get-tuple-element.113), channel_id=1, source_target_pairs={{3,1},{5,3},{7,5},{6,7},{4,6},{2,4},{0,2},{1,0},{11,9},{13,11},{15... | collective-permute-start | bytes 786440 | tf_op jit(solution)/shard_map/ppermute | solution.py:429
  60.0 1.1 %collective-permute-start.15 = (bf16[1024,128]{1,0:T(8,128)(2,1)S(1)}, bf16[1024,128]{1,0:T(8,128)(2,1)S(1)}, u32[]{:S(2)}, u32[]{:S(2)}) collective-permute-start(bf16[1024,128]{1,0:T(8,128)(2,1)S(1)} %get-tuple-element.112), channel_id=1, source_target_pairs={{1,3},{3,5},{5,7},{7,6},{6,4},{4,2},{2,0},{0,1},{9,11},{11,13},{13... | collective-permute-start | bytes 786440 | tf_op jit(solution)/shard_map/ppermute | solution.py:429
  61.0 1.5 %collective-permute-start.17 = (f32[2,27,128]{2,1,0:T(8,128)S(1)}, f32[2,27,128]{2,1,0:T(8,128)S(1)}, u32[]{:S(2)}, u32[]{:S(2)}) collective-permute-start(f32[2,27,128]{2,1,0:T(8,128)S(1)} %add.68), channel_id=1, source_target_pairs={{0,16},{8,24},{16,0},{24,8},{1,17},{9,25},{17,1},{25,9},{2,18},{10... | collective-permute-start | bytes 82952 | tf_op jit(solution)/shard_map/ppermute | solution.py:324
  62.6 3.9 %spread.8 = f32[1024,256]{1,0:T(8,128)S(1)} custom-call(bf16[3328,128]{1,0:T(8,128)(2,1)S(1)} %get-tuple-element.115.refs_0_, bf16[3328,128]{1,0:T(8,128)(2,1)S(1)} %get-tuple-element.116.refs_1_, bf16[1024,3328]{1,0:T(8,128)(2,1)S(1)} %get-tuple-element.117.refs_1_.counts_ref.refs_2_, bf16[3328,128]{1,0:T(8,128)(2,1)S(1)} %get-tuple-element.118.refs_0_.refs_3_, ...), custom_call_target="tpu_custom_call" | custom-call | tf_op jit(solution)/shard_map/spread/pallas_call | solution.py:285
  66.4 0.3 collective-permute-done.16
  66.8 0.2 collective-permute-done.15
  67.0 0.1 fusion.2
  67.1 1.5 %collective-permute-start.19 = (bf16[1024,128]{1,0:T(8,128)(2,1)S(1)}, bf16[1024,128]{1,0:T(8,128)(2,1)S(1)}, u32[]{:S(2)}, u32[]{:S(2)}) collective-permute-start(bf16[1024,128]{1,0:T(8,128)(2,1)S(1)} %get-tuple-element.122), channel_id=1, source_target_pairs={{3,1},{5,3},{7,5},{6,7},{4,6},{2,4},{0,2},{1,0},{11,9},{13,11},{15... | collective-permute-start | bytes 786440 | tf_op jit(solution)/shard_map/ppermute | solution.py:429
  68.6 0.5 collective-permute-start.18
  69.1 1.6 %collective-permute-start.20 = (f32[2,27,128]{2,1,0:T(8,128)S(1)}, f32[2,27,128]{2,1,0:T(8,128)S(1)}, u32[]{:S(2)}, u32[]{:S(2)}) collective-permute-start(f32[2,27,128]{2,1,0:T(8,128)S(1)} %add.73), channel_id=1, source_target_pairs={{0,1},{1,0},{2,3},{3,2},{4,5},{5,4},{6,7},{7,6},{8,9},{9,8},{10,11... | collective-permute-start | bytes 82952 | tf_op jit(solution)/shard_map/ppermute | solution.py:324
  70.7 3.9 %spread.9 = f32[1024,256]{1,0:T(8,128)S(1)} custom-call(bf16[3328,128]{1,0:T(8,128)(2,1)S(1)} %get-tuple-element.115.refs_0_, bf16[3328,128]{1,0:T(8,128)(2,1)S(1)} %get-tuple-element.116.refs_1_, bf16[1024,3328]{1,0:T(8,128)(2,1)S(1)} %get-tuple-element.117.refs_1_.counts_ref.refs_2_, bf16[3328,128]{1,0:T(8,128)(2,1)S(1)} %get-tuple-element.118.refs_0_.refs_3_, ...), custom_call_target="tpu_custom_call" | custom-call | tf_op jit(solution)/shard_map/spread/pallas_call | solution.py:285
  74.7 0.3 collective-permute-done.18
  75.0 0.1 fusion
  75.1 1.6 %collective-permute-start.22 = (bf16[1024,128]{1,0:T(8,128)(2,1)S(1)}, bf16[1024,128]{1,0:T(8,128)(2,1)S(1)}, u32[]{:S(2)}, u32[]{:S(2)}) collective-permute-start(bf16[1024,128]{1,0:T(8,128)(2,1)S(1)} %get-tuple-element.125), channel_id=1, source_target_pairs={{3,1},{5,3},{7,5},{6,7},{4,6},{2,4},{0,2},{1,0},{11,9},{13,11},{15... | collective-permute-start | bytes 786440 | tf_op jit(solution)/shard_map/ppermute | solution.py:429
  76.7 0.5 collective-permute-start.21
  77.2 1.6 %collective-permute-start.23 = (f32[2,27,128]{2,1,0:T(8,128)S(1)}, f32[2,27,128]{2,1,0:T(8,128)S(1)}, u32[]{:S(2)}, u32[]{:S(2)}) collective-permute-start(f32[2,27,128]{2,1,0:T(8,128)S(1)} %add.76), channel_id=1, source_target_pairs={{0,2},{1,3},{2,0},{3,1},{4,6},{5,7},{6,4},{7,5},{8,10},{9,11},{10,... | collective-permute-start | bytes 82952 | tf_op jit(solution)/shard_map/ppermute | solution.py:324
  78.7 4.7 %collective-permute-done.23 = f32[2,27,128]{2,1,0:T(8,128)S(1)} collective-permute-done((f32[2,27,128]{2,1,0:T(8,128)S(1)}, f32[2,27,128]{2,1,0:T(8,128)S(1)}, u32[]{:S(2)}, u32[]{:S(2)}) %collective-permute-start.23) | collective-permute-done | bytes 27680 | tf_op jit(solution)/shard_map/ppermute | solution.py:324
  83.4 0.1 fusion.7
  83.5 1.6 %collective-permute-start.24 = (bf16[1024,128]{1,0:T(8,128)(2,1)S(1)}, bf16[1024,128]{1,0:T(8,128)(2,1)S(1)}, u32[]{:S(2)}, u32[]{:S(2)}) collective-permute-start(bf16[1024,128]{1,0:T(8,128)(2,1)S(1)} %fusion.7), channel_id=1, source_target_pairs={{0,16},{8,24},{16,0},{24,8},{1,17},{9,25},{17,1},{25,9},{2,18},{10... | collective-permute-start | bytes 786440 | tf_op jit(solution)/shard_map/ppermute | solution.py:324
  85.1 3.1 %collective-permute-start.25 = (f32[2,27,128]{2,1,0:T(8,128)S(1)}, f32[2,27,128]{2,1,0:T(8,128)S(1)}, u32[]{:S(2)}, u32[]{:S(2)}) collective-permute-start(f32[2,27,128]{2,1,0:T(8,128)S(1)} %add.79), channel_id=1, source_target_pairs={{0,4},{1,5},{2,6},{3,7},{4,0},{5,1},{6,2},{7,3},{8,12},{9,13},{10,... | collective-permute-start | bytes 82952 | tf_op jit(solution)/shard_map/ppermute | solution.py:324
  88.3 1.9 %collective-permute-done.25 = f32[2,27,128]{2,1,0:T(8,128)S(1)} collective-permute-done((f32[2,27,128]{2,1,0:T(8,128)S(1)}, f32[2,27,128]{2,1,0:T(8,128)S(1)}, u32[]{:S(2)}, u32[]{:S(2)}) %collective-permute-start.25) | collective-permute-done | bytes 27680 | tf_op jit(solution)/shard_map/ppermute | solution.py:324
  90.2 0.1 collective-permute-start.26
  90.3 0.8 place_half.2.refs_0_
  91.1 0.6 slice_bitcast_fusion
  91.7 0.5 collective-permute-done.26.part_ref
  92.2 0.8 place_half.3
  (45 shorter events, 0.4 us)
Async XLA Ops:
  0.6 1.0 %copy-start = (bf16[2048,128]{1,0:T(8,128)(2,1)S(1)}, bf16[2048,128]{1,0:T(8,128)(2,1)}, u32[]{:S(2)}) copy-start(bf16[2048,128]{1,0:T(8,128)(2,1)} %param.11) | copy-start | bytes 1572868
  1.9 10.2 %collective-permute-start = (bf16[1024,128]{1,0:T(8,128)(2,1)S(1)}, bf16[1024,128]{1,0:T(8,128)(2,1)S(1)}, u32[]{:S(2)}, u32[]{:S(2)}) collective-permute-start(bf16[1024,128]{1,0:T(8,128)(2,1)S(1)} %bitcast.25), channel_id=1, source_target_pairs={{1,3},{3,5},{5,7},{7,6},{6,4},{4,2},{2,0},{0,1},{9,11},{11,13},{13... | collective-permute-start | bytes 786440 | tf_op jit(solution)/shard_map/ppermute | solution.py:375
  4.9 7.8 %collective-permute-start.1 = (bf16[1024,128]{1,0:T(8,128)(2,1)S(1)}, bf16[1024,128]{1,0:T(8,128)(2,1)S(1)}, u32[]{:S(2)}, u32[]{:S(2)}) collective-permute-start(bf16[1024,128]{1,0:T(8,128)(2,1)S(1)} %bitcast.26), channel_id=1, source_target_pairs={{3,1},{5,3},{7,5},{6,7},{4,6},{2,4},{0,2},{1,0},{11,9},{13,11},{15... | collective-permute-start | bytes 786440 | tf_op jit(solution)/shard_map/ppermute | solution.py:376
  6.7 5.4 %collective-permute-start.2 = (s32[26,8,128]{2,1,0:T(8,128)S(1)}, s32[26,8,128]{2,1,0:T(8,128)S(1)}, u32[]{:S(2)}, u32[]{:S(2)}) collective-permute-start(s32[26,8,128]{2,1,0:T(8,128)S(1)} %fusion.8.place_ref), channel_id=1, source_target_pairs={{0,8},{8,0},{16,24},{24,16},{1,9},{9,1},{17,25},{25,17},{2,10},{10... | collective-permute-start | bytes 319496 | tf_op jit(solution)/shard_map/ppermute | solution.py:324
  12.6 9.5 %collective-permute-start.3 = (bf16[1024,128]{1,0:T(8,128)(2,1)S(1)}, bf16[1024,128]{1,0:T(8,128)(2,1)S(1)}, u32[]{:S(2)}, u32[]{:S(2)}) collective-permute-start(bf16[1024,128]{1,0:T(8,128)(2,1)S(1)} %collective-permute-done.refs_4_.refs_2_), channel_id=1, source_target_pairs={{1,3},{3,5},{5,7},{7,6},{6,4},{4,2},{2,0},{0,1},{9,11},{11,13},{13... | collective-permute-start | bytes 786440 | tf_op jit(solution)/shard_map/ppermute | solution.py:375
  14.2 8.2 %collective-permute-start.4 = (bf16[1024,128]{1,0:T(8,128)(2,1)S(1)}, bf16[1024,128]{1,0:T(8,128)(2,1)S(1)}, u32[]{:S(2)}, u32[]{:S(2)}) collective-permute-start(bf16[1024,128]{1,0:T(8,128)(2,1)S(1)} %collective-permute-done.1.refs_3_.refs_1_), channel_id=1, source_target_pairs={{3,1},{5,3},{7,5},{6,7},{4,6},{2,4},{0,2},{1,0},{11,9},{13,11},{15... | collective-permute-start | bytes 786440 | tf_op jit(solution)/shard_map/ppermute | solution.py:376
  22.4 9.9 %collective-permute-start.5 = (bf16[1024,128]{1,0:T(8,128)(2,1)S(1)}, bf16[1024,128]{1,0:T(8,128)(2,1)S(1)}, u32[]{:S(2)}, u32[]{:S(2)}) collective-permute-start(bf16[1024,128]{1,0:T(8,128)(2,1)S(1)} %collective-permute-done.3.refs_1_), channel_id=1, source_target_pairs={{1,3},{3,5},{5,7},{7,6},{6,4},{4,2},{2,0},{0,1},{9,11},{11,13},{13... | collective-permute-start | bytes 786440 | tf_op jit(solution)/shard_map/ppermute | solution.py:375
  24.0 8.3 %collective-permute-start.6 = (bf16[1024,128]{1,0:T(8,128)(2,1)S(1)}, bf16[1024,128]{1,0:T(8,128)(2,1)S(1)}, u32[]{:S(2)}, u32[]{:S(2)}) collective-permute-start(bf16[1024,128]{1,0:T(8,128)(2,1)S(1)} %collective-permute-done.4.refs_0_), channel_id=1, source_target_pairs={{3,1},{5,3},{7,5},{6,7},{4,6},{2,4},{0,2},{1,0},{11,9},{13,11},{15... | collective-permute-start | bytes 786440 | tf_op jit(solution)/shard_map/ppermute | solution.py:376
  27.3 2.0 %copy-start.1 = (bf16[3456,512]{1,0:T(8,128)(2,1)S(1)}, bf16[3456,512]{1,0:T(8,128)(2,1)}, u32[]{:S(2)}) copy-start(bf16[3456,512]{1,0:T(8,128)(2,1)} %down_ref.1) | copy-start | bytes 10616836
  27.3 3.1 %copy-start.2 = (bf16[512,3456]{1,0:T(8,128)(2,1)S(1)}, bf16[512,3456]{1,0:T(8,128)(2,1)}, u32[]{:S(2)}) copy-start(bf16[512,3456]{1,0:T(8,128)(2,1)} %up_ref.1) | copy-start | bytes 10616836
  32.3 10.8 %collective-permute-start.9 = (f32[128,3328]{1,0:T(8,128)S(1)}, f32[128,3328]{1,0:T(8,128)S(1)}, u32[]{:S(2)}, u32[]{:S(2)}) collective-permute-start(f32[128,3328]{1,0:T(8,128)S(1)} %pool.9), channel_id=1, source_target_pairs={{0,8},{8,0},{16,24},{24,16},{1,9},{9,1},{17,25},{25,17},{2,10},{10... | collective-permute-start | bytes 5111816 | tf_op jit(solution)/shard_map/ppermute | solution.py:324
  32.4 6.0 %collective-permute-start.7 = (bf16[512,128]{1,0:T(8,128)(2,1)S(1)}, bf16[512,128]{1,0:T(8,128)(2,1)S(1)}, u32[]{:S(2)}, u32[]{:S(2)}) collective-permute-start(bf16[512,128]{1,0:T(8,128)(2,1)S(1)} %slice.57), channel_id=1, source_target_pairs={{1,3},{3,5},{5,7},{7,6},{6,4},{4,2},{2,0},{0,1},{9,11},{11,13},{13... | collective-permute-start | bytes 393224 | tf_op jit(solution)/shard_map/ppermute | solution.py:393
  34.1 5.6 %collective-permute-start.8 = (bf16[512,128]{1,0:T(8,128)(2,1)S(1)}, bf16[512,128]{1,0:T(8,128)(2,1)S(1)}, u32[]{:S(2)}, u32[]{:S(2)}) collective-permute-start(bf16[512,128]{1,0:T(8,128)(2,1)S(1)} %slice.58), channel_id=1, source_target_pairs={{3,1},{5,3},{7,5},{6,7},{4,6},{2,4},{0,2},{1,0},{11,9},{13,11},{15... | collective-permute-start | bytes 393224 | tf_op jit(solution)/shard_map/ppermute | solution.py:393
  38.4 2.4 %copy-start.7 = (s32[128]{0:T(128)S(1)}, s32[128]{0:T(128)}, u32[]{:S(2)}) copy-start(s32[128]{0:T(128)} %param.16) | copy-start | bytes 1540
  40.7 2.4 %collective-permute-start.10 = (bf16[128,3328]{1,0:T(8,128)(2,1)S(1)}, bf16[128,3328]{1,0:T(8,128)(2,1)S(1)}, u32[]{:S(2)}, u32[]{:S(2)}) collective-permute-start(bf16[128,3328]{1,0:T(8,128)(2,1)S(1)} %pool.13), channel_id=1, source_target_pairs={{0,8},{8,0},{16,24},{24,16},{1,9},{9,1},{17,25},{25,17},{2,10},{10... | collective-permute-start | bytes 2555912 | tf_op jit(solution)/shard_map/ppermute | solution.py:324
  40.8 2.4 %copy-start.3 = (bf16[128,128]{1,0:T(8,128)(2,1)S(1)}, bf16[128,128]{1,0:T(8,128)(2,1)}, u32[]{:S(2)}) copy-start(bf16[128,128]{1,0:T(8,128)(2,1)} %dense_ref.1) | copy-start | bytes 98308
  40.8 2.3 %copy-start.4 = (f32[3456]{0:T(1024)S(1)}, f32[3456]{0:T(1024)}, u32[]{:S(2)}) copy-start(f32[3456]{0:T(1024)} %param.20) | copy-start | bytes 41476
  40.9 2.3 %copy-start.5 = (f32[3456]{0:T(1024)S(1)}, f32[3456]{0:T(1024)}, u32[]{:S(2)}) copy-start(f32[3456]{0:T(1024)} %param.21) | copy-start | bytes 41476
  40.9 2.3 %copy-start.6 = (f32[128]{0:T(128)S(1)}, f32[128]{0:T(128)}, u32[]{:S(2)}) copy-start(f32[128]{0:T(128)} %param.17) | copy-start | bytes 1540
  47.7 2.7 %collective-permute-start.11 = (bf16[3328,128]{1,0:T(8,128)(2,1)S(1)}, bf16[3328,128]{1,0:T(8,128)(2,1)S(1)}, u32[]{:S(2)}, u32[]{:S(2)}) collective-permute-start(bf16[3328,128]{1,0:T(8,128)(2,1)S(1)} %get-tuple-element.116.refs_1_), channel_id=1, source_target_pairs={{0,8},{8,0},{16,24},{24,16},{1,9},{9,1},{17,25},{25,17},{2,10},{10... | collective-permute-start | bytes 2555912 | tf_op jit(solution)/shard_map/ppermute | solution.py:324
  47.9 2.5 %collective-permute-start.12 = (f32[2,27,128]{2,1,0:T(8,128)S(1)}, f32[2,27,128]{2,1,0:T(8,128)S(1)}, u32[]{:S(2)}, u32[]{:S(2)}) collective-permute-start(f32[2,27,128]{2,1,0:T(8,128)S(1)} %get-tuple-element.97), channel_id=1, source_target_pairs={{0,8},{8,0},{16,24},{24,16},{1,9},{9,1},{17,25},{25,17},{2,10},{10... | collective-permute-start | bytes 82952 | tf_op jit(solution)/shard_map/ppermute | solution.py:324
  52.6 6.2 %collective-permute-start.14 = (bf16[512,128]{1,0:T(8,128)(2,1)S(1)}, bf16[512,128]{1,0:T(8,128)(2,1)S(1)}, u32[]{:S(2)}, u32[]{:S(2)}) collective-permute-start(bf16[512,128]{1,0:T(8,128)(2,1)S(1)} %get-tuple-element.138), channel_id=1, source_target_pairs={{3,1},{5,3},{7,5},{6,7},{4,6},{2,4},{0,2},{1,0},{11,9},{13,11},{15... | collective-permute-start | bytes 393224 | tf_op jit(solution)/shard_map/ppermute | solution.py:429
  53.3 5.5 %collective-permute-start.13 = (bf16[512,128]{1,0:T(8,128)(2,1)S(1)}, bf16[512,128]{1,0:T(8,128)(2,1)S(1)}, u32[]{:S(2)}, u32[]{:S(2)}) collective-permute-start(bf16[512,128]{1,0:T(8,128)(2,1)S(1)} %get-tuple-element.139), channel_id=1, source_target_pairs={{1,3},{3,5},{5,7},{7,6},{6,4},{4,2},{2,0},{0,1},{9,11},{11,13},{13... | collective-permute-start | bytes 393224 | tf_op jit(solution)/shard_map/ppermute | solution.py:429
  58.9 7.8 %collective-permute-start.16 = (bf16[1024,128]{1,0:T(8,128)(2,1)S(1)}, bf16[1024,128]{1,0:T(8,128)(2,1)S(1)}, u32[]{:S(2)}, u32[]{:S(2)}) collective-permute-start(bf16[1024,128]{1,0:T(8,128)(2,1)S(1)} %get-tuple-element.113), channel_id=1, source_target_pairs={{3,1},{5,3},{7,5},{6,7},{4,6},{2,4},{0,2},{1,0},{11,9},{13,11},{15... | collective-permute-start | bytes 786440 | tf_op jit(solution)/shard_map/ppermute | solution.py:429
  60.0 7.0 %collective-permute-start.15 = (bf16[1024,128]{1,0:T(8,128)(2,1)S(1)}, bf16[1024,128]{1,0:T(8,128)(2,1)S(1)}, u32[]{:S(2)}, u32[]{:S(2)}) collective-permute-start(bf16[1024,128]{1,0:T(8,128)(2,1)S(1)} %get-tuple-element.112), channel_id=1, source_target_pairs={{1,3},{3,5},{5,7},{7,6},{6,4},{4,2},{2,0},{0,1},{9,11},{11,13},{13... | collective-permute-start | bytes 786440 | tf_op jit(solution)/shard_map/ppermute | solution.py:429
  61.0 5.4 %collective-permute-start.17 = (f32[2,27,128]{2,1,0:T(8,128)S(1)}, f32[2,27,128]{2,1,0:T(8,128)S(1)}, u32[]{:S(2)}, u32[]{:S(2)}) collective-permute-start(f32[2,27,128]{2,1,0:T(8,128)S(1)} %add.68), channel_id=1, source_target_pairs={{0,16},{8,24},{16,0},{24,8},{1,17},{9,25},{17,1},{25,9},{2,18},{10... | collective-permute-start | bytes 82952 | tf_op jit(solution)/shard_map/ppermute | solution.py:324
  67.1 7.6 %collective-permute-start.19 = (bf16[1024,128]{1,0:T(8,128)(2,1)S(1)}, bf16[1024,128]{1,0:T(8,128)(2,1)S(1)}, u32[]{:S(2)}, u32[]{:S(2)}) collective-permute-start(bf16[1024,128]{1,0:T(8,128)(2,1)S(1)} %get-tuple-element.122), channel_id=1, source_target_pairs={{3,1},{5,3},{7,5},{6,7},{4,6},{2,4},{0,2},{1,0},{11,9},{13,11},{15... | collective-permute-start | bytes 786440 | tf_op jit(solution)/shard_map/ppermute | solution.py:429
  68.6 6.4 %collective-permute-start.18 = (bf16[1024,128]{1,0:T(8,128)(2,1)S(1)}, bf16[1024,128]{1,0:T(8,128)(2,1)S(1)}, u32[]{:S(2)}, u32[]{:S(2)}) collective-permute-start(bf16[1024,128]{1,0:T(8,128)(2,1)S(1)} %get-tuple-element.121), channel_id=1, source_target_pairs={{1,3},{3,5},{5,7},{7,6},{6,4},{4,2},{2,0},{0,1},{9,11},{11,13},{13... | collective-permute-start | bytes 786440 | tf_op jit(solution)/shard_map/ppermute | solution.py:429
  69.1 5.5 %collective-permute-start.20 = (f32[2,27,128]{2,1,0:T(8,128)S(1)}, f32[2,27,128]{2,1,0:T(8,128)S(1)}, u32[]{:S(2)}, u32[]{:S(2)}) collective-permute-start(f32[2,27,128]{2,1,0:T(8,128)S(1)} %add.73), channel_id=1, source_target_pairs={{0,1},{1,0},{2,3},{3,2},{4,5},{5,4},{6,7},{7,6},{8,9},{9,8},{10,11... | collective-permute-start | bytes 82952 | tf_op jit(solution)/shard_map/ppermute | solution.py:324
  75.1 8.3 %collective-permute-start.22 = (bf16[1024,128]{1,0:T(8,128)(2,1)S(1)}, bf16[1024,128]{1,0:T(8,128)(2,1)S(1)}, u32[]{:S(2)}, u32[]{:S(2)}) collective-permute-start(bf16[1024,128]{1,0:T(8,128)(2,1)S(1)} %get-tuple-element.125), channel_id=1, source_target_pairs={{3,1},{5,3},{7,5},{6,7},{4,6},{2,4},{0,2},{1,0},{11,9},{13,11},{15... | collective-permute-start | bytes 786440 | tf_op jit(solution)/shard_map/ppermute | solution.py:429
  76.7 6.7 %collective-permute-start.21 = (bf16[1024,128]{1,0:T(8,128)(2,1)S(1)}, bf16[1024,128]{1,0:T(8,128)(2,1)S(1)}, u32[]{:S(2)}, u32[]{:S(2)}) collective-permute-start(bf16[1024,128]{1,0:T(8,128)(2,1)S(1)} %get-tuple-element.124), channel_id=1, source_target_pairs={{1,3},{3,5},{5,7},{7,6},{6,4},{4,2},{2,0},{0,1},{9,11},{11,13},{13... | collective-permute-start | bytes 786440 | tf_op jit(solution)/shard_map/ppermute | solution.py:429
  77.2 6.3 %collective-permute-start.23 = (f32[2,27,128]{2,1,0:T(8,128)S(1)}, f32[2,27,128]{2,1,0:T(8,128)S(1)}, u32[]{:S(2)}, u32[]{:S(2)}) collective-permute-start(f32[2,27,128]{2,1,0:T(8,128)S(1)} %add.76), channel_id=1, source_target_pairs={{0,2},{1,3},{2,0},{3,1},{4,6},{5,7},{6,4},{7,5},{8,10},{9,11},{10,... | collective-permute-start | bytes 82952 | tf_op jit(solution)/shard_map/ppermute | solution.py:324
  83.5 6.6 %collective-permute-start.24 = (bf16[1024,128]{1,0:T(8,128)(2,1)S(1)}, bf16[1024,128]{1,0:T(8,128)(2,1)S(1)}, u32[]{:S(2)}, u32[]{:S(2)}) collective-permute-start(bf16[1024,128]{1,0:T(8,128)(2,1)S(1)} %fusion.7), channel_id=1, source_target_pairs={{0,16},{8,24},{16,0},{24,8},{1,17},{9,25},{17,1},{25,9},{2,18},{10... | collective-permute-start | bytes 786440 | tf_op jit(solution)/shard_map/ppermute | solution.py:324
  85.1 5.0 %collective-permute-start.25 = (f32[2,27,128]{2,1,0:T(8,128)S(1)}, f32[2,27,128]{2,1,0:T(8,128)S(1)}, u32[]{:S(2)}, u32[]{:S(2)}) collective-permute-start(f32[2,27,128]{2,1,0:T(8,128)S(1)} %add.79), channel_id=1, source_target_pairs={{0,4},{1,5},{2,6},{3,7},{4,0},{5,1},{6,2},{7,3},{8,12},{9,13},{10,... | collective-permute-start | bytes 82952 | tf_op jit(solution)/shard_map/ppermute | solution.py:324
  90.2 2.0 %collective-permute-start.26 = (f32[1024,128]{1,0:T(8,128)S(1)}, f32[1024,128]{1,0:T(8,128)S(1)}, u32[]{:S(2)}, u32[]{:S(2)}) collective-permute-start(f32[1024,128]{1,0:T(8,128)S(1)} %convert_add_fusion.part_ref), channel_id=1, source_target_pairs={{0,8},{8,0},{16,24},{24,16},{1,9},{9,1},{17,25},{25,17},{2,10},{10... | collective-permute-start | bytes 1572872 | tf_op jit(solution)/shard_map/ppermute | solution.py:324

commit v4 on v2

--- a/solution.py
+++ b/solution.py
@@ -10,6 +10,7 @@
 BF16 = jnp.bfloat16
 F32 = jnp.float32
 LANES = 128
+SPAN = 2
 CHUNK = 32
 VMEM_BYTES = 16 * 1024 * 1024
 
@@ -202,13 +203,18 @@
             (own_ref[:, here] + other_ref[:, here]).T.astype(BF16)
         )
     low = jnp.dot(x0_ref[...], down_ref[...], preferred_element_type=F32).astype(BF16)
+    spans = [(block, min(block + SPAN, blocks)) for block in range(0, blocks, SPAN)]
+    columns = lambda span: slice(span[0] * LANES, span[1] * LANES)
+    row = lambda ref, span: jnp.concatenate([ref[i : i + 1, :] for i in range(*span)], axis=1)
     logit = jnp.zeros((samples, LANES), F32)
-    for block in range(blocks):
-        here = slice(block * LANES, (block + 1) * LANES)
-        cross = jnp.dot(low, up_ref[:, here], preferred_element_type=F32) + bias_ref[block : block + 1, :]
+    for span in spans:
+        here = columns(span)
+        cross = jnp.dot(low, up_ref[:, here], preferred_element_type=F32) + row(bias_ref, span)
         cross_ref[:, here] = cross
         x0f = x0_ref[:, here].astype(F32)
-        logit = logit + (x0f * cross + x0f) * head_ref[block : block + 1, :]
+        terms = (x0f * cross + x0f) * row(head_ref, span)
+        for start in range(0, terms.shape[1], LANES):
+            logit = logit + terms[:, start : start + LANES]
     logit = jnp.sum(logit, axis=1, keepdims=True)
     d_logit = column(weight_ref) * (jax.nn.sigmoid(logit) - column(label_ref))
     for block in range(blocks):
@@ -222,17 +228,18 @@
     d_low = lax.dot_general(
         d_cross_ref[...], up_ref[...], (((1,), (1,)), ((), ())), preferred_element_type=F32
     ).astype(BF16)
-    for block in range(blocks):
-        here = slice(block * LANES, (block + 1) * LANES)
-        d_x1 = d_logit * head_ref[block : block + 1, :]
+    for span in spans:
+        here = columns(span)
+        d_x1 = d_logit * row(head_ref, span)
         d_x0 = d_x1 * (cross_ref[:, here] + 1.0) + lax.dot_general(
             d_low, down_ref[here, :], (((1,), (1,)), ((), ())), preferred_element_type=F32
         )
-        if block == 0:
-            dense_grad_ref[...] = d_x0.astype(BF16)
-        else:
-            place = slice((block - 1) * samples, block * samples)
-            d_pooled_ref[place, :] = d_x0.astype(BF16)
+        for block in range(*span):
+            part = d_x0[:, (block - span[0]) * LANES : (block - span[0] + 1) * LANES]
+            if block == 0:
+                dense_grad_ref[...] = part.astype(BF16)
+            else:
+                d_pooled_ref[(block - 1) * samples : block * samples, :] = part.astype(BF16)
 
 
 def cross_layer(dense, own, other, labels, weights, down_w, up_w, bias, head):

time: 93.3 us -> 93 us (level)
  no operation moved by 1% of the time
where the time goes in v4:
time: 93 us; the launch traced here: 92.8 us
  Pallas kernels  47.3 us (51%)
  starting transfers between devices  24.5 us (26%)
  waiting for transfers between devices  15.3 us (16%)
  local copies, waits for them, and re-layouts  2.2 us (2%)
  other arithmetic  2.2 us (2%)
  between operations  1.27 us (1%)
    pallas_call x5, Pallas kernels, spread(): pl.pallas_call(functools.partial(spread_kernel, turns, len(sides), at), o...  16 us
    pallas_call x7, Pallas kernels, pool(): pl.pallas_call(functools.partial(pool_kernel, [len(shard) for shard in sh...  12.7 us
    pallas_call x2, Pallas kernels, bag_counts(): pl.pallas_call(functools.partial(count_kernel, owners, local_rows, turns)...  12.6 us
    ppermute x10, waiting for transfers between devices, swap(): return lax.ppermute(value, axis, [(i, i ^ stride) for i in range(size)])  11.5 us
    ppermute x10, starting transfers between devices, swap(): return lax.ppermute(value, axis, [(i, i ^ stride) for i in range(size)])  6.96 us
    ppermute x3, starting transfers between devices, step(): lefts.append(lax.ppermute(a, 'emb', right))  6.14 us
    ppermute x4, starting transfers between devices, send(): lax.ppermute(to_right, 'emb', right)  5.48 us
    pallas_call x1, Pallas kernels, cross_layer(): pl.pallas_call(functools.partial(cross_kernel, tables), out_shape=(jax.Sh...  4.4 us
  transfers between devices with their start and end apart: 26, of which 11 were waited for; matrix products, arithmetic and copies ran while one was open for 3% of the time, Pallas kernels for 42%

profile of v4, /device:TPU:0, one launch (start us, length us, event | category | flops | bytes accessed | tf_op | source)
XLA Modules:
  0.0 92.8 jit_solution(1992014469249326393)
XLA Ops:
  0.7 1.0 %copy-done = bf16[2048,128]{1,0:T(8,128)(2,1)S(1)} copy-done((bf16[2048,128]{1,0:T(8,128)(2,1)S(1)}, bf16[2048,128]{1,0:T(8,128)(2,1)}, u32[]{:S(2)}) %copy-start) | copy-done | bytes 524312
  1.7 0.2 copy.16
  1.9 3.0 %collective-permute-start = (bf16[1024,128]{1,0:T(8,128)(2,1)S(1)}, bf16[1024,128]{1,0:T(8,128)(2,1)S(1)}, u32[]{:S(2)}, u32[]{:S(2)}) collective-permute-start(bf16[1024,128]{1,0:T(8,128)(2,1)S(1)} %bitcast.25), channel_id=1, source_target_pairs={{1,3},{3,5},{5,7},{7,6},{6,4},{4,2},{2,0},{0,1},{9,11},{11,13},{13... | collective-permute-start | bytes 786440 | tf_op jit(solution)/shard_map/ppermute | solution.py:378
  4.9 0.2 collective-permute-start.1
  5.0 0.7 multiply_bitcast_fusion
  5.8 0.9 fusion.8.place_ref
  6.7 0.1 collective-permute-start.2
  6.8 0.1 pad_add_fusion.where_ref
  6.8 5.2 %bag_counts.2 = (bf16[1024,3328]{1,0:T(8,128)(2,1)S(1)}, f32[26,128]{1,0:T(8,128)S(1)}, bf16[3328,128]{1,0:T(8,128)(2,1)S(1)}) custom-call(s32[2]{0:T(128)S(1)} %pad_add_fusion.where_ref, s32[26,8,128]{2,1,0:T(8,128)S(1)} %fusion.8.place_ref), custom_call_target="tpu_custom_call" | custom-call | flops 5000000000 | tf_op jit(solution)/shard_map/bag_counts/pallas_call | solution.py:121
  12.1 0.6 collective-permute-done.1.refs_3_.refs_1_
  12.6 1.6 %collective-permute-start.3 = (bf16[1024,128]{1,0:T(8,128)(2,1)S(1)}, bf16[1024,128]{1,0:T(8,128)(2,1)S(1)}, u32[]{:S(2)}, u32[]{:S(2)}) collective-permute-start(bf16[1024,128]{1,0:T(8,128)(2,1)S(1)} %collective-permute-done.refs_4_.refs_2_), channel_id=1, source_target_pairs={{1,3},{3,5},{5,7},{7,6},{6,4},{4,2},{2,0},{0,1},{9,11},{11,13},{13... | collective-permute-start | bytes 786440 | tf_op jit(solution)/shard_map/ppermute | solution.py:378
  14.2 0.4 collective-permute-start.4
  14.7 7.5 %bag_counts.3 = (bf16[1024,3328]{1,0:T(8,128)(2,1)S(1)}, f32[26,128]{1,0:T(8,128)S(1)}, bf16[3328,128]{1,0:T(8,128)(2,1)S(1)}, f32[128,3328]{1,0:T(8,128)S(1)}) custom-call(s32[2]{0:T(128)S(1)} %pad_add_fusion.where_ref, s32[26,8,128]{2,1,0:T(8,128)S(1)} %collective-permute-done.2.place_ref, f32[26,128]{1,0:T(8,128)S(1)} %get-tuple-element.82.refs_0_.turn_ref, ...), custom_call_target="tpu_custom_call" | custom-call | flops 5000000000 | tf_op jit(solution)/shard_map/bag_counts/pallas_call | solution.py:121
  22.1 0.3 collective-permute-done.4.refs_0_
  22.4 1.6 %collective-permute-start.5 = (bf16[1024,128]{1,0:T(8,128)(2,1)S(1)}, bf16[1024,128]{1,0:T(8,128)(2,1)S(1)}, u32[]{:S(2)}, u32[]{:S(2)}) collective-permute-start(bf16[1024,128]{1,0:T(8,128)(2,1)S(1)} %collective-permute-done.3.refs_1_), channel_id=1, source_target_pairs={{1,3},{3,5},{5,7},{7,6},{6,4},{4,2},{2,0},{0,1},{9,11},{11,13},{13... | collective-permute-start | bytes 786440 | tf_op jit(solution)/shard_map/ppermute | solution.py:378
  24.0 0.4 collective-permute-start.6
  24.5 2.8 %pool.8.refs_2_ = f32[128,3328]{1,0:T(8,128)S(1)} custom-call(f32[26,128]{1,0:T(8,128)S(1)} %get-tuple-element.87.turn_ref, bf16[1024,3328]{1,0:T(8,128)(2,1)S(1)} %get-tuple-element.120.counts_ref.refs_2_.refs_5_, bf16[1024,128]{1,0:T(8,128)(2,1)S(1)} %bitcast.28, bf16[1024,128]{1,0:T(8,128)(2,1)S(1)} %collective-permute-done.1.refs_3_.refs_1_, ...), custom_call_target="tpu_custom_call" | custom-call | tf_op jit(solution)/shard_map/pool/pallas_call | solution.py:160
  27.3 0.3 copy-done.2
  27.5 1.9 %pool.9.refs_2_ = f32[128,3328]{1,0:T(8,128)S(1)} custom-call(f32[26,128]{1,0:T(8,128)S(1)} %get-tuple-element.87.turn_ref, bf16[1024,3328]{1,0:T(8,128)(2,1)S(1)} %get-tuple-element.120.counts_ref.refs_2_.refs_5_, bf16[1024,128]{1,0:T(8,128)(2,1)S(1)} %collective-permute-done.4.refs_0_, bf16[1024,128]{1,0:T(8,128)(2,1)S(1)} %collective-permute-done.3.refs_1_, ...), custom_call_target="tpu_custom_call" | custom-call | tf_op jit(solution)/shard_map/pool/pallas_call | solution.py:160
  29.5 1.9 %pool.7.refs_2_ = f32[128,3328]{1,0:T(8,128)S(1)} custom-call(f32[26,128]{1,0:T(8,128)S(1)} %get-tuple-element.82.refs_0_.turn_ref, bf16[1024,3328]{1,0:T(8,128)(2,1)S(1)} %get-tuple-element.117.refs_1_.counts_ref.refs_2_, bf16[1024,128]{1,0:T(8,128)(2,1)S(1)} %collective-permute-done.4.refs_0_, bf16[1024,128]{1,0:T(8,128)(2,1)S(1)} %collective-permute-done.3.refs_1_, ...), custom_call_target="tpu_custom_call" | custom-call | tf_op jit(solution)/shard_map/pool/pallas_call | solution.py:160
  31.5 1.6 %collective-permute-start.7 = (bf16[512,128]{1,0:T(8,128)(2,1)S(1)}, bf16[512,128]{1,0:T(8,128)(2,1)S(1)}, u32[]{:S(2)}, u32[]{:S(2)}) collective-permute-start(bf16[512,128]{1,0:T(8,128)(2,1)S(1)} %slice.57), channel_id=1, source_target_pairs={{1,3},{3,5},{5,7},{7,6},{6,4},{4,2},{2,0},{0,1},{9,11},{11,13},{13... | collective-permute-start | bytes 393224 | tf_op jit(solution)/shard_map/ppermute | solution.py:396
  33.1 0.4 collective-permute-start.8
  33.5 1.9 %pool.11.refs_2_ = f32[128,3328]{1,0:T(8,128)S(1)} custom-call(f32[26,128]{1,0:T(8,128)S(1)} %get-tuple-element.87.turn_ref, bf16[1024,3328]{1,0:T(8,128)(2,1)S(1)} %get-tuple-element.120.counts_ref.refs_2_.refs_5_, bf16[1024,128]{1,0:T(8,128)(2,1)S(1)} %collective-permute-done.6.refs_0_, bf16[1024,128]{1,0:T(8,128)(2,1)S(1)} %collective-permute-done.5.refs_1_, ...), custom_call_target="tpu_custom_call" | custom-call | tf_op jit(solution)/shard_map/pool/pallas_call | solution.py:160
  35.5 2.0 %pool.10.refs_2_ = f32[128,3328]{1,0:T(8,128)S(1)} custom-call(f32[26,128]{1,0:T(8,128)S(1)} %get-tuple-element.82.refs_0_.turn_ref, bf16[1024,3328]{1,0:T(8,128)(2,1)S(1)} %get-tuple-element.117.refs_1_.counts_ref.refs_2_, bf16[1024,128]{1,0:T(8,128)(2,1)S(1)} %collective-permute-done.6.refs_0_, bf16[1024,128]{1,0:T(8,128)(2,1)S(1)} %collective-permute-done.5.refs_1_, ...), custom_call_target="tpu_custom_call" | custom-call | tf_op jit(solution)/shard_map/pool/pallas_call | solution.py:160
  37.5 0.6 collective-permute-done.8.refs_1_
  38.1 1.1 %pool.13 = f32[128,3328]{1,0:T(8,128)S(1)} custom-call(f32[26,128]{1,0:T(8,128)S(1)} %get-tuple-element.87.turn_ref, bf16[1024,3328]{1,0:T(8,128)(2,1)S(1)} %get-tuple-element.120.counts_ref.refs_2_.refs_5_, bf16[512,128]{1,0:T(8,128)(2,1)S(1)} %collective-permute-done.7.refs_0_, bf16[512,128]{1,0:T(8,128)(2,1)S(1)} %collective-permute-done.8.refs_1_, ...), custom_call_target="tpu_custom_call" | custom-call | tf_op jit(solution)/shard_map/pool/pallas_call | solution.py:160
  39.1 0.1 collective-permute-start.9
  39.3 1.1 %pool.12.own_ref = f32[128,3328]{1,0:T(8,128)S(1)} custom-call(f32[26,128]{1,0:T(8,128)S(1)} %get-tuple-element.82.refs_0_.turn_ref, bf16[1024,3328]{1,0:T(8,128)(2,1)S(1)} %get-tuple-element.117.refs_1_.counts_ref.refs_2_, bf16[512,128]{1,0:T(8,128)(2,1)S(1)} %collective-permute-done.7.refs_0_, bf16[512,128]{1,0:T(8,128)(2,1)S(1)} %collective-permute-done.8.refs_1_, ...), custom_call_target="tpu_custom_call" | custom-call | tf_op jit(solution)/shard_map/pool/pallas_call | solution.py:160
  40.3 2.5 %collective-permute-done.9.other_ref = f32[128,3328]{1,0:T(8,128)S(1)} collective-permute-done((f32[128,3328]{1,0:T(8,128)S(1)}, f32[128,3328]{1,0:T(8,128)S(1)}, u32[]{:S(2)}, u32[]{:S(2)}) %collective-permute-start.9) | collective-permute-done | bytes 1703968 | tf_op jit(solution)/shard_map/ppermute | solution.py:328
  42.8 4.4 %cross_layer.1 = (bf16[3328,128]{1,0:T(8,128)(2,1)S(1)}, bf16[128,128]{1,0:T(8,128)(2,1)}, f32[2,27,128]{2,1,0:T(8,128)S(1)}) custom-call(bf16[128,128]{1,0:T(8,128)(2,1)S(1)} %copy-done.3, f32[128,3328]{1,0:T(8,128)S(1)} %pool.12.own_ref, f32[128,3328]{1,0:T(8,128)S(1)} %collective-permute-done.9.other_ref, f32[1,128]{1,0:T(1,128)S(1)} %convert_bitcast_fusion.label_ref, ...), custom_call_target="tpu_custom_call" | custom-call | flops 8000000000 | bytes 12000000 | tf_op jit(solution)/shard_map/cross_layer/pallas_call | solution.py:249
  47.2 0.2 collective-permute-start.10
  47.4 0.4 collective-permute-start.11
  47.8 2.1 %spread.5.refs_3_ = f32[1024,256]{1,0:T(8,128)S(1)} custom-call(bf16[3328,128]{1,0:T(8,128)(2,1)S(1)} %get-tuple-element.115.refs_0_, bf16[3328,128]{1,0:T(8,128)(2,1)S(1)} %get-tuple-element.116.refs_1_, bf16[1024,3328]{1,0:T(8,128)(2,1)S(1)} %get-tuple-element.117.refs_1_.counts_ref.refs_2_), custom_call_target="tpu_custom_call" | custom-call | tf_op jit(solution)/shard_map/spread/pallas_call | solution.py:289
  49.9 2.1 %spread.6 = f32[1024,256]{1,0:T(8,128)S(1)} custom-call(bf16[3328,128]{1,0:T(8,128)(2,1)S(1)} %get-tuple-element.118.refs_0_.refs_3_, bf16[3328,128]{1,0:T(8,128)(2,1)S(1)} %collective-permute-done.10.refs_1_.refs_4_, bf16[1024,3328]{1,0:T(8,128)(2,1)S(1)} %get-tuple-element.120.counts_ref.refs_2_.refs_5_, f32[1024,256]{1,0:T(8,128)S(1)} %spread.5.refs_3_), custom_call_target="tpu_custom_call" | custom-call | tf_op jit(solution)/shard_map/spread/pallas_call | solution.py:289
  52.1 1.6 %collective-permute-start.12 = (bf16[512,128]{1,0:T(8,128)(2,1)S(1)}, bf16[512,128]{1,0:T(8,128)(2,1)S(1)}, u32[]{:S(2)}, u32[]{:S(2)}) collective-permute-start(bf16[512,128]{1,0:T(8,128)(2,1)S(1)} %get-tuple-element.139), channel_id=1, source_target_pairs={{1,3},{3,5},{5,7},{7,6},{6,4},{4,2},{2,0},{0,1},{9,11},{11,13},{13... | collective-permute-start | bytes 393224 | tf_op jit(solution)/shard_map/ppermute | solution.py:430
  53.8 0.4 collective-permute-start.13
  54.2 3.9 %spread.7 = f32[1024,256]{1,0:T(8,128)S(1)} custom-call(bf16[3328,128]{1,0:T(8,128)(2,1)S(1)} %get-tuple-element.115.refs_0_, bf16[3328,128]{1,0:T(8,128)(2,1)S(1)} %get-tuple-element.116.refs_1_, bf16[1024,3328]{1,0:T(8,128)(2,1)S(1)} %get-tuple-element.117.refs_1_.counts_ref.refs_2_, bf16[3328,128]{1,0:T(8,128)(2,1)S(1)} %get-tuple-element.118.refs_0_.refs_3_, ...), custom_call_target="tpu_custom_call" | custom-call | tf_op jit(solution)/shard_map/spread/pallas_call | solution.py:289
  58.2 0.8 collective-permute-done.13
  59.0 0.1 fusion.4
  59.1 1.6 %collective-permute-start.14 = (bf16[1024,128]{1,0:T(8,128)(2,1)S(1)}, bf16[1024,128]{1,0:T(8,128)(2,1)S(1)}, u32[]{:S(2)}, u32[]{:S(2)}) collective-permute-start(bf16[1024,128]{1,0:T(8,128)(2,1)S(1)} %get-tuple-element.112), channel_id=1, source_target_pairs={{1,3},{3,5},{5,7},{7,6},{6,4},{4,2},{2,0},{0,1},{9,11},{11,13},{13... | collective-permute-start | bytes 786440 | tf_op jit(solution)/shard_map/ppermute | solution.py:430
  60.7 0.4 collective-permute-start.15
  61.2 1.5 %collective-permute-start.16 = (f32[2,27,128]{2,1,0:T(8,128)S(1)}, f32[2,27,128]{2,1,0:T(8,128)S(1)}, u32[]{:S(2)}, u32[]{:S(2)}) collective-permute-start(f32[2,27,128]{2,1,0:T(8,128)S(1)} %add.68), channel_id=1, source_target_pairs={{0,16},{8,24},{16,0},{24,8},{1,17},{9,25},{17,1},{25,9},{2,18},{10... | collective-permute-start | bytes 82952 | tf_op jit(solution)/shard_map/ppermute | solution.py:328
  62.7 3.9 %spread.8 = f32[1024,256]{1,0:T(8,128)S(1)} custom-call(bf16[3328,128]{1,0:T(8,128)(2,1)S(1)} %get-tuple-element.115.refs_0_, bf16[3328,128]{1,0:T(8,128)(2,1)S(1)} %get-tuple-element.116.refs_1_, bf16[1024,3328]{1,0:T(8,128)(2,1)S(1)} %get-tuple-element.117.refs_1_.counts_ref.refs_2_, bf16[3328,128]{1,0:T(8,128)(2,1)S(1)} %get-tuple-element.118.refs_0_.refs_3_, ...), custom_call_target="tpu_custom_call" | custom-call | tf_op jit(solution)/shard_map/spread/pallas_call | solution.py:289
  66.6 1.0 %collective-permute-done.15 = bf16[1024,128]{1,0:T(8,128)(2,1)S(1)} collective-permute-done((bf16[1024,128]{1,0:T(8,128)(2,1)S(1)}, bf16[1024,128]{1,0:T(8,128)(2,1)S(1)}, u32[]{:S(2)}, u32[]{:S(2)}) %collective-permute-start.15) | collective-permute-done | bytes 262176 | tf_op jit(solution)/shard_map/ppermute | solution.py:430
  67.7 0.1 fusion.2
  67.8 1.4 %collective-permute-start.17 = (bf16[1024,128]{1,0:T(8,128)(2,1)S(1)}, bf16[1024,128]{1,0:T(8,128)(2,1)S(1)}, u32[]{:S(2)}, u32[]{:S(2)}) collective-permute-start(bf16[1024,128]{1,0:T(8,128)(2,1)S(1)} %get-tuple-element.121), channel_id=1, source_target_pairs={{1,3},{3,5},{5,7},{7,6},{6,4},{4,2},{2,0},{0,1},{9,11},{11,13},{13... | collective-permute-start | bytes 786440 | tf_op jit(solution)/shard_map/ppermute | solution.py:430
  69.1 0.7 collective-permute-start.18
  69.8 1.3 %collective-permute-start.19 = (f32[2,27,128]{2,1,0:T(8,128)S(1)}, f32[2,27,128]{2,1,0:T(8,128)S(1)}, u32[]{:S(2)}, u32[]{:S(2)}) collective-permute-start(f32[2,27,128]{2,1,0:T(8,128)S(1)} %add.73), channel_id=1, source_target_pairs={{0,1},{1,0},{2,3},{3,2},{4,5},{5,4},{6,7},{7,6},{8,9},{9,8},{10,11... | collective-permute-start | bytes 82952 | tf_op jit(solution)/shard_map/ppermute | solution.py:328
  71.2 3.9 %spread.9 = f32[1024,256]{1,0:T(8,128)S(1)} custom-call(bf16[3328,128]{1,0:T(8,128)(2,1)S(1)} %get-tuple-element.115.refs_0_, bf16[3328,128]{1,0:T(8,128)(2,1)S(1)} %get-tuple-element.116.refs_1_, bf16[1024,3328]{1,0:T(8,128)(2,1)S(1)} %get-tuple-element.117.refs_1_.counts_ref.refs_2_, bf16[3328,128]{1,0:T(8,128)(2,1)S(1)} %get-tuple-element.118.refs_0_.refs_3_, ...), custom_call_target="tpu_custom_call" | custom-call | tf_op jit(solution)/shard_map/spread/pallas_call | solution.py:289
  75.1 0.8 collective-permute-done.19
  75.9 0.1 fusion
  76.0 0.8 collective-permute-start.20
  76.8 1.2 %collective-permute-start.21 = (bf16[1024,128]{1,0:T(8,128)(2,1)S(1)}, bf16[1024,128]{1,0:T(8,128)(2,1)S(1)}, u32[]{:S(2)}, u32[]{:S(2)}) collective-permute-start(bf16[1024,128]{1,0:T(8,128)(2,1)S(1)} %get-tuple-element.125), channel_id=1, source_target_pairs={{3,1},{5,3},{7,5},{6,7},{4,6},{2,4},{0,2},{1,0},{11,9},{13,11},{15... | collective-permute-start | bytes 786440 | tf_op jit(solution)/shard_map/ppermute | solution.py:430
  78.1 0.4 collective-permute-start.22
  78.5 4.3 %collective-permute-done.22 = f32[2,27,128]{2,1,0:T(8,128)S(1)} collective-permute-done((f32[2,27,128]{2,1,0:T(8,128)S(1)}, f32[2,27,128]{2,1,0:T(8,128)S(1)}, u32[]{:S(2)}, u32[]{:S(2)}) %collective-permute-start.22) | collective-permute-done | bytes 27680 | tf_op jit(solution)/shard_map/ppermute | solution.py:328
  82.8 0.4 collective-permute-done.21
  83.2 0.1 fusion.7
  83.3 1.6 %collective-permute-start.23 = (bf16[1024,128]{1,0:T(8,128)(2,1)S(1)}, bf16[1024,128]{1,0:T(8,128)(2,1)S(1)}, u32[]{:S(2)}, u32[]{:S(2)}) collective-permute-start(bf16[1024,128]{1,0:T(8,128)(2,1)S(1)} %fusion.7), channel_id=1, source_target_pairs={{0,16},{8,24},{16,0},{24,8},{1,17},{9,25},{17,1},{25,9},{2,18},{10... | collective-permute-start | bytes 786440 | tf_op jit(solution)/shard_map/ppermute | solution.py:328
  84.9 1.3 %collective-permute-start.24 = (f32[2,27,128]{2,1,0:T(8,128)S(1)}, f32[2,27,128]{2,1,0:T(8,128)S(1)}, u32[]{:S(2)}, u32[]{:S(2)}) collective-permute-start(f32[2,27,128]{2,1,0:T(8,128)S(1)} %add.79), channel_id=1, source_target_pairs={{0,4},{1,5},{2,6},{3,7},{4,0},{5,1},{6,2},{7,3},{8,12},{9,13},{10,... | collective-permute-start | bytes 82952 | tf_op jit(solution)/shard_map/ppermute | solution.py:328
  86.2 3.5 %collective-permute-done.24 = f32[2,27,128]{2,1,0:T(8,128)S(1)} collective-permute-done((f32[2,27,128]{2,1,0:T(8,128)S(1)}, f32[2,27,128]{2,1,0:T(8,128)S(1)}, u32[]{:S(2)}, u32[]{:S(2)}) %collective-permute-start.24) | collective-permute-done | bytes 27680 | tf_op jit(solution)/shard_map/ppermute | solution.py:328
  89.9 0.8 place_half.2.refs_0_
  90.7 0.6 slice_bitcast_fusion
  91.3 0.5 collective-permute-done.25.part_ref
  91.8 0.8 place_half.3
  (43 shorter events, 0.4 us)
Async XLA Ops:
  0.6 1.0 %copy-start = (bf16[2048,128]{1,0:T(8,128)(2,1)S(1)}, bf16[2048,128]{1,0:T(8,128)(2,1)}, u32[]{:S(2)}) copy-start(bf16[2048,128]{1,0:T(8,128)(2,1)} %param.11) | copy-start | bytes 1572868
  1.9 10.2 %collective-permute-start = (bf16[1024,128]{1,0:T(8,128)(2,1)S(1)}, bf16[1024,128]{1,0:T(8,128)(2,1)S(1)}, u32[]{:S(2)}, u32[]{:S(2)}) collective-permute-start(bf16[1024,128]{1,0:T(8,128)(2,1)S(1)} %bitcast.25), channel_id=1, source_target_pairs={{1,3},{3,5},{5,7},{7,6},{6,4},{4,2},{2,0},{0,1},{9,11},{11,13},{13... | collective-permute-start | bytes 786440 | tf_op jit(solution)/shard_map/ppermute | solution.py:378
  4.9 7.8 %collective-permute-start.1 = (bf16[1024,128]{1,0:T(8,128)(2,1)S(1)}, bf16[1024,128]{1,0:T(8,128)(2,1)S(1)}, u32[]{:S(2)}, u32[]{:S(2)}) collective-permute-start(bf16[1024,128]{1,0:T(8,128)(2,1)S(1)} %bitcast.26), channel_id=1, source_target_pairs={{3,1},{5,3},{7,5},{6,7},{4,6},{2,4},{0,2},{1,0},{11,9},{13,11},{15... | collective-permute-start | bytes 786440 | tf_op jit(solution)/shard_map/ppermute | solution.py:379
  6.7 5.4 %collective-permute-start.2 = (s32[26,8,128]{2,1,0:T(8,128)S(1)}, s32[26,8,128]{2,1,0:T(8,128)S(1)}, u32[]{:S(2)}, u32[]{:S(2)}) collective-permute-start(s32[26,8,128]{2,1,0:T(8,128)S(1)} %fusion.8.place_ref), channel_id=1, source_target_pairs={{0,8},{8,0},{16,24},{24,16},{1,9},{9,1},{17,25},{25,17},{2,10},{10... | collective-permute-start | bytes 319496 | tf_op jit(solution)/shard_map/ppermute | solution.py:328
  12.6 9.5 %collective-permute-start.3 = (bf16[1024,128]{1,0:T(8,128)(2,1)S(1)}, bf16[1024,128]{1,0:T(8,128)(2,1)S(1)}, u32[]{:S(2)}, u32[]{:S(2)}) collective-permute-start(bf16[1024,128]{1,0:T(8,128)(2,1)S(1)} %collective-permute-done.refs_4_.refs_2_), channel_id=1, source_target_pairs={{1,3},{3,5},{5,7},{7,6},{6,4},{4,2},{2,0},{0,1},{9,11},{11,13},{13... | collective-permute-start | bytes 786440 | tf_op jit(solution)/shard_map/ppermute | solution.py:378
  14.2 8.2 %collective-permute-start.4 = (bf16[1024,128]{1,0:T(8,128)(2,1)S(1)}, bf16[1024,128]{1,0:T(8,128)(2,1)S(1)}, u32[]{:S(2)}, u32[]{:S(2)}) collective-permute-start(bf16[1024,128]{1,0:T(8,128)(2,1)S(1)} %collective-permute-done.1.refs_3_.refs_1_), channel_id=1, source_target_pairs={{3,1},{5,3},{7,5},{6,7},{4,6},{2,4},{0,2},{1,0},{11,9},{13,11},{15... | collective-permute-start | bytes 786440 | tf_op jit(solution)/shard_map/ppermute | solution.py:379
  22.4 9.0 %collective-permute-start.5 = (bf16[1024,128]{1,0:T(8,128)(2,1)S(1)}, bf16[1024,128]{1,0:T(8,128)(2,1)S(1)}, u32[]{:S(2)}, u32[]{:S(2)}) collective-permute-start(bf16[1024,128]{1,0:T(8,128)(2,1)S(1)} %collective-permute-done.3.refs_1_), channel_id=1, source_target_pairs={{1,3},{3,5},{5,7},{7,6},{6,4},{4,2},{2,0},{0,1},{9,11},{11,13},{13... | collective-permute-start | bytes 786440 | tf_op jit(solution)/shard_map/ppermute | solution.py:378
  24.0 7.4 %collective-permute-start.6 = (bf16[1024,128]{1,0:T(8,128)(2,1)S(1)}, bf16[1024,128]{1,0:T(8,128)(2,1)S(1)}, u32[]{:S(2)}, u32[]{:S(2)}) collective-permute-start(bf16[1024,128]{1,0:T(8,128)(2,1)S(1)} %collective-permute-done.4.refs_0_), channel_id=1, source_target_pairs={{3,1},{5,3},{7,5},{6,7},{4,6},{2,4},{0,2},{1,0},{11,9},{13,11},{15... | collective-permute-start | bytes 786440 | tf_op jit(solution)/shard_map/ppermute | solution.py:379
  24.4 2.8 %copy-start.1 = (bf16[3456,512]{1,0:T(8,128)(2,1)S(1)}, bf16[3456,512]{1,0:T(8,128)(2,1)}, u32[]{:S(2)}) copy-start(bf16[3456,512]{1,0:T(8,128)(2,1)} %down_ref.1) | copy-start | bytes 10616836
  24.5 3.1 %copy-start.2 = (bf16[512,3456]{1,0:T(8,128)(2,1)S(1)}, bf16[512,3456]{1,0:T(8,128)(2,1)}, u32[]{:S(2)}) copy-start(bf16[512,3456]{1,0:T(8,128)(2,1)} %up_ref.1) | copy-start | bytes 10616836
  31.5 6.0 %collective-permute-start.7 = (bf16[512,128]{1,0:T(8,128)(2,1)S(1)}, bf16[512,128]{1,0:T(8,128)(2,1)S(1)}, u32[]{:S(2)}, u32[]{:S(2)}) collective-permute-start(bf16[512,128]{1,0:T(8,128)(2,1)S(1)} %slice.57), channel_id=1, source_target_pairs={{1,3},{3,5},{5,7},{7,6},{6,4},{4,2},{2,0},{0,1},{9,11},{11,13},{13... | collective-permute-start | bytes 393224 | tf_op jit(solution)/shard_map/ppermute | solution.py:396
  33.1 5.0 %collective-permute-start.8 = (bf16[512,128]{1,0:T(8,128)(2,1)S(1)}, bf16[512,128]{1,0:T(8,128)(2,1)S(1)}, u32[]{:S(2)}, u32[]{:S(2)}) collective-permute-start(bf16[512,128]{1,0:T(8,128)(2,1)S(1)} %slice.58), channel_id=1, source_target_pairs={{3,1},{5,3},{7,5},{6,7},{4,6},{2,4},{0,2},{1,0},{11,9},{13,11},{15... | collective-permute-start | bytes 393224 | tf_op jit(solution)/shard_map/ppermute | solution.py:396
  37.5 1.8 %copy-start.7 = (s32[128]{0:T(128)S(1)}, s32[128]{0:T(128)}, u32[]{:S(2)}) copy-start(s32[128]{0:T(128)} %param.16) | copy-start | bytes 1540
  39.1 3.7 %collective-permute-start.9 = (f32[128,3328]{1,0:T(8,128)S(1)}, f32[128,3328]{1,0:T(8,128)S(1)}, u32[]{:S(2)}, u32[]{:S(2)}) collective-permute-start(f32[128,3328]{1,0:T(8,128)S(1)} %pool.13), channel_id=1, source_target_pairs={{0,8},{8,0},{16,24},{24,16},{1,9},{9,1},{17,25},{25,17},{2,10},{10... | collective-permute-start | bytes 5111816 | tf_op jit(solution)/shard_map/ppermute | solution.py:328
  39.2 3.6 %copy-start.3 = (bf16[128,128]{1,0:T(8,128)(2,1)S(1)}, bf16[128,128]{1,0:T(8,128)(2,1)}, u32[]{:S(2)}) copy-start(bf16[128,128]{1,0:T(8,128)(2,1)} %dense_ref.1) | copy-start | bytes 98308
  39.2 3.6 %copy-start.4 = (f32[3456]{0:T(1024)S(1)}, f32[3456]{0:T(1024)}, u32[]{:S(2)}) copy-start(f32[3456]{0:T(1024)} %param.20) | copy-start | bytes 41476
  39.3 3.5 %copy-start.5 = (f32[3456]{0:T(1024)S(1)}, f32[3456]{0:T(1024)}, u32[]{:S(2)}) copy-start(f32[3456]{0:T(1024)} %param.21) | copy-start | bytes 41476
  39.3 3.5 %copy-start.6 = (f32[128]{0:T(128)S(1)}, f32[128]{0:T(128)}, u32[]{:S(2)}) copy-start(f32[128]{0:T(128)} %param.17) | copy-start | bytes 1540
  47.2 2.7 %collective-permute-start.10 = (bf16[3328,128]{1,0:T(8,128)(2,1)S(1)}, bf16[3328,128]{1,0:T(8,128)(2,1)S(1)}, u32[]{:S(2)}, u32[]{:S(2)}) collective-permute-start(bf16[3328,128]{1,0:T(8,128)(2,1)S(1)} %get-tuple-element.116.refs_1_), channel_id=1, source_target_pairs={{0,8},{8,0},{16,24},{24,16},{1,9},{9,1},{17,25},{25,17},{2,10},{10... | collective-permute-start | bytes 2555912 | tf_op jit(solution)/shard_map/ppermute | solution.py:328
  47.4 2.5 %collective-permute-start.11 = (f32[2,27,128]{2,1,0:T(8,128)S(1)}, f32[2,27,128]{2,1,0:T(8,128)S(1)}, u32[]{:S(2)}, u32[]{:S(2)}) collective-permute-start(f32[2,27,128]{2,1,0:T(8,128)S(1)} %get-tuple-element.97), channel_id=1, source_target_pairs={{0,8},{8,0},{16,24},{24,16},{1,9},{9,1},{17,25},{25,17},{2,10},{10... | collective-permute-start | bytes 82952 | tf_op jit(solution)/shard_map/ppermute | solution.py:328
  52.1 6.0 %collective-permute-start.12 = (bf16[512,128]{1,0:T(8,128)(2,1)S(1)}, bf16[512,128]{1,0:T(8,128)(2,1)S(1)}, u32[]{:S(2)}, u32[]{:S(2)}) collective-permute-start(bf16[512,128]{1,0:T(8,128)(2,1)S(1)} %get-tuple-element.139), channel_id=1, source_target_pairs={{1,3},{3,5},{5,7},{7,6},{6,4},{4,2},{2,0},{0,1},{9,11},{11,13},{13... | collective-permute-start | bytes 393224 | tf_op jit(solution)/shard_map/ppermute | solution.py:430
  53.8 5.2 %collective-permute-start.13 = (bf16[512,128]{1,0:T(8,128)(2,1)S(1)}, bf16[512,128]{1,0:T(8,128)(2,1)S(1)}, u32[]{:S(2)}, u32[]{:S(2)}) collective-permute-start(bf16[512,128]{1,0:T(8,128)(2,1)S(1)} %get-tuple-element.138), channel_id=1, source_target_pairs={{3,1},{5,3},{7,5},{6,7},{4,6},{2,4},{0,2},{1,0},{11,9},{13,11},{15... | collective-permute-start | bytes 393224 | tf_op jit(solution)/shard_map/ppermute | solution.py:430
  59.1 7.5 %collective-permute-start.14 = (bf16[1024,128]{1,0:T(8,128)(2,1)S(1)}, bf16[1024,128]{1,0:T(8,128)(2,1)S(1)}, u32[]{:S(2)}, u32[]{:S(2)}) collective-permute-start(bf16[1024,128]{1,0:T(8,128)(2,1)S(1)} %get-tuple-element.112), channel_id=1, source_target_pairs={{1,3},{3,5},{5,7},{7,6},{6,4},{4,2},{2,0},{0,1},{9,11},{11,13},{13... | collective-permute-start | bytes 786440 | tf_op jit(solution)/shard_map/ppermute | solution.py:430
  60.7 6.9 %collective-permute-start.15 = (bf16[1024,128]{1,0:T(8,128)(2,1)S(1)}, bf16[1024,128]{1,0:T(8,128)(2,1)S(1)}, u32[]{:S(2)}, u32[]{:S(2)}) collective-permute-start(bf16[1024,128]{1,0:T(8,128)(2,1)S(1)} %get-tuple-element.113), channel_id=1, source_target_pairs={{3,1},{5,3},{7,5},{6,7},{4,6},{2,4},{0,2},{1,0},{11,9},{13,11},{15... | collective-permute-start | bytes 786440 | tf_op jit(solution)/shard_map/ppermute | solution.py:430
  61.2 5.4 %collective-permute-start.16 = (f32[2,27,128]{2,1,0:T(8,128)S(1)}, f32[2,27,128]{2,1,0:T(8,128)S(1)}, u32[]{:S(2)}, u32[]{:S(2)}) collective-permute-start(f32[2,27,128]{2,1,0:T(8,128)S(1)} %add.68), channel_id=1, source_target_pairs={{0,16},{8,24},{16,0},{24,8},{1,17},{9,25},{17,1},{25,9},{2,18},{10... | collective-permute-start | bytes 82952 | tf_op jit(solution)/shard_map/ppermute | solution.py:328
  67.8 8.1 %collective-permute-start.17 = (bf16[1024,128]{1,0:T(8,128)(2,1)S(1)}, bf16[1024,128]{1,0:T(8,128)(2,1)S(1)}, u32[]{:S(2)}, u32[]{:S(2)}) collective-permute-start(bf16[1024,128]{1,0:T(8,128)(2,1)S(1)} %get-tuple-element.121), channel_id=1, source_target_pairs={{1,3},{3,5},{5,7},{7,6},{6,4},{4,2},{2,0},{0,1},{9,11},{11,13},{13... | collective-permute-start | bytes 786440 | tf_op jit(solution)/shard_map/ppermute | solution.py:430
  69.1 6.7 %collective-permute-start.18 = (bf16[1024,128]{1,0:T(8,128)(2,1)S(1)}, bf16[1024,128]{1,0:T(8,128)(2,1)S(1)}, u32[]{:S(2)}, u32[]{:S(2)}) collective-permute-start(bf16[1024,128]{1,0:T(8,128)(2,1)S(1)} %get-tuple-element.122), channel_id=1, source_target_pairs={{3,1},{5,3},{7,5},{6,7},{4,6},{2,4},{0,2},{1,0},{11,9},{13,11},{15... | collective-permute-start | bytes 786440 | tf_op jit(solution)/shard_map/ppermute | solution.py:430
  69.8 6.0 %collective-permute-start.19 = (f32[2,27,128]{2,1,0:T(8,128)S(1)}, f32[2,27,128]{2,1,0:T(8,128)S(1)}, u32[]{:S(2)}, u32[]{:S(2)}) collective-permute-start(f32[2,27,128]{2,1,0:T(8,128)S(1)} %add.73), channel_id=1, source_target_pairs={{0,1},{1,0},{2,3},{3,2},{4,5},{5,4},{6,7},{7,6},{8,9},{9,8},{10,11... | collective-permute-start | bytes 82952 | tf_op jit(solution)/shard_map/ppermute | solution.py:328
  76.0 6.8 %collective-permute-start.20 = (bf16[1024,128]{1,0:T(8,128)(2,1)S(1)}, bf16[1024,128]{1,0:T(8,128)(2,1)S(1)}, u32[]{:S(2)}, u32[]{:S(2)}) collective-permute-start(bf16[1024,128]{1,0:T(8,128)(2,1)S(1)} %get-tuple-element.124), channel_id=1, source_target_pairs={{1,3},{3,5},{5,7},{7,6},{6,4},{4,2},{2,0},{0,1},{9,11},{11,13},{13... | collective-permute-start | bytes 786440 | tf_op jit(solution)/shard_map/ppermute | solution.py:430
  76.8 6.4 %collective-permute-start.21 = (bf16[1024,128]{1,0:T(8,128)(2,1)S(1)}, bf16[1024,128]{1,0:T(8,128)(2,1)S(1)}, u32[]{:S(2)}, u32[]{:S(2)}) collective-permute-start(bf16[1024,128]{1,0:T(8,128)(2,1)S(1)} %get-tuple-element.125), channel_id=1, source_target_pairs={{3,1},{5,3},{7,5},{6,7},{4,6},{2,4},{0,2},{1,0},{11,9},{13,11},{15... | collective-permute-start | bytes 786440 | tf_op jit(solution)/shard_map/ppermute | solution.py:430
  78.1 4.7 %collective-permute-start.22 = (f32[2,27,128]{2,1,0:T(8,128)S(1)}, f32[2,27,128]{2,1,0:T(8,128)S(1)}, u32[]{:S(2)}, u32[]{:S(2)}) collective-permute-start(f32[2,27,128]{2,1,0:T(8,128)S(1)} %add.76), channel_id=1, source_target_pairs={{0,2},{1,3},{2,0},{3,1},{4,6},{5,7},{6,4},{7,5},{8,10},{9,11},{10,... | collective-permute-start | bytes 82952 | tf_op jit(solution)/shard_map/ppermute | solution.py:328
  83.3 6.4 %collective-permute-start.23 = (bf16[1024,128]{1,0:T(8,128)(2,1)S(1)}, bf16[1024,128]{1,0:T(8,128)(2,1)S(1)}, u32[]{:S(2)}, u32[]{:S(2)}) collective-permute-start(bf16[1024,128]{1,0:T(8,128)(2,1)S(1)} %fusion.7), channel_id=1, source_target_pairs={{0,16},{8,24},{16,0},{24,8},{1,17},{9,25},{17,1},{25,9},{2,18},{10... | collective-permute-start | bytes 786440 | tf_op jit(solution)/shard_map/ppermute | solution.py:328
  84.9 4.8 %collective-permute-start.24 = (f32[2,27,128]{2,1,0:T(8,128)S(1)}, f32[2,27,128]{2,1,0:T(8,128)S(1)}, u32[]{:S(2)}, u32[]{:S(2)}) collective-permute-start(f32[2,27,128]{2,1,0:T(8,128)S(1)} %add.79), channel_id=1, source_target_pairs={{0,4},{1,5},{2,6},{3,7},{4,0},{5,1},{6,2},{7,3},{8,12},{9,13},{10,... | collective-permute-start | bytes 82952 | tf_op jit(solution)/shard_map/ppermute | solution.py:328
  89.8 2.0 %collective-permute-start.25 = (f32[1024,128]{1,0:T(8,128)S(1)}, f32[1024,128]{1,0:T(8,128)S(1)}, u32[]{:S(2)}, u32[]{:S(2)}) collective-permute-start(f32[1024,128]{1,0:T(8,128)S(1)} %convert_add_fusion.part_ref), channel_id=1, source_target_pairs={{0,8},{8,0},{16,24},{24,16},{1,9},{9,1},{17,25},{25,17},{2,10},{10... | collective-permute-start | bytes 1572872 | tf_op jit(solution)/shard_map/ppermute | solution.py:328

commit v5 on v2

--- a/solution.py
+++ b/solution.py
@@ -128,7 +128,7 @@
     )(where, place, *operands)
 
 
-def pool_kernel(shards, turns, tables, added, turn_ref, counts_ref, *refs):
+def pool_kernel(shards, turns, tables, added, span, turn_ref, counts_ref, *refs):
     sum_ref = refs[-1]
     blocks = refs[: sum(shards)]
     before = refs[sum(shards) : sum(shards) + added]
@@ -137,7 +137,7 @@
         left.append(side_by_side(blocks[at : at + parts]))
         at += parts
     left = jnp.concatenate(left, axis=0)
-    for start in range(0, turn_ref.shape[0], tables):
+    for start in range(*span, tables):
         bags = slice(start * LANES, (start + tables) * LANES)
         product = jnp.dot(left, counts_ref[:, bags], preferred_element_type=F32)
         for table in range(tables):
@@ -147,24 +147,26 @@
             for i, one in enumerate(turns):
                 mine = product[i * LANES : (i + 1) * LANES, table * LANES : (table + 1) * LANES]
                 total = jnp.where(turn == one, mine, total)
-            sum_ref[:, here] = total
-
-
-def pool(turns, turn, counts, shards, before, ahead=()):
+            place = start + table - span[0]
+            sum_ref[:, place * LANES : (place + 1) * LANES] = total
+
+
+def pool(turns, turn, counts, shards, before, ahead=(), span=None):
     rows, bags = counts.shape
     blocks = [block for shard in shards for block in shard]
     width = blocks[0].shape[1]
-    tables = turn.shape[0]
+    first, last = span or (0, turn.shape[0])
     extra = ([] if before is None else [before]) + list(ahead)
     return pl.pallas_call(
         functools.partial(
             pool_kernel,
             [len(shard) for shard in shards],
             turns,
-            tables if len(turns) <= 4 else tables // 2,
+            (last - first) if len(turns) <= 4 else (last - first) // 2,
             0 if before is None else 1,
+            (first, last),
         ),
-        out_shape=jax.ShapeDtypeStruct((width, bags), F32),
+        out_shape=jax.ShapeDtypeStruct((width, (last - first) * LANES), F32),
         in_specs=[VMEM] * (2 + len(blocks) + len(extra)),
         out_specs=VMEM,
         compiler_params=params(),
@@ -177,7 +179,8 @@
     tables,
     dense_ref,
     own_ref,
-    other_ref,
+    first_ref,
+    second_ref,
     label_ref,
     weight_ref,
     down_ref,
@@ -198,8 +201,10 @@
     x0_ref[:, :LANES] = dense_ref[...]
     for table in range(tables):
         here = slice(table * LANES, (table + 1) * LANES)
+        part, start = (first_ref, 0) if table < tables // 2 else (second_ref, tables // 2)
+        other = part[:, (table - start) * LANES : (table - start + 1) * LANES]
         x0_ref[:, (table + 1) * LANES : (table + 2) * LANES] = (
-            (own_ref[:, here] + other_ref[:, here]).T.astype(BF16)
+            (own_ref[:, here] + other).T.astype(BF16)
         )
     low = jnp.dot(x0_ref[...], down_ref[...], preferred_element_type=F32).astype(BF16)
     logit = jnp.zeros((samples, LANES), F32)
@@ -235,7 +240,7 @@
             d_pooled_ref[place, :] = d_x0.astype(BF16)
 
 
-def cross_layer(dense, own, other, labels, weights, down_w, up_w, bias, head):
+def cross_layer(dense, own, first, second, labels, weights, down_w, up_w, bias, head):
     samples, width = dense.shape
     tables = own.shape[1] // samples
     cross = down_w.shape[0]
@@ -254,7 +259,7 @@
         compiler_params=params(),
         cost_estimate=cost(8 * 10**9, 12 * 10**6),
         name="cross_layer",
-    )(dense, own, other, labels, weights, down_w, up_w, bias, head)
+    )(dense, own, first, second, labels, weights, down_w, up_w, bias, head)
 
 
 def spread_kernel(turns, count, at, *refs):
@@ -361,6 +366,7 @@
             here = tuple(range(start, start + 8))
             for side in (1, 0):
                 add(side, here, [[table[one]] for one in here])
+        sums[1] = [swap(one, "grp", 1) for one in jnp.split(sums[1], 2, axis=1)]
         return sides, sums
     right, left = ring_turns(owners)
     lefts, rights = [shard], [shard]
@@ -390,8 +396,12 @@
     for side in (1, 0):
         add(side, (3, 5), [[rights[3]], [lefts[3]]])
     sums[0], sums[1] = lax.optimization_barrier((sums[0], sums[1]))
-    for side in (1, 0):
-        add(side, (4,), [far])
+    turn, lent, tables = sides[1][1], sums[1], places[0].shape[0]
+    sums[1] = [
+        swap(pool((4,), turn, sides[1][0], [far], lent, span=span), "grp", 1)
+        for span in ((0, tables // 2), (tables // 2, tables))
+    ]
+    add(0, (4,), [far])
     return sides, sums
 
 
@@ -470,12 +480,11 @@
     live = jnp.arange(hot, dtype=jnp.int32)[None, :, None] < bag_lengths.T[:, None, :]
     place = bag_owner.transpose(1, 2, 0) * local_rows + bag_rows.transpose(1, 2, 0)
     place = jnp.where(live, place, -1)
-    sides, (own, lent) = count_and_pool(where, place, shard, local_rows, (down_w, up_w))
-    other = swap(lent, "grp", 1)
+    sides, (own, other) = count_and_pool(where, place, shard, local_rows, (down_w, up_w))
     d_pooled, dense_grad, grads = cross_layer(
         dense_part,
         own,
-        other,
+        *other,
         labels.astype(F32).reshape(1, samples),
         sample_weight.reshape(1, samples),
         down_w,

time: 93.3 us -> 92.9 us (level)
  waiting for transfers between devices: 15.3 us -> 14 us
    ppermute x10 -> x11, waiting for transfers between devices: 11.5 us -> 10.3 us  [swap(): return lax.ppermute(value, axis, [(i, i ^ stride) for i in range(size)])]
    ppermute x10 -> x11, starting transfers between devices: 6.96 us -> 7.54 us  [swap(): return lax.ppermute(value, axis, [(i, i ^ stride) for i in range(size)])]
    pallas_call x7 -> x8, Pallas kernels: 12.7 us -> 12.9 us  [pool(): pl.pallas_call(functools.partial(pool_kernel, [len(shard) for shard in sh...]
  transfers between devices with their start and end apart: 26 -> 27, of which waited for: 11 -> 11; matrix products, arithmetic and copies ran while one was open for 3% -> 3% of each run, Pallas kernels for 42% -> 43%
where the time goes in v5:
time: 92.9 us; the launch traced here: 92.7 us
  Pallas kernels  47.9 us (52%)
  starting transfers between devices  25.1 us (27%)
  waiting for transfers between devices  14 us (15%)
  local copies, waits for them, and re-layouts  2.2 us (2%)
  other arithmetic  2.2 us (2%)
  between operations  1.25 us (1%)
    pallas_call x5, Pallas kernels, spread(): pl.pallas_call(functools.partial(spread_kernel, turns, len(sides), at), o...  16.2 us
    pallas_call x8, Pallas kernels, pool(): pl.pallas_call(functools.partial(pool_kernel, [len(shard) for shard in sh...  12.9 us
    pallas_call x2, Pallas kernels, bag_counts(): pl.pallas_call(functools.partial(count_kernel, owners, local_rows, turns)...  12.6 us
    ppermute x11, waiting for transfers between devices, swap(): return lax.ppermute(value, axis, [(i, i ^ stride) for i in range(size)])  10.3 us
    ppermute x11, starting transfers between devices, swap(): return lax.ppermute(value, axis, [(i, i ^ stride) for i in range(size)])  7.54 us
    ppermute x3, starting transfers between devices, step(): lefts.append(lax.ppermute(a, 'emb', right))  6.14 us
    ppermute x4, starting transfers between devices, send(): lax.ppermute(to_right, 'emb', right)  5.47 us
    pallas_call x1, Pallas kernels, cross_layer(): pl.pallas_call(functools.partial(cross_kernel, tables), out_shape=(jax.Sh...  4.48 us
  transfers between devices with their start and end apart: 27, of which 11 were waited for; matrix products, arithmetic and copies ran while one was open for 3% of the time, Pallas kernels for 43%

profile of v5, /device:TPU:0, one launch (start us, length us, event | category | flops | bytes accessed | tf_op | source)
XLA Modules:
  0.0 92.7 jit_solution(7061011661211268928)
XLA Ops:
  0.7 1.0 %copy-done = bf16[2048,128]{1,0:T(8,128)(2,1)S(1)} copy-done((bf16[2048,128]{1,0:T(8,128)(2,1)S(1)}, bf16[2048,128]{1,0:T(8,128)(2,1)}, u32[]{:S(2)}) %copy-start) | copy-done | bytes 524312
  1.7 0.2 copy.16
  1.9 3.0 %collective-permute-start = (bf16[1024,128]{1,0:T(8,128)(2,1)S(1)}, bf16[1024,128]{1,0:T(8,128)(2,1)S(1)}, u32[]{:S(2)}, u32[]{:S(2)}) collective-permute-start(bf16[1024,128]{1,0:T(8,128)(2,1)S(1)} %bitcast.25), channel_id=1, source_target_pairs={{1,3},{3,5},{5,7},{7,6},{6,4},{4,2},{2,0},{0,1},{9,11},{11,13},{13... | collective-permute-start | bytes 786440 | tf_op jit(solution)/shard_map/ppermute | solution.py:377
  4.9 0.2 collective-permute-start.1
  5.0 0.7 multiply_bitcast_fusion
  5.8 0.9 fusion.8.place_ref
  6.8 0.1 pad_add_fusion.where_ref
  6.8 5.2 %bag_counts.2 = (bf16[1024,3328]{1,0:T(8,128)(2,1)S(1)}, f32[26,128]{1,0:T(8,128)S(1)}, bf16[3328,128]{1,0:T(8,128)(2,1)S(1)}) custom-call(s32[2]{0:T(128)S(1)} %pad_add_fusion.where_ref, s32[26,8,128]{2,1,0:T(8,128)S(1)} %fusion.8.place_ref), custom_call_target="tpu_custom_call" | custom-call | flops 5000000000 | tf_op jit(solution)/shard_map/bag_counts/pallas_call | solution.py:120
  12.1 0.6 collective-permute-done.1.refs_3_.refs_1_
  12.6 1.6 %collective-permute-start.3 = (bf16[1024,128]{1,0:T(8,128)(2,1)S(1)}, bf16[1024,128]{1,0:T(8,128)(2,1)S(1)}, u32[]{:S(2)}, u32[]{:S(2)}) collective-permute-start(bf16[1024,128]{1,0:T(8,128)(2,1)S(1)} %collective-permute-done.refs_4_.refs_2_), channel_id=1, source_target_pairs={{1,3},{3,5},{5,7},{7,6},{6,4},{4,2},{2,0},{0,1},{9,11},{11,13},{13... | collective-permute-start | bytes 786440 | tf_op jit(solution)/shard_map/ppermute | solution.py:377
  14.2 0.4 collective-permute-start.4
  14.7 7.5 %bag_counts.3 = (bf16[1024,3328]{1,0:T(8,128)(2,1)S(1)}, f32[26,128]{1,0:T(8,128)S(1)}, bf16[3328,128]{1,0:T(8,128)(2,1)S(1)}, f32[128,3328]{1,0:T(8,128)S(1)}) custom-call(s32[2]{0:T(128)S(1)} %pad_add_fusion.where_ref, s32[26,8,128]{2,1,0:T(8,128)S(1)} %collective-permute-done.2.place_ref, f32[26,128]{1,0:T(8,128)S(1)} %get-tuple-element.82.refs_0_.turn_ref, ...), custom_call_target="tpu_custom_call" | custom-call | flops 5000000000 | tf_op jit(solution)/shard_map/bag_counts/pallas_call | solution.py:120
  22.1 0.3 collective-permute-done.4.refs_0_
  22.4 1.6 %collective-permute-start.5 = (bf16[1024,128]{1,0:T(8,128)(2,1)S(1)}, bf16[1024,128]{1,0:T(8,128)(2,1)S(1)}, u32[]{:S(2)}, u32[]{:S(2)}) collective-permute-start(bf16[1024,128]{1,0:T(8,128)(2,1)S(1)} %collective-permute-done.3.refs_1_), channel_id=1, source_target_pairs={{1,3},{3,5},{5,7},{7,6},{6,4},{4,2},{2,0},{0,1},{9,11},{11,13},{13... | collective-permute-start | bytes 786440 | tf_op jit(solution)/shard_map/ppermute | solution.py:377
  24.0 0.4 collective-permute-start.6
  24.5 2.8 %pool.9.refs_2_ = f32[128,3328]{1,0:T(8,128)S(1)} custom-call(f32[26,128]{1,0:T(8,128)S(1)} %get-tuple-element.87.turn_ref, bf16[1024,3328]{1,0:T(8,128)(2,1)S(1)} %get-tuple-element.120.counts_ref.refs_2_.refs_5_, bf16[1024,128]{1,0:T(8,128)(2,1)S(1)} %bitcast.28, bf16[1024,128]{1,0:T(8,128)(2,1)S(1)} %collective-permute-done.1.refs_3_.refs_1_, ...), custom_call_target="tpu_custom_call" | custom-call | tf_op jit(solution)/shard_map/pool/pallas_call | solution.py:160
  27.3 0.3 copy-done.2
  27.5 1.9 %pool.10.refs_2_ = f32[128,3328]{1,0:T(8,128)S(1)} custom-call(f32[26,128]{1,0:T(8,128)S(1)} %get-tuple-element.87.turn_ref, bf16[1024,3328]{1,0:T(8,128)(2,1)S(1)} %get-tuple-element.120.counts_ref.refs_2_.refs_5_, bf16[1024,128]{1,0:T(8,128)(2,1)S(1)} %collective-permute-done.4.refs_0_, bf16[1024,128]{1,0:T(8,128)(2,1)S(1)} %collective-permute-done.3.refs_1_, ...), custom_call_target="tpu_custom_call" | custom-call | tf_op jit(solution)/shard_map/pool/pallas_call | solution.py:160
  29.5 1.9 %pool.8.refs_2_ = f32[128,3328]{1,0:T(8,128)S(1)} custom-call(f32[26,128]{1,0:T(8,128)S(1)} %get-tuple-element.82.refs_0_.turn_ref, bf16[1024,3328]{1,0:T(8,128)(2,1)S(1)} %get-tuple-element.117.refs_1_.counts_ref.refs_2_, bf16[1024,128]{1,0:T(8,128)(2,1)S(1)} %collective-permute-done.4.refs_0_, bf16[1024,128]{1,0:T(8,128)(2,1)S(1)} %collective-permute-done.3.refs_1_, ...), custom_call_target="tpu_custom_call" | custom-call | tf_op jit(solution)/shard_map/pool/pallas_call | solution.py:160
  31.5 1.6 %collective-permute-start.7 = (bf16[512,128]{1,0:T(8,128)(2,1)S(1)}, bf16[512,128]{1,0:T(8,128)(2,1)S(1)}, u32[]{:S(2)}, u32[]{:S(2)}) collective-permute-start(bf16[512,128]{1,0:T(8,128)(2,1)S(1)} %slice.57), channel_id=1, source_target_pairs={{1,3},{3,5},{5,7},{7,6},{6,4},{4,2},{2,0},{0,1},{9,11},{11,13},{13... | collective-permute-start | bytes 393224 | tf_op jit(solution)/shard_map/ppermute | solution.py:395
  33.1 0.4 collective-permute-start.8
  33.5 1.9 %pool.12.refs_2_ = f32[128,3328]{1,0:T(8,128)S(1)} custom-call(f32[26,128]{1,0:T(8,128)S(1)} %get-tuple-element.87.turn_ref, bf16[1024,3328]{1,0:T(8,128)(2,1)S(1)} %get-tuple-element.120.counts_ref.refs_2_.refs_5_, bf16[1024,128]{1,0:T(8,128)(2,1)S(1)} %collective-permute-done.6.refs_0_, bf16[1024,128]{1,0:T(8,128)(2,1)S(1)} %collective-permute-done.5.refs_1_, ...), custom_call_target="tpu_custom_call" | custom-call | tf_op jit(solution)/shard_map/pool/pallas_call | solution.py:160
  35.5 2.0 %pool.11.refs_2_ = f32[128,3328]{1,0:T(8,128)S(1)} custom-call(f32[26,128]{1,0:T(8,128)S(1)} %get-tuple-element.82.refs_0_.turn_ref, bf16[1024,3328]{1,0:T(8,128)(2,1)S(1)} %get-tuple-element.117.refs_1_.counts_ref.refs_2_, bf16[1024,128]{1,0:T(8,128)(2,1)S(1)} %collective-permute-done.6.refs_0_, bf16[1024,128]{1,0:T(8,128)(2,1)S(1)} %collective-permute-done.5.refs_1_, ...), custom_call_target="tpu_custom_call" | custom-call | tf_op jit(solution)/shard_map/pool/pallas_call | solution.py:160
  37.5 0.6 collective-permute-done.8.refs_1_
  38.1 0.6 pool.15
  38.8 0.7 pool.14
  39.5 0.6 collective-permute-start.9
  40.1 1.1 %pool.13.own_ref = f32[128,3328]{1,0:T(8,128)S(1)} custom-call(f32[26,128]{1,0:T(8,128)S(1)} %get-tuple-element.82.refs_0_.turn_ref, bf16[1024,3328]{1,0:T(8,128)(2,1)S(1)} %get-tuple-element.117.refs_1_.counts_ref.refs_2_, bf16[512,128]{1,0:T(8,128)(2,1)S(1)} %collective-permute-done.7.refs_0_, bf16[512,128]{1,0:T(8,128)(2,1)S(1)} %collective-permute-done.8.refs_1_, ...), custom_call_target="tpu_custom_call" | custom-call | tf_op jit(solution)/shard_map/pool/pallas_call | solution.py:160
  41.2 1.2 %collective-permute-done.9.first_ref = f32[128,1664]{1,0:T(8,128)S(1)} collective-permute-done((f32[128,1664]{1,0:T(8,128)S(1)}, f32[128,1664]{1,0:T(8,128)S(1)}, u32[]{:S(2)}, u32[]{:S(2)}) %collective-permute-start.9) | collective-permute-done | bytes 852000 | tf_op jit(solution)/shard_map/ppermute | solution.py:326
  42.4 4.5 %cross_layer.1 = (bf16[3328,128]{1,0:T(8,128)(2,1)S(1)}, bf16[128,128]{1,0:T(8,128)(2,1)}, f32[2,27,128]{2,1,0:T(8,128)S(1)}) custom-call(bf16[128,128]{1,0:T(8,128)(2,1)S(1)} %copy-done.3, f32[128,3328]{1,0:T(8,128)S(1)} %pool.13.own_ref, f32[128,1664]{1,0:T(8,128)S(1)} %collective-permute-done.9.first_ref, ...), custom_call_target="tpu_custom_call" | custom-call | flops 8000000000 | bytes 12000000 | tf_op jit(solution)/shard_map/cross_layer/pallas_call | solution.py:247
  46.9 0.2 collective-permute-start.11
  47.1 0.4 collective-permute-start.12
  47.5 2.1 %spread.5.refs_3_ = f32[1024,256]{1,0:T(8,128)S(1)} custom-call(bf16[3328,128]{1,0:T(8,128)(2,1)S(1)} %get-tuple-element.115.refs_0_, bf16[3328,128]{1,0:T(8,128)(2,1)S(1)} %get-tuple-element.116.refs_1_, bf16[1024,3328]{1,0:T(8,128)(2,1)S(1)} %get-tuple-element.117.refs_1_.counts_ref.refs_2_), custom_call_target="tpu_custom_call" | custom-call | tf_op jit(solution)/shard_map/spread/pallas_call | solution.py:287
  49.6 2.4 %spread.6 = f32[1024,256]{1,0:T(8,128)S(1)} custom-call(bf16[3328,128]{1,0:T(8,128)(2,1)S(1)} %get-tuple-element.118.refs_0_.refs_3_, bf16[3328,128]{1,0:T(8,128)(2,1)S(1)} %collective-permute-done.11.refs_1_.refs_4_, bf16[1024,3328]{1,0:T(8,128)(2,1)S(1)} %get-tuple-element.120.counts_ref.refs_2_.refs_5_, f32[1024,256]{1,0:T(8,128)S(1)} %spread.5.refs_3_), custom_call_target="tpu_custom_call" | custom-call | tf_op jit(solution)/shard_map/spread/pallas_call | solution.py:287
  52.1 1.6 %collective-permute-start.13 = (bf16[512,128]{1,0:T(8,128)(2,1)S(1)}, bf16[512,128]{1,0:T(8,128)(2,1)S(1)}, u32[]{:S(2)}, u32[]{:S(2)}) collective-permute-start(bf16[512,128]{1,0:T(8,128)(2,1)S(1)} %get-tuple-element.139), channel_id=1, source_target_pairs={{1,3},{3,5},{5,7},{7,6},{6,4},{4,2},{2,0},{0,1},{9,11},{11,13},{13... | collective-permute-start | bytes 393224 | tf_op jit(solution)/shard_map/ppermute | solution.py:433
  53.7 0.5 collective-permute-start.14
  54.1 3.9 %spread.7 = f32[1024,256]{1,0:T(8,128)S(1)} custom-call(bf16[3328,128]{1,0:T(8,128)(2,1)S(1)} %get-tuple-element.115.refs_0_, bf16[3328,128]{1,0:T(8,128)(2,1)S(1)} %get-tuple-element.116.refs_1_, bf16[1024,3328]{1,0:T(8,128)(2,1)S(1)} %get-tuple-element.117.refs_1_.counts_ref.refs_2_, bf16[3328,128]{1,0:T(8,128)(2,1)S(1)} %get-tuple-element.118.refs_0_.refs_3_, ...), custom_call_target="tpu_custom_call" | custom-call | tf_op jit(solution)/shard_map/spread/pallas_call | solution.py:287
  58.1 0.8 collective-permute-done.14
  58.9 0.1 fusion.4
  59.0 1.6 %collective-permute-start.15 = (bf16[1024,128]{1,0:T(8,128)(2,1)S(1)}, bf16[1024,128]{1,0:T(8,128)(2,1)S(1)}, u32[]{:S(2)}, u32[]{:S(2)}) collective-permute-start(bf16[1024,128]{1,0:T(8,128)(2,1)S(1)} %get-tuple-element.112), channel_id=1, source_target_pairs={{1,3},{3,5},{5,7},{7,6},{6,4},{4,2},{2,0},{0,1},{9,11},{11,13},{13... | collective-permute-start | bytes 786440 | tf_op jit(solution)/shard_map/ppermute | solution.py:433
  60.6 0.4 collective-permute-start.16
  61.1 1.5 %collective-permute-start.17 = (f32[2,27,128]{2,1,0:T(8,128)S(1)}, f32[2,27,128]{2,1,0:T(8,128)S(1)}, u32[]{:S(2)}, u32[]{:S(2)}) collective-permute-start(f32[2,27,128]{2,1,0:T(8,128)S(1)} %add.68), channel_id=1, source_target_pairs={{0,16},{8,24},{16,0},{24,8},{1,17},{9,25},{17,1},{25,9},{2,18},{10... | collective-permute-start | bytes 82952 | tf_op jit(solution)/shard_map/ppermute | solution.py:326
  62.6 3.9 %spread.8 = f32[1024,256]{1,0:T(8,128)S(1)} custom-call(bf16[3328,128]{1,0:T(8,128)(2,1)S(1)} %get-tuple-element.115.refs_0_, bf16[3328,128]{1,0:T(8,128)(2,1)S(1)} %get-tuple-element.116.refs_1_, bf16[1024,3328]{1,0:T(8,128)(2,1)S(1)} %get-tuple-element.117.refs_1_.counts_ref.refs_2_, bf16[3328,128]{1,0:T(8,128)(2,1)S(1)} %get-tuple-element.118.refs_0_.refs_3_, ...), custom_call_target="tpu_custom_call" | custom-call | tf_op jit(solution)/shard_map/spread/pallas_call | solution.py:287
  66.5 1.0 %collective-permute-done.16 = bf16[1024,128]{1,0:T(8,128)(2,1)S(1)} collective-permute-done((bf16[1024,128]{1,0:T(8,128)(2,1)S(1)}, bf16[1024,128]{1,0:T(8,128)(2,1)S(1)}, u32[]{:S(2)}, u32[]{:S(2)}) %collective-permute-start.16) | collective-permute-done | bytes 262176 | tf_op jit(solution)/shard_map/ppermute | solution.py:433
  67.5 0.1 fusion.2
  67.6 1.4 %collective-permute-start.18 = (bf16[1024,128]{1,0:T(8,128)(2,1)S(1)}, bf16[1024,128]{1,0:T(8,128)(2,1)S(1)}, u32[]{:S(2)}, u32[]{:S(2)}) collective-permute-start(bf16[1024,128]{1,0:T(8,128)(2,1)S(1)} %get-tuple-element.121), channel_id=1, source_target_pairs={{1,3},{3,5},{5,7},{7,6},{6,4},{4,2},{2,0},{0,1},{9,11},{11,13},{13... | collective-permute-start | bytes 786440 | tf_op jit(solution)/shard_map/ppermute | solution.py:433
  69.0 0.7 collective-permute-start.19
  69.7 1.4 %collective-permute-start.20 = (f32[2,27,128]{2,1,0:T(8,128)S(1)}, f32[2,27,128]{2,1,0:T(8,128)S(1)}, u32[]{:S(2)}, u32[]{:S(2)}) collective-permute-start(f32[2,27,128]{2,1,0:T(8,128)S(1)} %add.73), channel_id=1, source_target_pairs={{0,1},{1,0},{2,3},{3,2},{4,5},{5,4},{6,7},{7,6},{8,9},{9,8},{10,11... | collective-permute-start | bytes 82952 | tf_op jit(solution)/shard_map/ppermute | solution.py:326
  71.1 3.9 %spread.9 = f32[1024,256]{1,0:T(8,128)S(1)} custom-call(bf16[3328,128]{1,0:T(8,128)(2,1)S(1)} %get-tuple-element.115.refs_0_, bf16[3328,128]{1,0:T(8,128)(2,1)S(1)} %get-tuple-element.116.refs_1_, bf16[1024,3328]{1,0:T(8,128)(2,1)S(1)} %get-tuple-element.117.refs_1_.counts_ref.refs_2_, bf16[3328,128]{1,0:T(8,128)(2,1)S(1)} %get-tuple-element.118.refs_0_.refs_3_, ...), custom_call_target="tpu_custom_call" | custom-call | tf_op jit(solution)/shard_map/spread/pallas_call | solution.py:287
  75.0 0.8 collective-permute-done.20
  75.8 0.1 fusion
  75.9 0.8 collective-permute-start.21
  76.7 1.2 %collective-permute-start.22 = (bf16[1024,128]{1,0:T(8,128)(2,1)S(1)}, bf16[1024,128]{1,0:T(8,128)(2,1)S(1)}, u32[]{:S(2)}, u32[]{:S(2)}) collective-permute-start(bf16[1024,128]{1,0:T(8,128)(2,1)S(1)} %get-tuple-element.125), channel_id=1, source_target_pairs={{3,1},{5,3},{7,5},{6,7},{4,6},{2,4},{0,2},{1,0},{11,9},{13,11},{15... | collective-permute-start | bytes 786440 | tf_op jit(solution)/shard_map/ppermute | solution.py:433
  78.0 0.4 collective-permute-start.23
  78.4 4.3 %collective-permute-done.23 = f32[2,27,128]{2,1,0:T(8,128)S(1)} collective-permute-done((f32[2,27,128]{2,1,0:T(8,128)S(1)}, f32[2,27,128]{2,1,0:T(8,128)S(1)}, u32[]{:S(2)}, u32[]{:S(2)}) %collective-permute-start.23) | collective-permute-done | bytes 27680 | tf_op jit(solution)/shard_map/ppermute | solution.py:326
  82.7 0.4 collective-permute-done.22
  83.1 0.1 fusion.7
  83.2 1.6 %collective-permute-start.24 = (bf16[1024,128]{1,0:T(8,128)(2,1)S(1)}, bf16[1024,128]{1,0:T(8,128)(2,1)S(1)}, u32[]{:S(2)}, u32[]{:S(2)}) collective-permute-start(bf16[1024,128]{1,0:T(8,128)(2,1)S(1)} %fusion.7), channel_id=1, source_target_pairs={{0,16},{8,24},{16,0},{24,8},{1,17},{9,25},{17,1},{25,9},{2,18},{10... | collective-permute-start | bytes 786440 | tf_op jit(solution)/shard_map/ppermute | solution.py:326
  84.8 1.3 %collective-permute-start.25 = (f32[2,27,128]{2,1,0:T(8,128)S(1)}, f32[2,27,128]{2,1,0:T(8,128)S(1)}, u32[]{:S(2)}, u32[]{:S(2)}) collective-permute-start(f32[2,27,128]{2,1,0:T(8,128)S(1)} %add.79), channel_id=1, source_target_pairs={{0,4},{1,5},{2,6},{3,7},{4,0},{5,1},{6,2},{7,3},{8,12},{9,13},{10,... | collective-permute-start | bytes 82952 | tf_op jit(solution)/shard_map/ppermute | solution.py:326
  86.1 3.5 %collective-permute-done.25 = f32[2,27,128]{2,1,0:T(8,128)S(1)} collective-permute-done((f32[2,27,128]{2,1,0:T(8,128)S(1)}, f32[2,27,128]{2,1,0:T(8,128)S(1)}, u32[]{:S(2)}, u32[]{:S(2)}) %collective-permute-start.25) | collective-permute-done | bytes 27680 | tf_op jit(solution)/shard_map/ppermute | solution.py:326
  89.8 0.8 place_half.2.refs_0_
  90.6 0.6 slice_bitcast_fusion
  91.2 0.5 collective-permute-done.26.part_ref
  91.7 0.8 place_half.3
  (46 shorter events, 0.6 us)
Async XLA Ops:
  0.6 1.0 %copy-start = (bf16[2048,128]{1,0:T(8,128)(2,1)S(1)}, bf16[2048,128]{1,0:T(8,128)(2,1)}, u32[]{:S(2)}) copy-start(bf16[2048,128]{1,0:T(8,128)(2,1)} %param.11) | copy-start | bytes 1572868
  1.9 10.2 %collective-permute-start = (bf16[1024,128]{1,0:T(8,128)(2,1)S(1)}, bf16[1024,128]{1,0:T(8,128)(2,1)S(1)}, u32[]{:S(2)}, u32[]{:S(2)}) collective-permute-start(bf16[1024,128]{1,0:T(8,128)(2,1)S(1)} %bitcast.25), channel_id=1, source_target_pairs={{1,3},{3,5},{5,7},{7,6},{6,4},{4,2},{2,0},{0,1},{9,11},{11,13},{13... | collective-permute-start | bytes 786440 | tf_op jit(solution)/shard_map/ppermute | solution.py:377
  4.9 7.8 %collective-permute-start.1 = (bf16[1024,128]{1,0:T(8,128)(2,1)S(1)}, bf16[1024,128]{1,0:T(8,128)(2,1)S(1)}, u32[]{:S(2)}, u32[]{:S(2)}) collective-permute-start(bf16[1024,128]{1,0:T(8,128)(2,1)S(1)} %bitcast.26), channel_id=1, source_target_pairs={{3,1},{5,3},{7,5},{6,7},{4,6},{2,4},{0,2},{1,0},{11,9},{13,11},{15... | collective-permute-start | bytes 786440 | tf_op jit(solution)/shard_map/ppermute | solution.py:378
  6.7 5.4 %collective-permute-start.2 = (s32[26,8,128]{2,1,0:T(8,128)S(1)}, s32[26,8,128]{2,1,0:T(8,128)S(1)}, u32[]{:S(2)}, u32[]{:S(2)}) collective-permute-start(s32[26,8,128]{2,1,0:T(8,128)S(1)} %fusion.8.place_ref), channel_id=1, source_target_pairs={{0,8},{8,0},{16,24},{24,16},{1,9},{9,1},{17,25},{25,17},{2,10},{10... | collective-permute-start | bytes 319496 | tf_op jit(solution)/shard_map/ppermute | solution.py:326
  12.6 9.5 %collective-permute-start.3 = (bf16[1024,128]{1,0:T(8,128)(2,1)S(1)}, bf16[1024,128]{1,0:T(8,128)(2,1)S(1)}, u32[]{:S(2)}, u32[]{:S(2)}) collective-permute-start(bf16[1024,128]{1,0:T(8,128)(2,1)S(1)} %collective-permute-done.refs_4_.refs_2_), channel_id=1, source_target_pairs={{1,3},{3,5},{5,7},{7,6},{6,4},{4,2},{2,0},{0,1},{9,11},{11,13},{13... | collective-permute-start | bytes 786440 | tf_op jit(solution)/shard_map/ppermute | solution.py:377
  14.2 8.2 %collective-permute-start.4 = (bf16[1024,128]{1,0:T(8,128)(2,1)S(1)}, bf16[1024,128]{1,0:T(8,128)(2,1)S(1)}, u32[]{:S(2)}, u32[]{:S(2)}) collective-permute-start(bf16[1024,128]{1,0:T(8,128)(2,1)S(1)} %collective-permute-done.1.refs_3_.refs_1_), channel_id=1, source_target_pairs={{3,1},{5,3},{7,5},{6,7},{4,6},{2,4},{0,2},{1,0},{11,9},{13,11},{15... | collective-permute-start | bytes 786440 | tf_op jit(solution)/shard_map/ppermute | solution.py:378
  22.4 9.0 %collective-permute-start.5 = (bf16[1024,128]{1,0:T(8,128)(2,1)S(1)}, bf16[1024,128]{1,0:T(8,128)(2,1)S(1)}, u32[]{:S(2)}, u32[]{:S(2)}) collective-permute-start(bf16[1024,128]{1,0:T(8,128)(2,1)S(1)} %collective-permute-done.3.refs_1_), channel_id=1, source_target_pairs={{1,3},{3,5},{5,7},{7,6},{6,4},{4,2},{2,0},{0,1},{9,11},{11,13},{13... | collective-permute-start | bytes 786440 | tf_op jit(solution)/shard_map/ppermute | solution.py:377
  24.0 7.4 %collective-permute-start.6 = (bf16[1024,128]{1,0:T(8,128)(2,1)S(1)}, bf16[1024,128]{1,0:T(8,128)(2,1)S(1)}, u32[]{:S(2)}, u32[]{:S(2)}) collective-permute-start(bf16[1024,128]{1,0:T(8,128)(2,1)S(1)} %collective-permute-done.4.refs_0_), channel_id=1, source_target_pairs={{3,1},{5,3},{7,5},{6,7},{4,6},{2,4},{0,2},{1,0},{11,9},{13,11},{15... | collective-permute-start | bytes 786440 | tf_op jit(solution)/shard_map/ppermute | solution.py:378
  24.4 2.8 %copy-start.1 = (bf16[3456,512]{1,0:T(8,128)(2,1)S(1)}, bf16[3456,512]{1,0:T(8,128)(2,1)}, u32[]{:S(2)}) copy-start(bf16[3456,512]{1,0:T(8,128)(2,1)} %down_ref.1) | copy-start | bytes 10616836
  24.5 3.1 %copy-start.2 = (bf16[512,3456]{1,0:T(8,128)(2,1)S(1)}, bf16[512,3456]{1,0:T(8,128)(2,1)}, u32[]{:S(2)}) copy-start(bf16[512,3456]{1,0:T(8,128)(2,1)} %up_ref.1) | copy-start | bytes 10616836
  31.5 6.0 %collective-permute-start.7 = (bf16[512,128]{1,0:T(8,128)(2,1)S(1)}, bf16[512,128]{1,0:T(8,128)(2,1)S(1)}, u32[]{:S(2)}, u32[]{:S(2)}) collective-permute-start(bf16[512,128]{1,0:T(8,128)(2,1)S(1)} %slice.57), channel_id=1, source_target_pairs={{1,3},{3,5},{5,7},{7,6},{6,4},{4,2},{2,0},{0,1},{9,11},{11,13},{13... | collective-permute-start | bytes 393224 | tf_op jit(solution)/shard_map/ppermute | solution.py:395
  33.1 5.0 %collective-permute-start.8 = (bf16[512,128]{1,0:T(8,128)(2,1)S(1)}, bf16[512,128]{1,0:T(8,128)(2,1)S(1)}, u32[]{:S(2)}, u32[]{:S(2)}) collective-permute-start(bf16[512,128]{1,0:T(8,128)(2,1)S(1)} %slice.58), channel_id=1, source_target_pairs={{3,1},{5,3},{7,5},{6,7},{4,6},{2,4},{0,2},{1,0},{11,9},{13,11},{15... | collective-permute-start | bytes 393224 | tf_op jit(solution)/shard_map/ppermute | solution.py:395
  38.7 1.3 %copy-start.7 = (s32[128]{0:T(128)S(1)}, s32[128]{0:T(128)}, u32[]{:S(2)}) copy-start(s32[128]{0:T(128)} %param.16) | copy-start | bytes 1540
  38.7 2.4 %collective-permute-start.10 = (f32[128,1664]{1,0:T(8,128)S(1)}, f32[128,1664]{1,0:T(8,128)S(1)}, u32[]{:S(2)}, u32[]{:S(2)}) collective-permute-start(f32[128,1664]{1,0:T(8,128)S(1)} %pool.15), channel_id=1, source_target_pairs={{0,8},{8,0},{16,24},{24,16},{1,9},{9,1},{17,25},{25,17},{2,10},{10... | collective-permute-start | bytes 2555912 | tf_op jit(solution)/shard_map/ppermute | solution.py:326
  39.5 2.9 %collective-permute-start.9 = (f32[128,1664]{1,0:T(8,128)S(1)}, f32[128,1664]{1,0:T(8,128)S(1)}, u32[]{:S(2)}, u32[]{:S(2)}) collective-permute-start(f32[128,1664]{1,0:T(8,128)S(1)} %pool.14), channel_id=1, source_target_pairs={{0,8},{8,0},{16,24},{24,16},{1,9},{9,1},{17,25},{25,17},{2,10},{10... | collective-permute-start | bytes 2555912 | tf_op jit(solution)/shard_map/ppermute | solution.py:326
  40.0 2.4 %copy-start.3 = (bf16[128,128]{1,0:T(8,128)(2,1)S(1)}, bf16[128,128]{1,0:T(8,128)(2,1)}, u32[]{:S(2)}) copy-start(bf16[128,128]{1,0:T(8,128)(2,1)} %dense_ref.1) | copy-start | bytes 98308
  40.0 2.4 %copy-start.4 = (f32[3456]{0:T(1024)S(1)}, f32[3456]{0:T(1024)}, u32[]{:S(2)}) copy-start(f32[3456]{0:T(1024)} %param.20) | copy-start | bytes 41476
  40.0 2.4 %copy-start.5 = (f32[3456]{0:T(1024)S(1)}, f32[3456]{0:T(1024)}, u32[]{:S(2)}) copy-start(f32[3456]{0:T(1024)} %param.21) | copy-start | bytes 41476
  40.1 2.4 %copy-start.6 = (f32[128]{0:T(128)S(1)}, f32[128]{0:T(128)}, u32[]{:S(2)}) copy-start(f32[128]{0:T(128)} %param.17) | copy-start | bytes 1540
  46.9 2.7 %collective-permute-start.11 = (bf16[3328,128]{1,0:T(8,128)(2,1)S(1)}, bf16[3328,128]{1,0:T(8,128)(2,1)S(1)}, u32[]{:S(2)}, u32[]{:S(2)}) collective-permute-start(bf16[3328,128]{1,0:T(8,128)(2,1)S(1)} %get-tuple-element.116.refs_1_), channel_id=1, source_target_pairs={{0,8},{8,0},{16,24},{24,16},{1,9},{9,1},{17,25},{25,17},{2,10},{10... | collective-permute-start | bytes 2555912 | tf_op jit(solution)/shard_map/ppermute | solution.py:326
  47.1 2.5 %collective-permute-start.12 = (f32[2,27,128]{2,1,0:T(8,128)S(1)}, f32[2,27,128]{2,1,0:T(8,128)S(1)}, u32[]{:S(2)}, u32[]{:S(2)}) collective-permute-start(f32[2,27,128]{2,1,0:T(8,128)S(1)} %get-tuple-element.97), channel_id=1, source_target_pairs={{0,8},{8,0},{16,24},{24,16},{1,9},{9,1},{17,25},{25,17},{2,10},{10... | collective-permute-start | bytes 82952 | tf_op jit(solution)/shard_map/ppermute | solution.py:326
  52.1 6.0 %collective-permute-start.13 = (bf16[512,128]{1,0:T(8,128)(2,1)S(1)}, bf16[512,128]{1,0:T(8,128)(2,1)S(1)}, u32[]{:S(2)}, u32[]{:S(2)}) collective-permute-start(bf16[512,128]{1,0:T(8,128)(2,1)S(1)} %get-tuple-element.139), channel_id=1, source_target_pairs={{1,3},{3,5},{5,7},{7,6},{6,4},{4,2},{2,0},{0,1},{9,11},{11,13},{13... | collective-permute-start | bytes 393224 | tf_op jit(solution)/shard_map/ppermute | solution.py:433
  53.7 5.3 %collective-permute-start.14 = (bf16[512,128]{1,0:T(8,128)(2,1)S(1)}, bf16[512,128]{1,0:T(8,128)(2,1)S(1)}, u32[]{:S(2)}, u32[]{:S(2)}) collective-permute-start(bf16[512,128]{1,0:T(8,128)(2,1)S(1)} %get-tuple-element.138), channel_id=1, source_target_pairs={{3,1},{5,3},{7,5},{6,7},{4,6},{2,4},{0,2},{1,0},{11,9},{13,11},{15... | collective-permute-start | bytes 393224 | tf_op jit(solution)/shard_map/ppermute | solution.py:433
  59.0 7.5 %collective-permute-start.15 = (bf16[1024,128]{1,0:T(8,128)(2,1)S(1)}, bf16[1024,128]{1,0:T(8,128)(2,1)S(1)}, u32[]{:S(2)}, u32[]{:S(2)}) collective-permute-start(bf16[1024,128]{1,0:T(8,128)(2,1)S(1)} %get-tuple-element.112), channel_id=1, source_target_pairs={{1,3},{3,5},{5,7},{7,6},{6,4},{4,2},{2,0},{0,1},{9,11},{11,13},{13... | collective-permute-start | bytes 786440 | tf_op jit(solution)/shard_map/ppermute | solution.py:433
  60.6 6.9 %collective-permute-start.16 = (bf16[1024,128]{1,0:T(8,128)(2,1)S(1)}, bf16[1024,128]{1,0:T(8,128)(2,1)S(1)}, u32[]{:S(2)}, u32[]{:S(2)}) collective-permute-start(bf16[1024,128]{1,0:T(8,128)(2,1)S(1)} %get-tuple-element.113), channel_id=1, source_target_pairs={{3,1},{5,3},{7,5},{6,7},{4,6},{2,4},{0,2},{1,0},{11,9},{13,11},{15... | collective-permute-start | bytes 786440 | tf_op jit(solution)/shard_map/ppermute | solution.py:433
  61.1 5.4 %collective-permute-start.17 = (f32[2,27,128]{2,1,0:T(8,128)S(1)}, f32[2,27,128]{2,1,0:T(8,128)S(1)}, u32[]{:S(2)}, u32[]{:S(2)}) collective-permute-start(f32[2,27,128]{2,1,0:T(8,128)S(1)} %add.68), channel_id=1, source_target_pairs={{0,16},{8,24},{16,0},{24,8},{1,17},{9,25},{17,1},{25,9},{2,18},{10... | collective-permute-start | bytes 82952 | tf_op jit(solution)/shard_map/ppermute | solution.py:326
  67.6 8.1 %collective-permute-start.18 = (bf16[1024,128]{1,0:T(8,128)(2,1)S(1)}, bf16[1024,128]{1,0:T(8,128)(2,1)S(1)}, u32[]{:S(2)}, u32[]{:S(2)}) collective-permute-start(bf16[1024,128]{1,0:T(8,128)(2,1)S(1)} %get-tuple-element.121), channel_id=1, source_target_pairs={{1,3},{3,5},{5,7},{7,6},{6,4},{4,2},{2,0},{0,1},{9,11},{11,13},{13... | collective-permute-start | bytes 786440 | tf_op jit(solution)/shard_map/ppermute | solution.py:433
  69.0 6.7 %collective-permute-start.19 = (bf16[1024,128]{1,0:T(8,128)(2,1)S(1)}, bf16[1024,128]{1,0:T(8,128)(2,1)S(1)}, u32[]{:S(2)}, u32[]{:S(2)}) collective-permute-start(bf16[1024,128]{1,0:T(8,128)(2,1)S(1)} %get-tuple-element.122), channel_id=1, source_target_pairs={{3,1},{5,3},{7,5},{6,7},{4,6},{2,4},{0,2},{1,0},{11,9},{13,11},{15... | collective-permute-start | bytes 786440 | tf_op jit(solution)/shard_map/ppermute | solution.py:433
  69.7 6.1 %collective-permute-start.20 = (f32[2,27,128]{2,1,0:T(8,128)S(1)}, f32[2,27,128]{2,1,0:T(8,128)S(1)}, u32[]{:S(2)}, u32[]{:S(2)}) collective-permute-start(f32[2,27,128]{2,1,0:T(8,128)S(1)} %add.73), channel_id=1, source_target_pairs={{0,1},{1,0},{2,3},{3,2},{4,5},{5,4},{6,7},{7,6},{8,9},{9,8},{10,11... | collective-permute-start | bytes 82952 | tf_op jit(solution)/shard_map/ppermute | solution.py:326
  75.9 6.8 %collective-permute-start.21 = (bf16[1024,128]{1,0:T(8,128)(2,1)S(1)}, bf16[1024,128]{1,0:T(8,128)(2,1)S(1)}, u32[]{:S(2)}, u32[]{:S(2)}) collective-permute-start(bf16[1024,128]{1,0:T(8,128)(2,1)S(1)} %get-tuple-element.124), channel_id=1, source_target_pairs={{1,3},{3,5},{5,7},{7,6},{6,4},{4,2},{2,0},{0,1},{9,11},{11,13},{13... | collective-permute-start | bytes 786440 | tf_op jit(solution)/shard_map/ppermute | solution.py:433
  76.7 6.4 %collective-permute-start.22 = (bf16[1024,128]{1,0:T(8,128)(2,1)S(1)}, bf16[1024,128]{1,0:T(8,128)(2,1)S(1)}, u32[]{:S(2)}, u32[]{:S(2)}) collective-permute-start(bf16[1024,128]{1,0:T(8,128)(2,1)S(1)} %get-tuple-element.125), channel_id=1, source_target_pairs={{3,1},{5,3},{7,5},{6,7},{4,6},{2,4},{0,2},{1,0},{11,9},{13,11},{15... | collective-permute-start | bytes 786440 | tf_op jit(solution)/shard_map/ppermute | solution.py:433
  78.0 4.7 %collective-permute-start.23 = (f32[2,27,128]{2,1,0:T(8,128)S(1)}, f32[2,27,128]{2,1,0:T(8,128)S(1)}, u32[]{:S(2)}, u32[]{:S(2)}) collective-permute-start(f32[2,27,128]{2,1,0:T(8,128)S(1)} %add.76), channel_id=1, source_target_pairs={{0,2},{1,3},{2,0},{3,1},{4,6},{5,7},{6,4},{7,5},{8,10},{9,11},{10,... | collective-permute-start | bytes 82952 | tf_op jit(solution)/shard_map/ppermute | solution.py:326
  83.2 6.4 %collective-permute-start.24 = (bf16[1024,128]{1,0:T(8,128)(2,1)S(1)}, bf16[1024,128]{1,0:T(8,128)(2,1)S(1)}, u32[]{:S(2)}, u32[]{:S(2)}) collective-permute-start(bf16[1024,128]{1,0:T(8,128)(2,1)S(1)} %fusion.7), channel_id=1, source_target_pairs={{0,16},{8,24},{16,0},{24,8},{1,17},{9,25},{17,1},{25,9},{2,18},{10... | collective-permute-start | bytes 786440 | tf_op jit(solution)/shard_map/ppermute | solution.py:326
  84.8 4.8 %collective-permute-start.25 = (f32[2,27,128]{2,1,0:T(8,128)S(1)}, f32[2,27,128]{2,1,0:T(8,128)S(1)}, u32[]{:S(2)}, u32[]{:S(2)}) collective-permute-start(f32[2,27,128]{2,1,0:T(8,128)S(1)} %add.79), channel_id=1, source_target_pairs={{0,4},{1,5},{2,6},{3,7},{4,0},{5,1},{6,2},{7,3},{8,12},{9,13},{10,... | collective-permute-start | bytes 82952 | tf_op jit(solution)/shard_map/ppermute | solution.py:326
  89.7 2.0 %collective-permute-start.26 = (f32[1024,128]{1,0:T(8,128)S(1)}, f32[1024,128]{1,0:T(8,128)S(1)}, u32[]{:S(2)}, u32[]{:S(2)}) collective-permute-start(f32[1024,128]{1,0:T(8,128)S(1)} %convert_add_fusion.part_ref), channel_id=1, source_target_pairs={{0,8},{8,0},{16,24},{24,16},{1,9},{9,1},{17,25},{25,17},{2,10},{10... | collective-permute-start | bytes 1572872 | tf_op jit(solution)/shard_map/ppermute | solution.py:326

commit v6 on v5

--- a/solution.py
+++ b/solution.py
@@ -10,6 +10,7 @@
 BF16 = jnp.bfloat16
 F32 = jnp.float32
 LANES = 128
+RING = ("grp", "emb")
 CHUNK = 32
 VMEM_BYTES = 16 * 1024 * 1024
 
@@ -59,7 +60,8 @@
         place = place_ref[at]
         owner = place[0:1, :] >> shift
         if owners == 8:
-            turn = (ring_place(owner) - ring_place(index) + owners) & (owners - 1)
+            turn = ring_place(owner) - ring_place(index)
+            turn = jnp.where(half == 0, turn, -turn) & (owners - 1)
         else:
             turn = owner
         turn = turn.astype(F32)
@@ -346,7 +348,13 @@
 
 def ring_turns(owners):
     order = ring_order(owners)
-    right = [(order[i], order[(i + 1) % owners]) for i in range(owners)]
+    right = []
+    for group in range(lax.axis_size("grp")):
+        for i in range(owners):
+            here, there = order[i], order[(i + 1) % owners]
+            if group % 2 == 1:
+                here, there = there, here
+            right.append((group * owners + here, group * owners + there))
     return right, [(there, here) for here, there in right]
 
 
@@ -374,8 +382,8 @@
     def step(beside):
         before = lefts[-1], rights[-1], beside
         a, b, beside = before if beside is None else lax.optimization_barrier(before)
-        lefts.append(lax.ppermute(a, "emb", right))
-        rights.append(lax.ppermute(b, "emb", left))
+        lefts.append(lax.ppermute(a, RING, right))
+        rights.append(lax.ppermute(b, RING, left))
         return beside
 
     step(None)
@@ -392,7 +400,7 @@
     a, b, sums[0], sums[1] = lax.optimization_barrier(
         (lefts[3][:middle], rights[3][middle:], sums[0], sums[1])
     )
-    far = [lax.ppermute(a, "emb", right), lax.ppermute(b, "emb", left)]
+    far = [lax.ppermute(a, RING, right), lax.ppermute(b, RING, left)]
     for side in (1, 0):
         add(side, (3, 5), [[rights[3]], [lefts[3]]])
     sums[0], sums[1] = lax.optimization_barrier((sums[0], sums[1]))
@@ -430,7 +438,7 @@
         return grads + swap(grads, *exchanges.pop(0))
 
     def send(to_right, to_left):
-        return lax.ppermute(to_right, "emb", right), lax.ppermute(to_left, "emb", left)
+        return lax.ppermute(to_right, RING, right), lax.ppermute(to_left, RING, left)
 
     def messages(part, went_right, went_left):
         to_right, to_left = part[:, :width], part[:, width:]

time: 92.9 us -> 97.3 us (1.047)
  waiting for transfers between devices: 14 us -> 17.7 us
    ppermute x11, waiting for transfers between devices: 10.3 us -> 15 us  [swap(): return lax.ppermute(value, axis, [(i, i ^ stride) for i in range(size)])]
    ppermute x16, waiting for transfers between devices: 3.73 us -> 2.74 us  [the longest x4 1.77 us: send(): lax.ppermute(to_right, RING, right)]
  transfers between devices with their start and end apart: 27 -> 27, of which waited for: 11 -> 11; matrix products, arithmetic and copies ran while one was open for 3% -> 2% of each run, Pallas kernels for 43% -> 41%
where the time goes in v6:
time: 97.3 us; the launch traced here: 97 us
  Pallas kernels  47.9 us (49%)
  starting transfers between devices  25.8 us (27%)
  waiting for transfers between devices  17.7 us (18%)
  local copies, waits for them, and re-layouts  2.2 us (2%)
  other arithmetic  2.2 us (2%)
  between operations  1.24 us (1%)
    pallas_call x5, Pallas kernels, spread(): pl.pallas_call(functools.partial(spread_kernel, turns, len(sides), at), o...  16.2 us
    ppermute x11, waiting for transfers between devices, swap(): return lax.ppermute(value, axis, [(i, i ^ stride) for i in range(size)])  15 us
    pallas_call x8, Pallas kernels, pool(): pl.pallas_call(functools.partial(pool_kernel, [len(shard) for shard in sh...  12.9 us
    pallas_call x2, Pallas kernels, bag_counts(): pl.pallas_call(functools.partial(count_kernel, owners, local_rows, turns)...  12.7 us
    ppermute x11, starting transfers between devices, swap(): return lax.ppermute(value, axis, [(i, i ^ stride) for i in range(size)])  7.9 us
    ppermute x3, starting transfers between devices, step(): lefts.append(lax.ppermute(a, RING, right))  6.85 us
    ppermute x4, starting transfers between devices, send(): lax.ppermute(to_right, RING, right)  6.18 us
    pallas_call x1, Pallas kernels, cross_layer(): pl.pallas_call(functools.partial(cross_kernel, tables), out_shape=(jax.Sh...  4.47 us
  transfers between devices with their start and end apart: 27, of which 11 were waited for; matrix products, arithmetic and copies ran while one was open for 2% of the time, Pallas kernels for 41%

profile of v6, /device:TPU:0, one launch (start us, length us, event | category | flops | bytes accessed | tf_op | source)
XLA Modules:
  0.0 97.0 jit_solution(9840384636851890978)
XLA Ops:
  0.7 1.0 %copy-done = bf16[2048,128]{1,0:T(8,128)(2,1)S(1)} copy-done((bf16[2048,128]{1,0:T(8,128)(2,1)S(1)}, bf16[2048,128]{1,0:T(8,128)(2,1)}, u32[]{:S(2)}) %copy-start) | copy-done | bytes 524312
  1.7 0.2 copy.16
  1.9 3.0 %collective-permute-start = (bf16[1024,128]{1,0:T(8,128)(2,1)S(1)}, bf16[1024,128]{1,0:T(8,128)(2,1)S(1)}, u32[]{:S(2)}, u32[]{:S(2)}) collective-permute-start(bf16[1024,128]{1,0:T(8,128)(2,1)S(1)} %bitcast.25), channel_id=1, source_target_pairs={{1,3},{3,5},{5,7},{7,6},{6,4},{4,2},{2,0},{0,1},{11,9},{13,11},{15... | collective-permute-start | bytes 786440 | tf_op jit(solution)/shard_map/ppermute | solution.py:385
  4.9 0.2 collective-permute-start.1
  5.0 0.7 multiply_bitcast_fusion
  5.8 0.9 fusion.8.place_ref
  6.8 0.1 pad_add_fusion.where_ref
  6.8 5.2 %bag_counts.2 = (bf16[1024,3328]{1,0:T(8,128)(2,1)S(1)}, f32[26,128]{1,0:T(8,128)S(1)}, bf16[3328,128]{1,0:T(8,128)(2,1)S(1)}) custom-call(s32[2]{0:T(128)S(1)} %pad_add_fusion.where_ref, s32[26,8,128]{2,1,0:T(8,128)S(1)} %fusion.8.place_ref), custom_call_target="tpu_custom_call" | custom-call | flops 5000000000 | tf_op jit(solution)/shard_map/bag_counts/pallas_call | solution.py:122
  12.1 1.9 %collective-permute-start.3 = (bf16[1024,128]{1,0:T(8,128)(2,1)S(1)}, bf16[1024,128]{1,0:T(8,128)(2,1)S(1)}, u32[]{:S(2)}, u32[]{:S(2)}) collective-permute-start(bf16[1024,128]{1,0:T(8,128)(2,1)S(1)} %collective-permute-done.refs_4_.refs_2_), channel_id=1, source_target_pairs={{1,3},{3,5},{5,7},{7,6},{6,4},{4,2},{2,0},{0,1},{11,9},{13,11},{15... | collective-permute-start | bytes 786440 | tf_op jit(solution)/shard_map/ppermute | solution.py:385
  14.0 0.2 collective-permute-start.4
  14.2 7.5 %bag_counts.3 = (bf16[1024,3328]{1,0:T(8,128)(2,1)S(1)}, f32[26,128]{1,0:T(8,128)S(1)}, bf16[3328,128]{1,0:T(8,128)(2,1)S(1)}, f32[128,3328]{1,0:T(8,128)S(1)}) custom-call(s32[2]{0:T(128)S(1)} %pad_add_fusion.where_ref, s32[26,8,128]{2,1,0:T(8,128)S(1)} %collective-permute-done.2.place_ref, f32[26,128]{1,0:T(8,128)S(1)} %get-tuple-element.82.refs_0_.turn_ref, ...), custom_call_target="tpu_custom_call" | custom-call | flops 5000000000 | tf_op jit(solution)/shard_map/bag_counts/pallas_call | solution.py:122
  21.7 1.9 %collective-permute-start.5 = (bf16[1024,128]{1,0:T(8,128)(2,1)S(1)}, bf16[1024,128]{1,0:T(8,128)(2,1)S(1)}, u32[]{:S(2)}, u32[]{:S(2)}) collective-permute-start(bf16[1024,128]{1,0:T(8,128)(2,1)S(1)} %collective-permute-done.3.refs_1_), channel_id=1, source_target_pairs={{1,3},{3,5},{5,7},{7,6},{6,4},{4,2},{2,0},{0,1},{11,9},{13,11},{15... | collective-permute-start | bytes 786440 | tf_op jit(solution)/shard_map/ppermute | solution.py:385
  23.6 0.2 collective-permute-start.6
  23.8 2.8 %pool.9.refs_2_ = f32[128,3328]{1,0:T(8,128)S(1)} custom-call(f32[26,128]{1,0:T(8,128)S(1)} %get-tuple-element.87.turn_ref, bf16[1024,3328]{1,0:T(8,128)(2,1)S(1)} %get-tuple-element.120.counts_ref.refs_2_.refs_5_, bf16[1024,128]{1,0:T(8,128)(2,1)S(1)} %bitcast.28, bf16[1024,128]{1,0:T(8,128)(2,1)S(1)} %collective-permute-done.1.refs_3_.refs_1_, ...), custom_call_target="tpu_custom_call" | custom-call | tf_op jit(solution)/shard_map/pool/pallas_call | solution.py:162
  26.6 0.3 copy-done.2
  26.9 1.9 %pool.10.refs_2_ = f32[128,3328]{1,0:T(8,128)S(1)} custom-call(f32[26,128]{1,0:T(8,128)S(1)} %get-tuple-element.87.turn_ref, bf16[1024,3328]{1,0:T(8,128)(2,1)S(1)} %get-tuple-element.120.counts_ref.refs_2_.refs_5_, bf16[1024,128]{1,0:T(8,128)(2,1)S(1)} %collective-permute-done.4.refs_0_, bf16[1024,128]{1,0:T(8,128)(2,1)S(1)} %collective-permute-done.3.refs_1_, ...), custom_call_target="tpu_custom_call" | custom-call | tf_op jit(solution)/shard_map/pool/pallas_call | solution.py:162
  28.8 1.9 %pool.8.refs_2_ = f32[128,3328]{1,0:T(8,128)S(1)} custom-call(f32[26,128]{1,0:T(8,128)S(1)} %get-tuple-element.82.refs_0_.turn_ref, bf16[1024,3328]{1,0:T(8,128)(2,1)S(1)} %get-tuple-element.117.refs_1_.counts_ref.refs_2_, bf16[1024,128]{1,0:T(8,128)(2,1)S(1)} %collective-permute-done.4.refs_0_, bf16[1024,128]{1,0:T(8,128)(2,1)S(1)} %collective-permute-done.3.refs_1_, ...), custom_call_target="tpu_custom_call" | custom-call | tf_op jit(solution)/shard_map/pool/pallas_call | solution.py:162
  30.8 1.9 %collective-permute-start.7 = (bf16[512,128]{1,0:T(8,128)(2,1)S(1)}, bf16[512,128]{1,0:T(8,128)(2,1)S(1)}, u32[]{:S(2)}, u32[]{:S(2)}) collective-permute-start(bf16[512,128]{1,0:T(8,128)(2,1)S(1)} %slice.57), channel_id=1, source_target_pairs={{1,3},{3,5},{5,7},{7,6},{6,4},{4,2},{2,0},{0,1},{11,9},{13,11},{15... | collective-permute-start | bytes 393224 | tf_op jit(solution)/shard_map/ppermute | solution.py:403
  32.7 0.3 collective-permute-start.8
  33.1 1.9 %pool.12.refs_2_ = f32[128,3328]{1,0:T(8,128)S(1)} custom-call(f32[26,128]{1,0:T(8,128)S(1)} %get-tuple-element.87.turn_ref, bf16[1024,3328]{1,0:T(8,128)(2,1)S(1)} %get-tuple-element.120.counts_ref.refs_2_.refs_5_, bf16[1024,128]{1,0:T(8,128)(2,1)S(1)} %collective-permute-done.6.refs_0_, bf16[1024,128]{1,0:T(8,128)(2,1)S(1)} %collective-permute-done.5.refs_1_, ...), custom_call_target="tpu_custom_call" | custom-call | tf_op jit(solution)/shard_map/pool/pallas_call | solution.py:162
  35.0 1.9 %pool.11.refs_2_ = f32[128,3328]{1,0:T(8,128)S(1)} custom-call(f32[26,128]{1,0:T(8,128)S(1)} %get-tuple-element.82.refs_0_.turn_ref, bf16[1024,3328]{1,0:T(8,128)(2,1)S(1)} %get-tuple-element.117.refs_1_.counts_ref.refs_2_, bf16[1024,128]{1,0:T(8,128)(2,1)S(1)} %collective-permute-done.6.refs_0_, bf16[1024,128]{1,0:T(8,128)(2,1)S(1)} %collective-permute-done.5.refs_1_, ...), custom_call_target="tpu_custom_call" | custom-call | tf_op jit(solution)/shard_map/pool/pallas_call | solution.py:162
  37.0 0.7 collective-permute-done.8.refs_1_
  37.7 0.6 pool.15
  38.4 0.7 pool.14
  39.1 0.6 collective-permute-start.9
  39.7 1.1 %pool.13.own_ref = f32[128,3328]{1,0:T(8,128)S(1)} custom-call(f32[26,128]{1,0:T(8,128)S(1)} %get-tuple-element.82.refs_0_.turn_ref, bf16[1024,3328]{1,0:T(8,128)(2,1)S(1)} %get-tuple-element.117.refs_1_.counts_ref.refs_2_, bf16[512,128]{1,0:T(8,128)(2,1)S(1)} %collective-permute-done.7.refs_0_, bf16[512,128]{1,0:T(8,128)(2,1)S(1)} %collective-permute-done.8.refs_1_, ...), custom_call_target="tpu_custom_call" | custom-call | tf_op jit(solution)/shard_map/pool/pallas_call | solution.py:162
  40.8 1.2 %collective-permute-done.9.first_ref = f32[128,1664]{1,0:T(8,128)S(1)} collective-permute-done((f32[128,1664]{1,0:T(8,128)S(1)}, f32[128,1664]{1,0:T(8,128)S(1)}, u32[]{:S(2)}, u32[]{:S(2)}) %collective-permute-start.9) | collective-permute-done | bytes 852000 | tf_op jit(solution)/shard_map/ppermute | solution.py:328
  42.0 4.5 %cross_layer.1 = (bf16[3328,128]{1,0:T(8,128)(2,1)S(1)}, bf16[128,128]{1,0:T(8,128)(2,1)}, f32[2,27,128]{2,1,0:T(8,128)S(1)}) custom-call(bf16[128,128]{1,0:T(8,128)(2,1)S(1)} %copy-done.3, f32[128,3328]{1,0:T(8,128)S(1)} %pool.13.own_ref, f32[128,1664]{1,0:T(8,128)S(1)} %collective-permute-done.9.first_ref, ...), custom_call_target="tpu_custom_call" | custom-call | flops 8000000000 | bytes 12000000 | tf_op jit(solution)/shard_map/cross_layer/pallas_call | solution.py:249
  46.5 0.2 collective-permute-start.11
  46.7 0.4 collective-permute-start.12
  47.1 2.1 %spread.5.refs_3_ = f32[1024,256]{1,0:T(8,128)S(1)} custom-call(bf16[3328,128]{1,0:T(8,128)(2,1)S(1)} %get-tuple-element.115.refs_0_, bf16[3328,128]{1,0:T(8,128)(2,1)S(1)} %get-tuple-element.116.refs_1_, bf16[1024,3328]{1,0:T(8,128)(2,1)S(1)} %get-tuple-element.117.refs_1_.counts_ref.refs_2_), custom_call_target="tpu_custom_call" | custom-call | tf_op jit(solution)/shard_map/spread/pallas_call | solution.py:289
  49.2 2.4 %spread.6 = f32[1024,256]{1,0:T(8,128)S(1)} custom-call(bf16[3328,128]{1,0:T(8,128)(2,1)S(1)} %get-tuple-element.118.refs_0_.refs_3_, bf16[3328,128]{1,0:T(8,128)(2,1)S(1)} %collective-permute-done.11.refs_1_.refs_4_, bf16[1024,3328]{1,0:T(8,128)(2,1)S(1)} %get-tuple-element.120.counts_ref.refs_2_.refs_5_, f32[1024,256]{1,0:T(8,128)S(1)} %spread.5.refs_3_), custom_call_target="tpu_custom_call" | custom-call | tf_op jit(solution)/shard_map/spread/pallas_call | solution.py:289
  51.7 1.6 %collective-permute-start.13 = (bf16[512,128]{1,0:T(8,128)(2,1)S(1)}, bf16[512,128]{1,0:T(8,128)(2,1)S(1)}, u32[]{:S(2)}, u32[]{:S(2)}) collective-permute-start(bf16[512,128]{1,0:T(8,128)(2,1)S(1)} %get-tuple-element.139), channel_id=1, source_target_pairs={{1,3},{3,5},{5,7},{7,6},{6,4},{4,2},{2,0},{0,1},{11,9},{13,11},{15... | collective-permute-start | bytes 393224 | tf_op jit(solution)/shard_map/ppermute | solution.py:441
  53.3 0.5 collective-permute-start.14
  53.8 3.9 %spread.7 = f32[1024,256]{1,0:T(8,128)S(1)} custom-call(bf16[3328,128]{1,0:T(8,128)(2,1)S(1)} %get-tuple-element.115.refs_0_, bf16[3328,128]{1,0:T(8,128)(2,1)S(1)} %get-tuple-element.116.refs_1_, bf16[1024,3328]{1,0:T(8,128)(2,1)S(1)} %get-tuple-element.117.refs_1_.counts_ref.refs_2_, bf16[3328,128]{1,0:T(8,128)(2,1)S(1)} %get-tuple-element.118.refs_0_.refs_3_, ...), custom_call_target="tpu_custom_call" | custom-call | tf_op jit(solution)/shard_map/spread/pallas_call | solution.py:289
  57.7 0.3 collective-permute-done.13
  58.0 0.2 collective-permute-done.14
  58.3 0.1 fusion.4
  58.3 1.6 %collective-permute-start.15 = (bf16[1024,128]{1,0:T(8,128)(2,1)S(1)}, bf16[1024,128]{1,0:T(8,128)(2,1)S(1)}, u32[]{:S(2)}, u32[]{:S(2)}) collective-permute-start(bf16[1024,128]{1,0:T(8,128)(2,1)S(1)} %get-tuple-element.112), channel_id=1, source_target_pairs={{1,3},{3,5},{5,7},{7,6},{6,4},{4,2},{2,0},{0,1},{11,9},{13,11},{15... | collective-permute-start | bytes 786440 | tf_op jit(solution)/shard_map/ppermute | solution.py:441
  60.0 0.4 collective-permute-start.16
  60.4 1.5 %collective-permute-start.17 = (f32[2,27,128]{2,1,0:T(8,128)S(1)}, f32[2,27,128]{2,1,0:T(8,128)S(1)}, u32[]{:S(2)}, u32[]{:S(2)}) collective-permute-start(f32[2,27,128]{2,1,0:T(8,128)S(1)} %add.68), channel_id=1, source_target_pairs={{0,16},{8,24},{16,0},{24,8},{1,17},{9,25},{17,1},{25,9},{2,18},{10... | collective-permute-start | bytes 82952 | tf_op jit(solution)/shard_map/ppermute | solution.py:328
  61.9 3.9 %spread.8 = f32[1024,256]{1,0:T(8,128)S(1)} custom-call(bf16[3328,128]{1,0:T(8,128)(2,1)S(1)} %get-tuple-element.115.refs_0_, bf16[3328,128]{1,0:T(8,128)(2,1)S(1)} %get-tuple-element.116.refs_1_, bf16[1024,3328]{1,0:T(8,128)(2,1)S(1)} %get-tuple-element.117.refs_1_.counts_ref.refs_2_, bf16[3328,128]{1,0:T(8,128)(2,1)S(1)} %get-tuple-element.118.refs_0_.refs_3_, ...), custom_call_target="tpu_custom_call" | custom-call | tf_op jit(solution)/shard_map/spread/pallas_call | solution.py:289
  65.8 1.3 %collective-permute-done.15 = bf16[1024,128]{1,0:T(8,128)(2,1)S(1)} collective-permute-done((bf16[1024,128]{1,0:T(8,128)(2,1)S(1)}, bf16[1024,128]{1,0:T(8,128)(2,1)S(1)}, u32[]{:S(2)}, u32[]{:S(2)}) %collective-permute-start.15) | collective-permute-done | bytes 262176 | tf_op jit(solution)/shard_map/ppermute | solution.py:441
  67.1 0.1 fusion.2
  67.3 1.2 %collective-permute-start.18 = (bf16[1024,128]{1,0:T(8,128)(2,1)S(1)}, bf16[1024,128]{1,0:T(8,128)(2,1)S(1)}, u32[]{:S(2)}, u32[]{:S(2)}) collective-permute-start(bf16[1024,128]{1,0:T(8,128)(2,1)S(1)} %get-tuple-element.121), channel_id=1, source_target_pairs={{1,3},{3,5},{5,7},{7,6},{6,4},{4,2},{2,0},{0,1},{11,9},{13,11},{15... | collective-permute-start | bytes 786440 | tf_op jit(solution)/shard_map/ppermute | solution.py:441
  68.5 0.9 collective-permute-start.19
  69.3 1.2 %collective-permute-start.20 = (f32[2,27,128]{2,1,0:T(8,128)S(1)}, f32[2,27,128]{2,1,0:T(8,128)S(1)}, u32[]{:S(2)}, u32[]{:S(2)}) collective-permute-start(f32[2,27,128]{2,1,0:T(8,128)S(1)} %add.73), channel_id=1, source_target_pairs={{0,1},{1,0},{2,3},{3,2},{4,5},{5,4},{6,7},{7,6},{8,9},{9,8},{10,11... | collective-permute-start | bytes 82952 | tf_op jit(solution)/shard_map/ppermute | solution.py:328
  70.5 3.9 %spread.9 = f32[1024,256]{1,0:T(8,128)S(1)} custom-call(bf16[3328,128]{1,0:T(8,128)(2,1)S(1)} %get-tuple-element.115.refs_0_, bf16[3328,128]{1,0:T(8,128)(2,1)S(1)} %get-tuple-element.116.refs_1_, bf16[1024,3328]{1,0:T(8,128)(2,1)S(1)} %get-tuple-element.117.refs_1_.counts_ref.refs_2_, bf16[3328,128]{1,0:T(8,128)(2,1)S(1)} %get-tuple-element.118.refs_0_.refs_3_, ...), custom_call_target="tpu_custom_call" | custom-call | tf_op jit(solution)/shard_map/spread/pallas_call | solution.py:289
  74.4 1.5 %collective-permute-done.20 = f32[2,27,128]{2,1,0:T(8,128)S(1)} collective-permute-done((f32[2,27,128]{2,1,0:T(8,128)S(1)}, f32[2,27,128]{2,1,0:T(8,128)S(1)}, u32[]{:S(2)}, u32[]{:S(2)}) %collective-permute-start.20) | collective-permute-done | bytes 27680 | tf_op jit(solution)/shard_map/ppermute | solution.py:328
  76.0 0.1 collective-permute-done.18
  76.1 0.1 fusion
  76.2 1.7 %collective-permute-start.21 = (bf16[1024,128]{1,0:T(8,128)(2,1)S(1)}, bf16[1024,128]{1,0:T(8,128)(2,1)S(1)}, u32[]{:S(2)}, u32[]{:S(2)}) collective-permute-start(bf16[1024,128]{1,0:T(8,128)(2,1)S(1)} %get-tuple-element.124), channel_id=1, source_target_pairs={{1,3},{3,5},{5,7},{7,6},{6,4},{4,2},{2,0},{0,1},{11,9},{13,11},{15... | collective-permute-start | bytes 786440 | tf_op jit(solution)/shard_map/ppermute | solution.py:441
  77.9 0.4 collective-permute-start.22
  78.3 0.5 collective-permute-start.23
  78.8 7.0 %collective-permute-done.23 = f32[2,27,128]{2,1,0:T(8,128)S(1)} collective-permute-done((f32[2,27,128]{2,1,0:T(8,128)S(1)}, f32[2,27,128]{2,1,0:T(8,128)S(1)}, u32[]{:S(2)}, u32[]{:S(2)}) %collective-permute-start.23) | collective-permute-done | bytes 27680 | tf_op jit(solution)/shard_map/ppermute | solution.py:328
  85.8 0.1 fusion.7
  85.9 1.5 %collective-permute-start.24 = (bf16[1024,128]{1,0:T(8,128)(2,1)S(1)}, bf16[1024,128]{1,0:T(8,128)(2,1)S(1)}, u32[]{:S(2)}, u32[]{:S(2)}) collective-permute-start(bf16[1024,128]{1,0:T(8,128)(2,1)S(1)} %fusion.7), channel_id=1, source_target_pairs={{0,16},{8,24},{16,0},{24,8},{1,17},{9,25},{17,1},{25,9},{2,18},{10... | collective-permute-start | bytes 786440 | tf_op jit(solution)/shard_map/ppermute | solution.py:328
  87.4 1.9 %collective-permute-start.25 = (f32[2,27,128]{2,1,0:T(8,128)S(1)}, f32[2,27,128]{2,1,0:T(8,128)S(1)}, u32[]{:S(2)}, u32[]{:S(2)}) collective-permute-start(f32[2,27,128]{2,1,0:T(8,128)S(1)} %add.79), channel_id=1, source_target_pairs={{0,4},{1,5},{2,6},{3,7},{4,0},{5,1},{6,2},{7,3},{8,12},{9,13},{10,... | collective-permute-start | bytes 82952 | tf_op jit(solution)/shard_map/ppermute | solution.py:328
  89.3 3.0 %collective-permute-done.25 = f32[2,27,128]{2,1,0:T(8,128)S(1)} collective-permute-done((f32[2,27,128]{2,1,0:T(8,128)S(1)}, f32[2,27,128]{2,1,0:T(8,128)S(1)}, u32[]{:S(2)}, u32[]{:S(2)}) %collective-permute-start.25) | collective-permute-done | bytes 27680 | tf_op jit(solution)/shard_map/ppermute | solution.py:328
  92.3 1.7 %collective-permute-done.24 = bf16[1024,128]{1,0:T(8,128)(2,1)S(1)} collective-permute-done((bf16[1024,128]{1,0:T(8,128)(2,1)S(1)}, bf16[1024,128]{1,0:T(8,128)(2,1)S(1)}, u32[]{:S(2)}, u32[]{:S(2)}) %collective-permute-start.24) | collective-permute-done | bytes 262176 | tf_op jit(solution)/shard_map/ppermute | solution.py:328
  94.2 0.8 place_half.2.refs_0_
  95.0 0.6 slice_bitcast_fusion
  95.6 0.5 collective-permute-done.26.part_ref
  96.1 0.8 place_half.3
  (46 shorter events, 0.5 us)
Async XLA Ops:
  0.6 1.0 %copy-start = (bf16[2048,128]{1,0:T(8,128)(2,1)S(1)}, bf16[2048,128]{1,0:T(8,128)(2,1)}, u32[]{:S(2)}) copy-start(bf16[2048,128]{1,0:T(8,128)(2,1)} %param.11) | copy-start | bytes 1572868
  1.9 10.2 %collective-permute-start = (bf16[1024,128]{1,0:T(8,128)(2,1)S(1)}, bf16[1024,128]{1,0:T(8,128)(2,1)S(1)}, u32[]{:S(2)}, u32[]{:S(2)}) collective-permute-start(bf16[1024,128]{1,0:T(8,128)(2,1)S(1)} %bitcast.25), channel_id=1, source_target_pairs={{1,3},{3,5},{5,7},{7,6},{6,4},{4,2},{2,0},{0,1},{11,9},{13,11},{15... | collective-permute-start | bytes 786440 | tf_op jit(solution)/shard_map/ppermute | solution.py:385
  4.9 7.2 %collective-permute-start.1 = (bf16[1024,128]{1,0:T(8,128)(2,1)S(1)}, bf16[1024,128]{1,0:T(8,128)(2,1)S(1)}, u32[]{:S(2)}, u32[]{:S(2)}) collective-permute-start(bf16[1024,128]{1,0:T(8,128)(2,1)S(1)} %bitcast.26), channel_id=1, source_target_pairs={{3,1},{5,3},{7,5},{6,7},{4,6},{2,4},{0,2},{1,0},{9,11},{11,13},{13... | collective-permute-start | bytes 786440 | tf_op jit(solution)/shard_map/ppermute | solution.py:386
  6.7 5.4 %collective-permute-start.2 = (s32[26,8,128]{2,1,0:T(8,128)S(1)}, s32[26,8,128]{2,1,0:T(8,128)S(1)}, u32[]{:S(2)}, u32[]{:S(2)}) collective-permute-start(s32[26,8,128]{2,1,0:T(8,128)S(1)} %fusion.8.place_ref), channel_id=1, source_target_pairs={{0,8},{8,0},{16,24},{24,16},{1,9},{9,1},{17,25},{25,17},{2,10},{10... | collective-permute-start | bytes 319496 | tf_op jit(solution)/shard_map/ppermute | solution.py:328
  12.1 9.6 %collective-permute-start.3 = (bf16[1024,128]{1,0:T(8,128)(2,1)S(1)}, bf16[1024,128]{1,0:T(8,128)(2,1)S(1)}, u32[]{:S(2)}, u32[]{:S(2)}) collective-permute-start(bf16[1024,128]{1,0:T(8,128)(2,1)S(1)} %collective-permute-done.refs_4_.refs_2_), channel_id=1, source_target_pairs={{1,3},{3,5},{5,7},{7,6},{6,4},{4,2},{2,0},{0,1},{11,9},{13,11},{15... | collective-permute-start | bytes 786440 | tf_op jit(solution)/shard_map/ppermute | solution.py:385
  14.0 7.7 %collective-permute-start.4 = (bf16[1024,128]{1,0:T(8,128)(2,1)S(1)}, bf16[1024,128]{1,0:T(8,128)(2,1)S(1)}, u32[]{:S(2)}, u32[]{:S(2)}) collective-permute-start(bf16[1024,128]{1,0:T(8,128)(2,1)S(1)} %collective-permute-done.1.refs_3_.refs_1_), channel_id=1, source_target_pairs={{3,1},{5,3},{7,5},{6,7},{4,6},{2,4},{0,2},{1,0},{9,11},{11,13},{13... | collective-permute-start | bytes 786440 | tf_op jit(solution)/shard_map/ppermute | solution.py:386
  21.7 9.0 %collective-permute-start.5 = (bf16[1024,128]{1,0:T(8,128)(2,1)S(1)}, bf16[1024,128]{1,0:T(8,128)(2,1)S(1)}, u32[]{:S(2)}, u32[]{:S(2)}) collective-permute-start(bf16[1024,128]{1,0:T(8,128)(2,1)S(1)} %collective-permute-done.3.refs_1_), channel_id=1, source_target_pairs={{1,3},{3,5},{5,7},{7,6},{6,4},{4,2},{2,0},{0,1},{11,9},{13,11},{15... | collective-permute-start | bytes 786440 | tf_op jit(solution)/shard_map/ppermute | solution.py:385
  23.6 7.1 %collective-permute-start.6 = (bf16[1024,128]{1,0:T(8,128)(2,1)S(1)}, bf16[1024,128]{1,0:T(8,128)(2,1)S(1)}, u32[]{:S(2)}, u32[]{:S(2)}) collective-permute-start(bf16[1024,128]{1,0:T(8,128)(2,1)S(1)} %collective-permute-done.4.refs_0_), channel_id=1, source_target_pairs={{3,1},{5,3},{7,5},{6,7},{4,6},{2,4},{0,2},{1,0},{9,11},{11,13},{13... | collective-permute-start | bytes 786440 | tf_op jit(solution)/shard_map/ppermute | solution.py:386
  23.8 2.8 %copy-start.1 = (bf16[3456,512]{1,0:T(8,128)(2,1)S(1)}, bf16[3456,512]{1,0:T(8,128)(2,1)}, u32[]{:S(2)}) copy-start(bf16[3456,512]{1,0:T(8,128)(2,1)} %down_ref.1) | copy-start | bytes 10616836
  23.8 3.1 %copy-start.2 = (bf16[512,3456]{1,0:T(8,128)(2,1)S(1)}, bf16[512,3456]{1,0:T(8,128)(2,1)}, u32[]{:S(2)}) copy-start(bf16[512,3456]{1,0:T(8,128)(2,1)} %up_ref.1) | copy-start | bytes 10616836
  30.8 6.2 %collective-permute-start.7 = (bf16[512,128]{1,0:T(8,128)(2,1)S(1)}, bf16[512,128]{1,0:T(8,128)(2,1)S(1)}, u32[]{:S(2)}, u32[]{:S(2)}) collective-permute-start(bf16[512,128]{1,0:T(8,128)(2,1)S(1)} %slice.57), channel_id=1, source_target_pairs={{1,3},{3,5},{5,7},{7,6},{6,4},{4,2},{2,0},{0,1},{11,9},{13,11},{15... | collective-permute-start | bytes 393224 | tf_op jit(solution)/shard_map/ppermute | solution.py:403
  32.7 5.0 %collective-permute-start.8 = (bf16[512,128]{1,0:T(8,128)(2,1)S(1)}, bf16[512,128]{1,0:T(8,128)(2,1)S(1)}, u32[]{:S(2)}, u32[]{:S(2)}) collective-permute-start(bf16[512,128]{1,0:T(8,128)(2,1)S(1)} %slice.58), channel_id=1, source_target_pairs={{3,1},{5,3},{7,5},{6,7},{4,6},{2,4},{0,2},{1,0},{9,11},{11,13},{13... | collective-permute-start | bytes 393224 | tf_op jit(solution)/shard_map/ppermute | solution.py:403
  38.3 1.3 %copy-start.7 = (s32[128]{0:T(128)S(1)}, s32[128]{0:T(128)}, u32[]{:S(2)}) copy-start(s32[128]{0:T(128)} %param.16) | copy-start | bytes 1540
  38.4 2.4 %collective-permute-start.10 = (f32[128,1664]{1,0:T(8,128)S(1)}, f32[128,1664]{1,0:T(8,128)S(1)}, u32[]{:S(2)}, u32[]{:S(2)}) collective-permute-start(f32[128,1664]{1,0:T(8,128)S(1)} %pool.15), channel_id=1, source_target_pairs={{0,8},{8,0},{16,24},{24,16},{1,9},{9,1},{17,25},{25,17},{2,10},{10... | collective-permute-start | bytes 2555912 | tf_op jit(solution)/shard_map/ppermute | solution.py:328
  39.1 2.9 %collective-permute-start.9 = (f32[128,1664]{1,0:T(8,128)S(1)}, f32[128,1664]{1,0:T(8,128)S(1)}, u32[]{:S(2)}, u32[]{:S(2)}) collective-permute-start(f32[128,1664]{1,0:T(8,128)S(1)} %pool.14), channel_id=1, source_target_pairs={{0,8},{8,0},{16,24},{24,16},{1,9},{9,1},{17,25},{25,17},{2,10},{10... | collective-permute-start | bytes 2555912 | tf_op jit(solution)/shard_map/ppermute | solution.py:328
  39.7 2.4 %copy-start.3 = (bf16[128,128]{1,0:T(8,128)(2,1)S(1)}, bf16[128,128]{1,0:T(8,128)(2,1)}, u32[]{:S(2)}) copy-start(bf16[128,128]{1,0:T(8,128)(2,1)} %dense_ref.1) | copy-start | bytes 98308
  39.7 2.4 %copy-start.4 = (f32[3456]{0:T(1024)S(1)}, f32[3456]{0:T(1024)}, u32[]{:S(2)}) copy-start(f32[3456]{0:T(1024)} %param.20) | copy-start | bytes 41476
  39.7 2.4 %copy-start.5 = (f32[3456]{0:T(1024)S(1)}, f32[3456]{0:T(1024)}, u32[]{:S(2)}) copy-start(f32[3456]{0:T(1024)} %param.21) | copy-start | bytes 41476
  39.7 2.4 %copy-start.6 = (f32[128]{0:T(128)S(1)}, f32[128]{0:T(128)}, u32[]{:S(2)}) copy-start(f32[128]{0:T(128)} %param.17) | copy-start | bytes 1540
  46.5 2.7 %collective-permute-start.11 = (bf16[3328,128]{1,0:T(8,128)(2,1)S(1)}, bf16[3328,128]{1,0:T(8,128)(2,1)S(1)}, u32[]{:S(2)}, u32[]{:S(2)}) collective-permute-start(bf16[3328,128]{1,0:T(8,128)(2,1)S(1)} %get-tuple-element.116.refs_1_), channel_id=1, source_target_pairs={{0,8},{8,0},{16,24},{24,16},{1,9},{9,1},{17,25},{25,17},{2,10},{10... | collective-permute-start | bytes 2555912 | tf_op jit(solution)/shard_map/ppermute | solution.py:328
  46.7 2.5 %collective-permute-start.12 = (f32[2,27,128]{2,1,0:T(8,128)S(1)}, f32[2,27,128]{2,1,0:T(8,128)S(1)}, u32[]{:S(2)}, u32[]{:S(2)}) collective-permute-start(f32[2,27,128]{2,1,0:T(8,128)S(1)} %get-tuple-element.97), channel_id=1, source_target_pairs={{0,8},{8,0},{16,24},{24,16},{1,9},{9,1},{17,25},{25,17},{2,10},{10... | collective-permute-start | bytes 82952 | tf_op jit(solution)/shard_map/ppermute | solution.py:328
  51.7 6.4 %collective-permute-start.13 = (bf16[512,128]{1,0:T(8,128)(2,1)S(1)}, bf16[512,128]{1,0:T(8,128)(2,1)S(1)}, u32[]{:S(2)}, u32[]{:S(2)}) collective-permute-start(bf16[512,128]{1,0:T(8,128)(2,1)S(1)} %get-tuple-element.139), channel_id=1, source_target_pairs={{1,3},{3,5},{5,7},{7,6},{6,4},{4,2},{2,0},{0,1},{11,9},{13,11},{15... | collective-permute-start | bytes 393224 | tf_op jit(solution)/shard_map/ppermute | solution.py:441
  53.3 5.0 %collective-permute-start.14 = (bf16[512,128]{1,0:T(8,128)(2,1)S(1)}, bf16[512,128]{1,0:T(8,128)(2,1)S(1)}, u32[]{:S(2)}, u32[]{:S(2)}) collective-permute-start(bf16[512,128]{1,0:T(8,128)(2,1)S(1)} %get-tuple-element.138), channel_id=1, source_target_pairs={{3,1},{5,3},{7,5},{6,7},{4,6},{2,4},{0,2},{1,0},{9,11},{11,13},{13... | collective-permute-start | bytes 393224 | tf_op jit(solution)/shard_map/ppermute | solution.py:441
  58.3 8.8 %collective-permute-start.15 = (bf16[1024,128]{1,0:T(8,128)(2,1)S(1)}, bf16[1024,128]{1,0:T(8,128)(2,1)S(1)}, u32[]{:S(2)}, u32[]{:S(2)}) collective-permute-start(bf16[1024,128]{1,0:T(8,128)(2,1)S(1)} %get-tuple-element.112), channel_id=1, source_target_pairs={{1,3},{3,5},{5,7},{7,6},{6,4},{4,2},{2,0},{0,1},{11,9},{13,11},{15... | collective-permute-start | bytes 786440 | tf_op jit(solution)/shard_map/ppermute | solution.py:441
  60.0 7.2 %collective-permute-start.16 = (bf16[1024,128]{1,0:T(8,128)(2,1)S(1)}, bf16[1024,128]{1,0:T(8,128)(2,1)S(1)}, u32[]{:S(2)}, u32[]{:S(2)}) collective-permute-start(bf16[1024,128]{1,0:T(8,128)(2,1)S(1)} %get-tuple-element.113), channel_id=1, source_target_pairs={{3,1},{5,3},{7,5},{6,7},{4,6},{2,4},{0,2},{1,0},{9,11},{11,13},{13... | collective-permute-start | bytes 786440 | tf_op jit(solution)/shard_map/ppermute | solution.py:441
  60.4 5.4 %collective-permute-start.17 = (f32[2,27,128]{2,1,0:T(8,128)S(1)}, f32[2,27,128]{2,1,0:T(8,128)S(1)}, u32[]{:S(2)}, u32[]{:S(2)}) collective-permute-start(f32[2,27,128]{2,1,0:T(8,128)S(1)} %add.68), channel_id=1, source_target_pairs={{0,16},{8,24},{16,0},{24,8},{1,17},{9,25},{17,1},{25,9},{2,18},{10... | collective-permute-start | bytes 82952 | tf_op jit(solution)/shard_map/ppermute | solution.py:328
  67.3 8.9 %collective-permute-start.18 = (bf16[1024,128]{1,0:T(8,128)(2,1)S(1)}, bf16[1024,128]{1,0:T(8,128)(2,1)S(1)}, u32[]{:S(2)}, u32[]{:S(2)}) collective-permute-start(bf16[1024,128]{1,0:T(8,128)(2,1)S(1)} %get-tuple-element.121), channel_id=1, source_target_pairs={{1,3},{3,5},{5,7},{7,6},{6,4},{4,2},{2,0},{0,1},{11,9},{13,11},{15... | collective-permute-start | bytes 786440 | tf_op jit(solution)/shard_map/ppermute | solution.py:441
  68.5 7.6 %collective-permute-start.19 = (bf16[1024,128]{1,0:T(8,128)(2,1)S(1)}, bf16[1024,128]{1,0:T(8,128)(2,1)S(1)}, u32[]{:S(2)}, u32[]{:S(2)}) collective-permute-start(bf16[1024,128]{1,0:T(8,128)(2,1)S(1)} %get-tuple-element.122), channel_id=1, source_target_pairs={{3,1},{5,3},{7,5},{6,7},{4,6},{2,4},{0,2},{1,0},{9,11},{11,13},{13... | collective-permute-start | bytes 786440 | tf_op jit(solution)/shard_map/ppermute | solution.py:441
  69.3 6.6 %collective-permute-start.20 = (f32[2,27,128]{2,1,0:T(8,128)S(1)}, f32[2,27,128]{2,1,0:T(8,128)S(1)}, u32[]{:S(2)}, u32[]{:S(2)}) collective-permute-start(f32[2,27,128]{2,1,0:T(8,128)S(1)} %add.73), channel_id=1, source_target_pairs={{0,1},{1,0},{2,3},{3,2},{4,5},{5,4},{6,7},{7,6},{8,9},{9,8},{10,11... | collective-permute-start | bytes 82952 | tf_op jit(solution)/shard_map/ppermute | solution.py:328
  76.2 9.6 %collective-permute-start.21 = (bf16[1024,128]{1,0:T(8,128)(2,1)S(1)}, bf16[1024,128]{1,0:T(8,128)(2,1)S(1)}, u32[]{:S(2)}, u32[]{:S(2)}) collective-permute-start(bf16[1024,128]{1,0:T(8,128)(2,1)S(1)} %get-tuple-element.124), channel_id=1, source_target_pairs={{1,3},{3,5},{5,7},{7,6},{6,4},{4,2},{2,0},{0,1},{11,9},{13,11},{15... | collective-permute-start | bytes 786440 | tf_op jit(solution)/shard_map/ppermute | solution.py:441
  77.9 7.9 %collective-permute-start.22 = (bf16[1024,128]{1,0:T(8,128)(2,1)S(1)}, bf16[1024,128]{1,0:T(8,128)(2,1)S(1)}, u32[]{:S(2)}, u32[]{:S(2)}) collective-permute-start(bf16[1024,128]{1,0:T(8,128)(2,1)S(1)} %get-tuple-element.125), channel_id=1, source_target_pairs={{3,1},{5,3},{7,5},{6,7},{4,6},{2,4},{0,2},{1,0},{9,11},{11,13},{13... | collective-permute-start | bytes 786440 | tf_op jit(solution)/shard_map/ppermute | solution.py:441
  78.3 7.5 %collective-permute-start.23 = (f32[2,27,128]{2,1,0:T(8,128)S(1)}, f32[2,27,128]{2,1,0:T(8,128)S(1)}, u32[]{:S(2)}, u32[]{:S(2)}) collective-permute-start(f32[2,27,128]{2,1,0:T(8,128)S(1)} %add.76), channel_id=1, source_target_pairs={{0,2},{1,3},{2,0},{3,1},{4,6},{5,7},{6,4},{7,5},{8,10},{9,11},{10,... | collective-permute-start | bytes 82952 | tf_op jit(solution)/shard_map/ppermute | solution.py:328
  85.9 8.1 %collective-permute-start.24 = (bf16[1024,128]{1,0:T(8,128)(2,1)S(1)}, bf16[1024,128]{1,0:T(8,128)(2,1)S(1)}, u32[]{:S(2)}, u32[]{:S(2)}) collective-permute-start(bf16[1024,128]{1,0:T(8,128)(2,1)S(1)} %fusion.7), channel_id=1, source_target_pairs={{0,16},{8,24},{16,0},{24,8},{1,17},{9,25},{17,1},{25,9},{2,18},{10... | collective-permute-start | bytes 786440 | tf_op jit(solution)/shard_map/ppermute | solution.py:328
  87.4 4.9 %collective-permute-start.25 = (f32[2,27,128]{2,1,0:T(8,128)S(1)}, f32[2,27,128]{2,1,0:T(8,128)S(1)}, u32[]{:S(2)}, u32[]{:S(2)}) collective-permute-start(f32[2,27,128]{2,1,0:T(8,128)S(1)} %add.79), channel_id=1, source_target_pairs={{0,4},{1,5},{2,6},{3,7},{4,0},{5,1},{6,2},{7,3},{8,12},{9,13},{10,... | collective-permute-start | bytes 82952 | tf_op jit(solution)/shard_map/ppermute | solution.py:328
  94.1 2.0 %collective-permute-start.26 = (f32[1024,128]{1,0:T(8,128)S(1)}, f32[1024,128]{1,0:T(8,128)S(1)}, u32[]{:S(2)}, u32[]{:S(2)}) collective-permute-start(f32[1024,128]{1,0:T(8,128)S(1)} %convert_add_fusion.part_ref), channel_id=1, source_target_pairs={{0,8},{8,0},{16,24},{24,16},{1,9},{9,1},{17,25},{25,17},{2,10},{10... | collective-permute-start | bytes 1572872 | tf_op jit(solution)/shard_map/ppermute | solution.py:328

commit v7 on v6

--- a/solution.py
+++ b/solution.py
@@ -61,11 +61,11 @@
         owner = place[0:1, :] >> shift
         if owners == 8:
             turn = ring_place(owner) - ring_place(index)
-            turn = jnp.where(half == 0, turn, -turn) & (owners - 1)
+            turn_ref[pl.ds(at, 1), :] = (jnp.where(half == 0, turn, -turn) & 7).astype(F32)
+            turn = (turn & 7).astype(F32)
         else:
-            turn = owner
-        turn = turn.astype(F32)
-        turn_ref[pl.ds(at, 1), :] = turn
+            turn = owner.astype(F32)
+            turn_ref[pl.ds(at, 1), :] = turn
         lanes = pl.ds(pl.multiple_of(at * LANES, LANES), LANES)
         column_ref[lanes, :] = jnp.dot(
             jnp.where(eye, turn, 0.0).astype(BF16), ones, preferred_element_type=F32
@@ -346,13 +346,13 @@
     return cycle + [far * inner for far in range(outer - 1, -1, -1)]
 
 
-def ring_turns(owners):
+def ring_turns(owners, opposite):
     order = ring_order(owners)
     right = []
     for group in range(lax.axis_size("grp")):
         for i in range(owners):
             here, there = order[i], order[(i + 1) % owners]
-            if group % 2 == 1:
+            if opposite and group % 2 == 1:
                 here, there = there, here
             right.append((group * owners + here, group * owners + there))
     return right, [(there, here) for here, there in right]
@@ -376,7 +376,7 @@
                 add(side, here, [[table[one]] for one in here])
         sums[1] = [swap(one, "grp", 1) for one in jnp.split(sums[1], 2, axis=1)]
         return sides, sums
-    right, left = ring_turns(owners)
+    right, left = ring_turns(owners, True)
     lefts, rights = [shard], [shard]
 
     def step(beside):
@@ -432,7 +432,7 @@
             jnp.concatenate(parts, axis=1), "emb", scatter_dimension=1, tiled=True
         )
         return sum_pairs(part, "grp", 2, BF16), grads
-    right, left = ring_turns(owners)
+    right, left = ring_turns(owners, False)
 
     def exchange(grads):
         return grads + swap(grads, *exchanges.pop(0))

time: 97.3 us -> 93 us (0.956)
  waiting for transfers between devices: 17.7 us -> 13.3 us
    ppermute x11, waiting for transfers between devices: 15 us -> 10.1 us  [swap(): return lax.ppermute(value, axis, [(i, i ^ stride) for i in range(size)])]
    ppermute x4, waiting for transfers between devices: 0.23 us -> 2.5 us  [send(): lax.ppermute(to_left, RING, left)]
    ppermute x4, waiting for transfers between devices: 1.77 us -> 0.01 us  [send(): lax.ppermute(to_right, RING, right)]
  transfers between devices with their start and end apart: 27 -> 27, of which waited for: 11 -> 9; matrix products, arithmetic and copies ran while one was open for 2% -> 3% of each run, Pallas kernels for 41% -> 43%
where the time goes in v7:
time: 93 us; the launch traced here: 92.7 us
  Pallas kernels  47.9 us (52%)
  starting transfers between devices  25.8 us (28%)
  waiting for transfers between devices  13.3 us (14%)
  local copies, waits for them, and re-layouts  2.2 us (2%)
  other arithmetic  2.2 us (2%)
  between operations  1.26 us (1%)
    pallas_call x5, Pallas kernels, spread(): pl.pallas_call(functools.partial(spread_kernel, turns, len(sides), at), o...  16.2 us
    pallas_call x8, Pallas kernels, pool(): pl.pallas_call(functools.partial(pool_kernel, [len(shard) for shard in sh...  12.9 us
    pallas_call x2, Pallas kernels, bag_counts(): pl.pallas_call(functools.partial(count_kernel, owners, local_rows, turns)...  12.7 us
    ppermute x11, waiting for transfers between devices, swap(): return lax.ppermute(value, axis, [(i, i ^ stride) for i in range(size)])  10.1 us
    ppermute x11, starting transfers between devices, swap(): return lax.ppermute(value, axis, [(i, i ^ stride) for i in range(size)])  7.96 us
    ppermute x3, starting transfers between devices, step(): lefts.append(lax.ppermute(a, RING, right))  6.85 us
    ppermute x4, starting transfers between devices, send(): lax.ppermute(to_right, RING, right)  5.91 us
    pallas_call x1, Pallas kernels, cross_layer(): pl.pallas_call(functools.partial(cross_kernel, tables), out_shape=(jax.Sh...  4.45 us
  transfers between devices with their start and end apart: 27, of which 9 were waited for; matrix products, arithmetic and copies ran while one was open for 3% of the time, Pallas kernels for 43%

profile of v7, /device:TPU:0, one launch (start us, length us, event | category | flops | bytes accessed | tf_op | source)
XLA Modules:
  0.0 92.7 jit_solution(6622343800593392426)
XLA Ops:
  0.7 1.0 %copy-done = bf16[2048,128]{1,0:T(8,128)(2,1)S(1)} copy-done((bf16[2048,128]{1,0:T(8,128)(2,1)S(1)}, bf16[2048,128]{1,0:T(8,128)(2,1)}, u32[]{:S(2)}) %copy-start) | copy-done | bytes 524312
  1.7 0.2 copy.16
  1.9 3.0 %collective-permute-start = (bf16[1024,128]{1,0:T(8,128)(2,1)S(1)}, bf16[1024,128]{1,0:T(8,128)(2,1)S(1)}, u32[]{:S(2)}, u32[]{:S(2)}) collective-permute-start(bf16[1024,128]{1,0:T(8,128)(2,1)S(1)} %bitcast.25), channel_id=1, source_target_pairs={{1,3},{3,5},{5,7},{7,6},{6,4},{4,2},{2,0},{0,1},{11,9},{13,11},{15... | collective-permute-start | bytes 786440 | tf_op jit(solution)/shard_map/ppermute | solution.py:385
  4.9 0.2 collective-permute-start.1
  5.0 0.7 multiply_bitcast_fusion
  5.8 0.9 fusion.8.place_ref
  6.7 0.1 collective-permute-start.2
  6.8 0.1 pad_add_fusion.where_ref
  6.8 5.2 %bag_counts.2 = (bf16[1024,3328]{1,0:T(8,128)(2,1)S(1)}, f32[26,128]{1,0:T(8,128)S(1)}, bf16[3328,128]{1,0:T(8,128)(2,1)S(1)}) custom-call(s32[2]{0:T(128)S(1)} %pad_add_fusion.where_ref, s32[26,8,128]{2,1,0:T(8,128)S(1)} %fusion.8.place_ref), custom_call_target="tpu_custom_call" | custom-call | flops 5000000000 | tf_op jit(solution)/shard_map/bag_counts/pallas_call | solution.py:122
  12.1 1.9 %collective-permute-start.3 = (bf16[1024,128]{1,0:T(8,128)(2,1)S(1)}, bf16[1024,128]{1,0:T(8,128)(2,1)S(1)}, u32[]{:S(2)}, u32[]{:S(2)}) collective-permute-start(bf16[1024,128]{1,0:T(8,128)(2,1)S(1)} %collective-permute-done.refs_4_.refs_2_), channel_id=1, source_target_pairs={{1,3},{3,5},{5,7},{7,6},{6,4},{4,2},{2,0},{0,1},{11,9},{13,11},{15... | collective-permute-start | bytes 786440 | tf_op jit(solution)/shard_map/ppermute | solution.py:385
  14.0 0.2 collective-permute-start.4
  14.2 7.5 %bag_counts.3 = (bf16[1024,3328]{1,0:T(8,128)(2,1)S(1)}, f32[26,128]{1,0:T(8,128)S(1)}, bf16[3328,128]{1,0:T(8,128)(2,1)S(1)}, f32[128,3328]{1,0:T(8,128)S(1)}) custom-call(s32[2]{0:T(128)S(1)} %pad_add_fusion.where_ref, s32[26,8,128]{2,1,0:T(8,128)S(1)} %collective-permute-done.2.place_ref, f32[26,128]{1,0:T(8,128)S(1)} %get-tuple-element.82.refs_0_.turn_ref, ...), custom_call_target="tpu_custom_call" | custom-call | flops 5000000000 | tf_op jit(solution)/shard_map/bag_counts/pallas_call | solution.py:122
  21.7 1.9 %collective-permute-start.5 = (bf16[1024,128]{1,0:T(8,128)(2,1)S(1)}, bf16[1024,128]{1,0:T(8,128)(2,1)S(1)}, u32[]{:S(2)}, u32[]{:S(2)}) collective-permute-start(bf16[1024,128]{1,0:T(8,128)(2,1)S(1)} %collective-permute-done.3.refs_1_), channel_id=1, source_target_pairs={{1,3},{3,5},{5,7},{7,6},{6,4},{4,2},{2,0},{0,1},{11,9},{13,11},{15... | collective-permute-start | bytes 786440 | tf_op jit(solution)/shard_map/ppermute | solution.py:385
  23.6 0.2 collective-permute-start.6
  23.8 2.8 %pool.9.refs_2_ = f32[128,3328]{1,0:T(8,128)S(1)} custom-call(f32[26,128]{1,0:T(8,128)S(1)} %get-tuple-element.87.turn_ref, bf16[1024,3328]{1,0:T(8,128)(2,1)S(1)} %get-tuple-element.120.counts_ref.refs_2_.refs_5_, bf16[1024,128]{1,0:T(8,128)(2,1)S(1)} %bitcast.28, bf16[1024,128]{1,0:T(8,128)(2,1)S(1)} %collective-permute-done.1.refs_3_.refs_1_, ...), custom_call_target="tpu_custom_call" | custom-call | tf_op jit(solution)/shard_map/pool/pallas_call | solution.py:162
  26.6 0.3 copy-done.2
  26.9 1.9 %pool.10.refs_2_ = f32[128,3328]{1,0:T(8,128)S(1)} custom-call(f32[26,128]{1,0:T(8,128)S(1)} %get-tuple-element.87.turn_ref, bf16[1024,3328]{1,0:T(8,128)(2,1)S(1)} %get-tuple-element.120.counts_ref.refs_2_.refs_5_, bf16[1024,128]{1,0:T(8,128)(2,1)S(1)} %collective-permute-done.4.refs_0_, bf16[1024,128]{1,0:T(8,128)(2,1)S(1)} %collective-permute-done.3.refs_1_, ...), custom_call_target="tpu_custom_call" | custom-call | tf_op jit(solution)/shard_map/pool/pallas_call | solution.py:162
  28.8 1.9 %pool.8.refs_2_ = f32[128,3328]{1,0:T(8,128)S(1)} custom-call(f32[26,128]{1,0:T(8,128)S(1)} %get-tuple-element.82.refs_0_.turn_ref, bf16[1024,3328]{1,0:T(8,128)(2,1)S(1)} %get-tuple-element.117.refs_1_.counts_ref.refs_2_, bf16[1024,128]{1,0:T(8,128)(2,1)S(1)} %collective-permute-done.4.refs_0_, bf16[1024,128]{1,0:T(8,128)(2,1)S(1)} %collective-permute-done.3.refs_1_, ...), custom_call_target="tpu_custom_call" | custom-call | tf_op jit(solution)/shard_map/pool/pallas_call | solution.py:162
  30.8 1.9 %collective-permute-start.7 = (bf16[512,128]{1,0:T(8,128)(2,1)S(1)}, bf16[512,128]{1,0:T(8,128)(2,1)S(1)}, u32[]{:S(2)}, u32[]{:S(2)}) collective-permute-start(bf16[512,128]{1,0:T(8,128)(2,1)S(1)} %slice.57), channel_id=1, source_target_pairs={{1,3},{3,5},{5,7},{7,6},{6,4},{4,2},{2,0},{0,1},{11,9},{13,11},{15... | collective-permute-start | bytes 393224 | tf_op jit(solution)/shard_map/ppermute | solution.py:403
  32.7 0.4 collective-permute-start.8
  33.1 1.9 %pool.12.refs_2_ = f32[128,3328]{1,0:T(8,128)S(1)} custom-call(f32[26,128]{1,0:T(8,128)S(1)} %get-tuple-element.87.turn_ref, bf16[1024,3328]{1,0:T(8,128)(2,1)S(1)} %get-tuple-element.120.counts_ref.refs_2_.refs_5_, bf16[1024,128]{1,0:T(8,128)(2,1)S(1)} %collective-permute-done.6.refs_0_, bf16[1024,128]{1,0:T(8,128)(2,1)S(1)} %collective-permute-done.5.refs_1_, ...), custom_call_target="tpu_custom_call" | custom-call | tf_op jit(solution)/shard_map/pool/pallas_call | solution.py:162
  35.0 1.9 %pool.11.refs_2_ = f32[128,3328]{1,0:T(8,128)S(1)} custom-call(f32[26,128]{1,0:T(8,128)S(1)} %get-tuple-element.82.refs_0_.turn_ref, bf16[1024,3328]{1,0:T(8,128)(2,1)S(1)} %get-tuple-element.117.refs_1_.counts_ref.refs_2_, bf16[1024,128]{1,0:T(8,128)(2,1)S(1)} %collective-permute-done.6.refs_0_, bf16[1024,128]{1,0:T(8,128)(2,1)S(1)} %collective-permute-done.5.refs_1_, ...), custom_call_target="tpu_custom_call" | custom-call | tf_op jit(solution)/shard_map/pool/pallas_call | solution.py:162
  37.0 0.7 collective-permute-done.8.refs_1_
  37.7 0.6 pool.15
  38.5 0.7 pool.14
  39.1 0.6 collective-permute-start.9
  39.7 1.1 %pool.13.own_ref = f32[128,3328]{1,0:T(8,128)S(1)} custom-call(f32[26,128]{1,0:T(8,128)S(1)} %get-tuple-element.82.refs_0_.turn_ref, bf16[1024,3328]{1,0:T(8,128)(2,1)S(1)} %get-tuple-element.117.refs_1_.counts_ref.refs_2_, bf16[512,128]{1,0:T(8,128)(2,1)S(1)} %collective-permute-done.7.refs_0_, bf16[512,128]{1,0:T(8,128)(2,1)S(1)} %collective-permute-done.8.refs_1_, ...), custom_call_target="tpu_custom_call" | custom-call | tf_op jit(solution)/shard_map/pool/pallas_call | solution.py:162
  40.8 1.2 %collective-permute-done.9.first_ref = f32[128,1664]{1,0:T(8,128)S(1)} collective-permute-done((f32[128,1664]{1,0:T(8,128)S(1)}, f32[128,1664]{1,0:T(8,128)S(1)}, u32[]{:S(2)}, u32[]{:S(2)}) %collective-permute-start.9) | collective-permute-done | bytes 852000 | tf_op jit(solution)/shard_map/ppermute | solution.py:328
  42.1 4.5 %cross_layer.1 = (bf16[3328,128]{1,0:T(8,128)(2,1)S(1)}, bf16[128,128]{1,0:T(8,128)(2,1)}, f32[2,27,128]{2,1,0:T(8,128)S(1)}) custom-call(bf16[128,128]{1,0:T(8,128)(2,1)S(1)} %copy-done.3, f32[128,3328]{1,0:T(8,128)S(1)} %pool.13.own_ref, f32[128,1664]{1,0:T(8,128)S(1)} %collective-permute-done.9.first_ref, ...), custom_call_target="tpu_custom_call" | custom-call | flops 8000000000 | bytes 12000000 | tf_op jit(solution)/shard_map/cross_layer/pallas_call | solution.py:249
  46.5 0.2 collective-permute-start.11
  46.7 0.4 collective-permute-start.12
  47.1 2.1 %spread.5.refs_3_ = f32[1024,256]{1,0:T(8,128)S(1)} custom-call(bf16[3328,128]{1,0:T(8,128)(2,1)S(1)} %get-tuple-element.115.refs_0_, bf16[3328,128]{1,0:T(8,128)(2,1)S(1)} %get-tuple-element.116.refs_1_, bf16[1024,3328]{1,0:T(8,128)(2,1)S(1)} %get-tuple-element.117.refs_1_.counts_ref.refs_2_), custom_call_target="tpu_custom_call" | custom-call | tf_op jit(solution)/shard_map/spread/pallas_call | solution.py:289
  49.2 2.4 %spread.6 = f32[1024,256]{1,0:T(8,128)S(1)} custom-call(bf16[3328,128]{1,0:T(8,128)(2,1)S(1)} %get-tuple-element.118.refs_0_.refs_3_, bf16[3328,128]{1,0:T(8,128)(2,1)S(1)} %collective-permute-done.11.refs_1_.refs_4_, bf16[1024,3328]{1,0:T(8,128)(2,1)S(1)} %get-tuple-element.120.counts_ref.refs_2_.refs_5_, f32[1024,256]{1,0:T(8,128)S(1)} %spread.5.refs_3_), custom_call_target="tpu_custom_call" | custom-call | tf_op jit(solution)/shard_map/spread/pallas_call | solution.py:289
  51.7 1.6 %collective-permute-start.13 = (bf16[512,128]{1,0:T(8,128)(2,1)S(1)}, bf16[512,128]{1,0:T(8,128)(2,1)S(1)}, u32[]{:S(2)}, u32[]{:S(2)}) collective-permute-start(bf16[512,128]{1,0:T(8,128)(2,1)S(1)} %get-tuple-element.139), channel_id=1, source_target_pairs={{1,3},{3,5},{5,7},{7,6},{6,4},{4,2},{2,0},{0,1},{9,11},{11,13},{13... | collective-permute-start | bytes 393224 | tf_op jit(solution)/shard_map/ppermute | solution.py:441
  53.3 0.4 collective-permute-start.14
  53.8 3.9 %spread.7 = f32[1024,256]{1,0:T(8,128)S(1)} custom-call(bf16[3328,128]{1,0:T(8,128)(2,1)S(1)} %get-tuple-element.115.refs_0_, bf16[3328,128]{1,0:T(8,128)(2,1)S(1)} %get-tuple-element.116.refs_1_, bf16[1024,3328]{1,0:T(8,128)(2,1)S(1)} %get-tuple-element.117.refs_1_.counts_ref.refs_2_, bf16[3328,128]{1,0:T(8,128)(2,1)S(1)} %get-tuple-element.118.refs_0_.refs_3_, ...), custom_call_target="tpu_custom_call" | custom-call | tf_op jit(solution)/shard_map/spread/pallas_call | solution.py:289
  57.7 0.9 collective-permute-done.14
  58.6 0.1 fusion.4
  58.7 1.6 %collective-permute-start.15 = (bf16[1024,128]{1,0:T(8,128)(2,1)S(1)}, bf16[1024,128]{1,0:T(8,128)(2,1)S(1)}, u32[]{:S(2)}, u32[]{:S(2)}) collective-permute-start(bf16[1024,128]{1,0:T(8,128)(2,1)S(1)} %get-tuple-element.112), channel_id=1, source_target_pairs={{1,3},{3,5},{5,7},{7,6},{6,4},{4,2},{2,0},{0,1},{9,11},{11,13},{13... | collective-permute-start | bytes 786440 | tf_op jit(solution)/shard_map/ppermute | solution.py:441
  60.3 0.4 collective-permute-start.16
  60.7 1.5 %collective-permute-start.17 = (f32[2,27,128]{2,1,0:T(8,128)S(1)}, f32[2,27,128]{2,1,0:T(8,128)S(1)}, u32[]{:S(2)}, u32[]{:S(2)}) collective-permute-start(f32[2,27,128]{2,1,0:T(8,128)S(1)} %add.68), channel_id=1, source_target_pairs={{0,16},{8,24},{16,0},{24,8},{1,17},{9,25},{17,1},{25,9},{2,18},{10... | collective-permute-start | bytes 82952 | tf_op jit(solution)/shard_map/ppermute | solution.py:328
  62.3 3.9 %spread.8 = f32[1024,256]{1,0:T(8,128)S(1)} custom-call(bf16[3328,128]{1,0:T(8,128)(2,1)S(1)} %get-tuple-element.115.refs_0_, bf16[3328,128]{1,0:T(8,128)(2,1)S(1)} %get-tuple-element.116.refs_1_, bf16[1024,3328]{1,0:T(8,128)(2,1)S(1)} %get-tuple-element.117.refs_1_.counts_ref.refs_2_, bf16[3328,128]{1,0:T(8,128)(2,1)S(1)} %get-tuple-element.118.refs_0_.refs_3_, ...), custom_call_target="tpu_custom_call" | custom-call | tf_op jit(solution)/shard_map/spread/pallas_call | solution.py:289
  66.2 1.0 %collective-permute-done.16 = bf16[1024,128]{1,0:T(8,128)(2,1)S(1)} collective-permute-done((bf16[1024,128]{1,0:T(8,128)(2,1)S(1)}, bf16[1024,128]{1,0:T(8,128)(2,1)S(1)}, u32[]{:S(2)}, u32[]{:S(2)}) %collective-permute-start.16) | collective-permute-done | bytes 262176 | tf_op jit(solution)/shard_map/ppermute | solution.py:441
  67.2 0.1 fusion.2
  67.3 1.6 %collective-permute-start.18 = (bf16[1024,128]{1,0:T(8,128)(2,1)S(1)}, bf16[1024,128]{1,0:T(8,128)(2,1)S(1)}, u32[]{:S(2)}, u32[]{:S(2)}) collective-permute-start(bf16[1024,128]{1,0:T(8,128)(2,1)S(1)} %get-tuple-element.121), channel_id=1, source_target_pairs={{1,3},{3,5},{5,7},{7,6},{6,4},{4,2},{2,0},{0,1},{9,11},{11,13},{13... | collective-permute-start | bytes 786440 | tf_op jit(solution)/shard_map/ppermute | solution.py:441
  68.9 0.5 collective-permute-start.19
  69.4 1.6 %collective-permute-start.20 = (f32[2,27,128]{2,1,0:T(8,128)S(1)}, f32[2,27,128]{2,1,0:T(8,128)S(1)}, u32[]{:S(2)}, u32[]{:S(2)}) collective-permute-start(f32[2,27,128]{2,1,0:T(8,128)S(1)} %add.73), channel_id=1, source_target_pairs={{0,1},{1,0},{2,3},{3,2},{4,5},{5,4},{6,7},{7,6},{8,9},{9,8},{10,11... | collective-permute-start | bytes 82952 | tf_op jit(solution)/shard_map/ppermute | solution.py:328
  71.0 3.9 %spread.9 = f32[1024,256]{1,0:T(8,128)S(1)} custom-call(bf16[3328,128]{1,0:T(8,128)(2,1)S(1)} %get-tuple-element.115.refs_0_, bf16[3328,128]{1,0:T(8,128)(2,1)S(1)} %get-tuple-element.116.refs_1_, bf16[1024,3328]{1,0:T(8,128)(2,1)S(1)} %get-tuple-element.117.refs_1_.counts_ref.refs_2_, bf16[3328,128]{1,0:T(8,128)(2,1)S(1)} %get-tuple-element.118.refs_0_.refs_3_, ...), custom_call_target="tpu_custom_call" | custom-call | tf_op jit(solution)/shard_map/spread/pallas_call | solution.py:289
  74.9 0.8 collective-permute-done.20
  75.7 0.1 fusion
  75.8 1.0 %collective-permute-start.21 = (bf16[1024,128]{1,0:T(8,128)(2,1)S(1)}, bf16[1024,128]{1,0:T(8,128)(2,1)S(1)}, u32[]{:S(2)}, u32[]{:S(2)}) collective-permute-start(bf16[1024,128]{1,0:T(8,128)(2,1)S(1)} %get-tuple-element.124), channel_id=1, source_target_pairs={{1,3},{3,5},{5,7},{7,6},{6,4},{4,2},{2,0},{0,1},{9,11},{11,13},{13... | collective-permute-start | bytes 786440 | tf_op jit(solution)/shard_map/ppermute | solution.py:441
  76.8 1.1 %collective-permute-start.22 = (bf16[1024,128]{1,0:T(8,128)(2,1)S(1)}, bf16[1024,128]{1,0:T(8,128)(2,1)S(1)}, u32[]{:S(2)}, u32[]{:S(2)}) collective-permute-start(bf16[1024,128]{1,0:T(8,128)(2,1)S(1)} %get-tuple-element.125), channel_id=1, source_target_pairs={{3,1},{5,3},{7,5},{6,7},{4,6},{2,4},{0,2},{1,0},{11,9},{13,11},{15... | collective-permute-start | bytes 786440 | tf_op jit(solution)/shard_map/ppermute | solution.py:441
  77.9 0.6 collective-permute-start.23
  78.5 4.1 %collective-permute-done.23 = f32[2,27,128]{2,1,0:T(8,128)S(1)} collective-permute-done((f32[2,27,128]{2,1,0:T(8,128)S(1)}, f32[2,27,128]{2,1,0:T(8,128)S(1)}, u32[]{:S(2)}, u32[]{:S(2)}) %collective-permute-start.23) | collective-permute-done | bytes 27680 | tf_op jit(solution)/shard_map/ppermute | solution.py:328
  82.6 0.6 collective-permute-done.22
  83.2 0.1 fusion.7
  83.3 1.6 %collective-permute-start.24 = (bf16[1024,128]{1,0:T(8,128)(2,1)S(1)}, bf16[1024,128]{1,0:T(8,128)(2,1)S(1)}, u32[]{:S(2)}, u32[]{:S(2)}) collective-permute-start(bf16[1024,128]{1,0:T(8,128)(2,1)S(1)} %fusion.7), channel_id=1, source_target_pairs={{0,16},{8,24},{16,0},{24,8},{1,17},{9,25},{17,1},{25,9},{2,18},{10... | collective-permute-start | bytes 786440 | tf_op jit(solution)/shard_map/ppermute | solution.py:328
  84.9 1.3 %collective-permute-start.25 = (f32[2,27,128]{2,1,0:T(8,128)S(1)}, f32[2,27,128]{2,1,0:T(8,128)S(1)}, u32[]{:S(2)}, u32[]{:S(2)}) collective-permute-start(f32[2,27,128]{2,1,0:T(8,128)S(1)} %add.79), channel_id=1, source_target_pairs={{0,4},{1,5},{2,6},{3,7},{4,0},{5,1},{6,2},{7,3},{8,12},{9,13},{10,... | collective-permute-start | bytes 82952 | tf_op jit(solution)/shard_map/ppermute | solution.py:328
  86.2 3.5 %collective-permute-done.25 = f32[2,27,128]{2,1,0:T(8,128)S(1)} collective-permute-done((f32[2,27,128]{2,1,0:T(8,128)S(1)}, f32[2,27,128]{2,1,0:T(8,128)S(1)}, u32[]{:S(2)}, u32[]{:S(2)}) %collective-permute-start.25) | collective-permute-done | bytes 27680 | tf_op jit(solution)/shard_map/ppermute | solution.py:328
  89.8 0.1 collective-permute-start.26
  89.9 0.8 place_half.2.refs_0_
  90.7 0.6 slice_bitcast_fusion
  91.3 0.5 collective-permute-done.26.part_ref
  91.7 0.8 place_half.3
  (46 shorter events, 0.4 us)
Async XLA Ops:
  0.6 1.0 %copy-start = (bf16[2048,128]{1,0:T(8,128)(2,1)S(1)}, bf16[2048,128]{1,0:T(8,128)(2,1)}, u32[]{:S(2)}) copy-start(bf16[2048,128]{1,0:T(8,128)(2,1)} %param.11) | copy-start | bytes 1572868
  1.9 10.2 %collective-permute-start = (bf16[1024,128]{1,0:T(8,128)(2,1)S(1)}, bf16[1024,128]{1,0:T(8,128)(2,1)S(1)}, u32[]{:S(2)}, u32[]{:S(2)}) collective-permute-start(bf16[1024,128]{1,0:T(8,128)(2,1)S(1)} %bitcast.25), channel_id=1, source_target_pairs={{1,3},{3,5},{5,7},{7,6},{6,4},{4,2},{2,0},{0,1},{11,9},{13,11},{15... | collective-permute-start | bytes 786440 | tf_op jit(solution)/shard_map/ppermute | solution.py:385
  4.9 7.2 %collective-permute-start.1 = (bf16[1024,128]{1,0:T(8,128)(2,1)S(1)}, bf16[1024,128]{1,0:T(8,128)(2,1)S(1)}, u32[]{:S(2)}, u32[]{:S(2)}) collective-permute-start(bf16[1024,128]{1,0:T(8,128)(2,1)S(1)} %bitcast.26), channel_id=1, source_target_pairs={{3,1},{5,3},{7,5},{6,7},{4,6},{2,4},{0,2},{1,0},{9,11},{11,13},{13... | collective-permute-start | bytes 786440 | tf_op jit(solution)/shard_map/ppermute | solution.py:386
  6.7 5.4 %collective-permute-start.2 = (s32[26,8,128]{2,1,0:T(8,128)S(1)}, s32[26,8,128]{2,1,0:T(8,128)S(1)}, u32[]{:S(2)}, u32[]{:S(2)}) collective-permute-start(s32[26,8,128]{2,1,0:T(8,128)S(1)} %fusion.8.place_ref), channel_id=1, source_target_pairs={{0,8},{8,0},{16,24},{24,16},{1,9},{9,1},{17,25},{25,17},{2,10},{10... | collective-permute-start | bytes 319496 | tf_op jit(solution)/shard_map/ppermute | solution.py:328
  12.1 9.6 %collective-permute-start.3 = (bf16[1024,128]{1,0:T(8,128)(2,1)S(1)}, bf16[1024,128]{1,0:T(8,128)(2,1)S(1)}, u32[]{:S(2)}, u32[]{:S(2)}) collective-permute-start(bf16[1024,128]{1,0:T(8,128)(2,1)S(1)} %collective-permute-done.refs_4_.refs_2_), channel_id=1, source_target_pairs={{1,3},{3,5},{5,7},{7,6},{6,4},{4,2},{2,0},{0,1},{11,9},{13,11},{15... | collective-permute-start | bytes 786440 | tf_op jit(solution)/shard_map/ppermute | solution.py:385
  14.0 7.7 %collective-permute-start.4 = (bf16[1024,128]{1,0:T(8,128)(2,1)S(1)}, bf16[1024,128]{1,0:T(8,128)(2,1)S(1)}, u32[]{:S(2)}, u32[]{:S(2)}) collective-permute-start(bf16[1024,128]{1,0:T(8,128)(2,1)S(1)} %collective-permute-done.1.refs_3_.refs_1_), channel_id=1, source_target_pairs={{3,1},{5,3},{7,5},{6,7},{4,6},{2,4},{0,2},{1,0},{9,11},{11,13},{13... | collective-permute-start | bytes 786440 | tf_op jit(solution)/shard_map/ppermute | solution.py:386
  21.7 9.1 %collective-permute-start.5 = (bf16[1024,128]{1,0:T(8,128)(2,1)S(1)}, bf16[1024,128]{1,0:T(8,128)(2,1)S(1)}, u32[]{:S(2)}, u32[]{:S(2)}) collective-permute-start(bf16[1024,128]{1,0:T(8,128)(2,1)S(1)} %collective-permute-done.3.refs_1_), channel_id=1, source_target_pairs={{1,3},{3,5},{5,7},{7,6},{6,4},{4,2},{2,0},{0,1},{11,9},{13,11},{15... | collective-permute-start | bytes 786440 | tf_op jit(solution)/shard_map/ppermute | solution.py:385
  23.6 7.2 %collective-permute-start.6 = (bf16[1024,128]{1,0:T(8,128)(2,1)S(1)}, bf16[1024,128]{1,0:T(8,128)(2,1)S(1)}, u32[]{:S(2)}, u32[]{:S(2)}) collective-permute-start(bf16[1024,128]{1,0:T(8,128)(2,1)S(1)} %collective-permute-done.4.refs_0_), channel_id=1, source_target_pairs={{3,1},{5,3},{7,5},{6,7},{4,6},{2,4},{0,2},{1,0},{9,11},{11,13},{13... | collective-permute-start | bytes 786440 | tf_op jit(solution)/shard_map/ppermute | solution.py:386
  23.8 2.8 %copy-start.1 = (bf16[3456,512]{1,0:T(8,128)(2,1)S(1)}, bf16[3456,512]{1,0:T(8,128)(2,1)}, u32[]{:S(2)}) copy-start(bf16[3456,512]{1,0:T(8,128)(2,1)} %down_ref.1) | copy-start | bytes 10616836
  23.8 3.1 %copy-start.2 = (bf16[512,3456]{1,0:T(8,128)(2,1)S(1)}, bf16[512,3456]{1,0:T(8,128)(2,1)}, u32[]{:S(2)}) copy-start(bf16[512,3456]{1,0:T(8,128)(2,1)} %up_ref.1) | copy-start | bytes 10616836
  30.8 6.2 %collective-permute-start.7 = (bf16[512,128]{1,0:T(8,128)(2,1)S(1)}, bf16[512,128]{1,0:T(8,128)(2,1)S(1)}, u32[]{:S(2)}, u32[]{:S(2)}) collective-permute-start(bf16[512,128]{1,0:T(8,128)(2,1)S(1)} %slice.57), channel_id=1, source_target_pairs={{1,3},{3,5},{5,7},{7,6},{6,4},{4,2},{2,0},{0,1},{11,9},{13,11},{15... | collective-permute-start | bytes 393224 | tf_op jit(solution)/shard_map/ppermute | solution.py:403
  32.7 5.0 %collective-permute-start.8 = (bf16[512,128]{1,0:T(8,128)(2,1)S(1)}, bf16[512,128]{1,0:T(8,128)(2,1)S(1)}, u32[]{:S(2)}, u32[]{:S(2)}) collective-permute-start(bf16[512,128]{1,0:T(8,128)(2,1)S(1)} %slice.58), channel_id=1, source_target_pairs={{3,1},{5,3},{7,5},{6,7},{4,6},{2,4},{0,2},{1,0},{9,11},{11,13},{13... | collective-permute-start | bytes 393224 | tf_op jit(solution)/shard_map/ppermute | solution.py:403
  38.4 1.3 %copy-start.7 = (s32[128]{0:T(128)S(1)}, s32[128]{0:T(128)}, u32[]{:S(2)}) copy-start(s32[128]{0:T(128)} %param.16) | copy-start | bytes 1540
  38.4 2.4 %collective-permute-start.10 = (f32[128,1664]{1,0:T(8,128)S(1)}, f32[128,1664]{1,0:T(8,128)S(1)}, u32[]{:S(2)}, u32[]{:S(2)}) collective-permute-start(f32[128,1664]{1,0:T(8,128)S(1)} %pool.15), channel_id=1, source_target_pairs={{0,8},{8,0},{16,24},{24,16},{1,9},{9,1},{17,25},{25,17},{2,10},{10... | collective-permute-start | bytes 2555912 | tf_op jit(solution)/shard_map/ppermute | solution.py:328
  39.1 2.9 %collective-permute-start.9 = (f32[128,1664]{1,0:T(8,128)S(1)}, f32[128,1664]{1,0:T(8,128)S(1)}, u32[]{:S(2)}, u32[]{:S(2)}) collective-permute-start(f32[128,1664]{1,0:T(8,128)S(1)} %pool.14), channel_id=1, source_target_pairs={{0,8},{8,0},{16,24},{24,16},{1,9},{9,1},{17,25},{25,17},{2,10},{10... | collective-permute-start | bytes 2555912 | tf_op jit(solution)/shard_map/ppermute | solution.py:328
  39.7 2.4 %copy-start.3 = (bf16[128,128]{1,0:T(8,128)(2,1)S(1)}, bf16[128,128]{1,0:T(8,128)(2,1)}, u32[]{:S(2)}) copy-start(bf16[128,128]{1,0:T(8,128)(2,1)} %dense_ref.1) | copy-start | bytes 98308
  39.7 2.4 %copy-start.4 = (f32[3456]{0:T(1024)S(1)}, f32[3456]{0:T(1024)}, u32[]{:S(2)}) copy-start(f32[3456]{0:T(1024)} %param.20) | copy-start | bytes 41476
  39.7 2.4 %copy-start.5 = (f32[3456]{0:T(1024)S(1)}, f32[3456]{0:T(1024)}, u32[]{:S(2)}) copy-start(f32[3456]{0:T(1024)} %param.21) | copy-start | bytes 41476
  39.7 2.4 %copy-start.6 = (f32[128]{0:T(128)S(1)}, f32[128]{0:T(128)}, u32[]{:S(2)}) copy-start(f32[128]{0:T(128)} %param.17) | copy-start | bytes 1540
  46.5 2.7 %collective-permute-start.11 = (bf16[3328,128]{1,0:T(8,128)(2,1)S(1)}, bf16[3328,128]{1,0:T(8,128)(2,1)S(1)}, u32[]{:S(2)}, u32[]{:S(2)}) collective-permute-start(bf16[3328,128]{1,0:T(8,128)(2,1)S(1)} %get-tuple-element.116.refs_1_), channel_id=1, source_target_pairs={{0,8},{8,0},{16,24},{24,16},{1,9},{9,1},{17,25},{25,17},{2,10},{10... | collective-permute-start | bytes 2555912 | tf_op jit(solution)/shard_map/ppermute | solution.py:328
  46.7 2.5 %collective-permute-start.12 = (f32[2,27,128]{2,1,0:T(8,128)S(1)}, f32[2,27,128]{2,1,0:T(8,128)S(1)}, u32[]{:S(2)}, u32[]{:S(2)}) collective-permute-start(f32[2,27,128]{2,1,0:T(8,128)S(1)} %get-tuple-element.97), channel_id=1, source_target_pairs={{0,8},{8,0},{16,24},{24,16},{1,9},{9,1},{17,25},{25,17},{2,10},{10... | collective-permute-start | bytes 82952 | tf_op jit(solution)/shard_map/ppermute | solution.py:328
  51.7 6.0 %collective-permute-start.13 = (bf16[512,128]{1,0:T(8,128)(2,1)S(1)}, bf16[512,128]{1,0:T(8,128)(2,1)S(1)}, u32[]{:S(2)}, u32[]{:S(2)}) collective-permute-start(bf16[512,128]{1,0:T(8,128)(2,1)S(1)} %get-tuple-element.139), channel_id=1, source_target_pairs={{1,3},{3,5},{5,7},{7,6},{6,4},{4,2},{2,0},{0,1},{9,11},{11,13},{13... | collective-permute-start | bytes 393224 | tf_op jit(solution)/shard_map/ppermute | solution.py:441
  53.3 5.3 %collective-permute-start.14 = (bf16[512,128]{1,0:T(8,128)(2,1)S(1)}, bf16[512,128]{1,0:T(8,128)(2,1)S(1)}, u32[]{:S(2)}, u32[]{:S(2)}) collective-permute-start(bf16[512,128]{1,0:T(8,128)(2,1)S(1)} %get-tuple-element.138), channel_id=1, source_target_pairs={{3,1},{5,3},{7,5},{6,7},{4,6},{2,4},{0,2},{1,0},{11,9},{13,11},{15... | collective-permute-start | bytes 393224 | tf_op jit(solution)/shard_map/ppermute | solution.py:441
  58.7 7.5 %collective-permute-start.15 = (bf16[1024,128]{1,0:T(8,128)(2,1)S(1)}, bf16[1024,128]{1,0:T(8,128)(2,1)S(1)}, u32[]{:S(2)}, u32[]{:S(2)}) collective-permute-start(bf16[1024,128]{1,0:T(8,128)(2,1)S(1)} %get-tuple-element.112), channel_id=1, source_target_pairs={{1,3},{3,5},{5,7},{7,6},{6,4},{4,2},{2,0},{0,1},{9,11},{11,13},{13... | collective-permute-start | bytes 786440 | tf_op jit(solution)/shard_map/ppermute | solution.py:441
  60.3 6.9 %collective-permute-start.16 = (bf16[1024,128]{1,0:T(8,128)(2,1)S(1)}, bf16[1024,128]{1,0:T(8,128)(2,1)S(1)}, u32[]{:S(2)}, u32[]{:S(2)}) collective-permute-start(bf16[1024,128]{1,0:T(8,128)(2,1)S(1)} %get-tuple-element.113), channel_id=1, source_target_pairs={{3,1},{5,3},{7,5},{6,7},{4,6},{2,4},{0,2},{1,0},{11,9},{13,11},{15... | collective-permute-start | bytes 786440 | tf_op jit(solution)/shard_map/ppermute | solution.py:441
  60.7 5.4 %collective-permute-start.17 = (f32[2,27,128]{2,1,0:T(8,128)S(1)}, f32[2,27,128]{2,1,0:T(8,128)S(1)}, u32[]{:S(2)}, u32[]{:S(2)}) collective-permute-start(f32[2,27,128]{2,1,0:T(8,128)S(1)} %add.68), channel_id=1, source_target_pairs={{0,16},{8,24},{16,0},{24,8},{1,17},{9,25},{17,1},{25,9},{2,18},{10... | collective-permute-start | bytes 82952 | tf_op jit(solution)/shard_map/ppermute | solution.py:328
  67.3 8.4 %collective-permute-start.18 = (bf16[1024,128]{1,0:T(8,128)(2,1)S(1)}, bf16[1024,128]{1,0:T(8,128)(2,1)S(1)}, u32[]{:S(2)}, u32[]{:S(2)}) collective-permute-start(bf16[1024,128]{1,0:T(8,128)(2,1)S(1)} %get-tuple-element.121), channel_id=1, source_target_pairs={{1,3},{3,5},{5,7},{7,6},{6,4},{4,2},{2,0},{0,1},{9,11},{11,13},{13... | collective-permute-start | bytes 786440 | tf_op jit(solution)/shard_map/ppermute | solution.py:441
  68.9 6.7 %collective-permute-start.19 = (bf16[1024,128]{1,0:T(8,128)(2,1)S(1)}, bf16[1024,128]{1,0:T(8,128)(2,1)S(1)}, u32[]{:S(2)}, u32[]{:S(2)}) collective-permute-start(bf16[1024,128]{1,0:T(8,128)(2,1)S(1)} %get-tuple-element.122), channel_id=1, source_target_pairs={{3,1},{5,3},{7,5},{6,7},{4,6},{2,4},{0,2},{1,0},{11,9},{13,11},{15... | collective-permute-start | bytes 786440 | tf_op jit(solution)/shard_map/ppermute | solution.py:441
  69.4 6.3 %collective-permute-start.20 = (f32[2,27,128]{2,1,0:T(8,128)S(1)}, f32[2,27,128]{2,1,0:T(8,128)S(1)}, u32[]{:S(2)}, u32[]{:S(2)}) collective-permute-start(f32[2,27,128]{2,1,0:T(8,128)S(1)} %add.73), channel_id=1, source_target_pairs={{0,1},{1,0},{2,3},{3,2},{4,5},{5,4},{6,7},{7,6},{8,9},{9,8},{10,11... | collective-permute-start | bytes 82952 | tf_op jit(solution)/shard_map/ppermute | solution.py:328
  75.8 6.8 %collective-permute-start.21 = (bf16[1024,128]{1,0:T(8,128)(2,1)S(1)}, bf16[1024,128]{1,0:T(8,128)(2,1)S(1)}, u32[]{:S(2)}, u32[]{:S(2)}) collective-permute-start(bf16[1024,128]{1,0:T(8,128)(2,1)S(1)} %get-tuple-element.124), channel_id=1, source_target_pairs={{1,3},{3,5},{5,7},{7,6},{6,4},{4,2},{2,0},{0,1},{9,11},{11,13},{13... | collective-permute-start | bytes 786440 | tf_op jit(solution)/shard_map/ppermute | solution.py:441
  76.8 6.4 %collective-permute-start.22 = (bf16[1024,128]{1,0:T(8,128)(2,1)S(1)}, bf16[1024,128]{1,0:T(8,128)(2,1)S(1)}, u32[]{:S(2)}, u32[]{:S(2)}) collective-permute-start(bf16[1024,128]{1,0:T(8,128)(2,1)S(1)} %get-tuple-element.125), channel_id=1, source_target_pairs={{3,1},{5,3},{7,5},{6,7},{4,6},{2,4},{0,2},{1,0},{11,9},{13,11},{15... | collective-permute-start | bytes 786440 | tf_op jit(solution)/shard_map/ppermute | solution.py:441
  77.9 4.7 %collective-permute-start.23 = (f32[2,27,128]{2,1,0:T(8,128)S(1)}, f32[2,27,128]{2,1,0:T(8,128)S(1)}, u32[]{:S(2)}, u32[]{:S(2)}) collective-permute-start(f32[2,27,128]{2,1,0:T(8,128)S(1)} %add.76), channel_id=1, source_target_pairs={{0,2},{1,3},{2,0},{3,1},{4,6},{5,7},{6,4},{7,5},{8,10},{9,11},{10,... | collective-permute-start | bytes 82952 | tf_op jit(solution)/shard_map/ppermute | solution.py:328
  83.3 6.4 %collective-permute-start.24 = (bf16[1024,128]{1,0:T(8,128)(2,1)S(1)}, bf16[1024,128]{1,0:T(8,128)(2,1)S(1)}, u32[]{:S(2)}, u32[]{:S(2)}) collective-permute-start(bf16[1024,128]{1,0:T(8,128)(2,1)S(1)} %fusion.7), channel_id=1, source_target_pairs={{0,16},{8,24},{16,0},{24,8},{1,17},{9,25},{17,1},{25,9},{2,18},{10... | collective-permute-start | bytes 786440 | tf_op jit(solution)/shard_map/ppermute | solution.py:328
  84.9 4.8 %collective-permute-start.25 = (f32[2,27,128]{2,1,0:T(8,128)S(1)}, f32[2,27,128]{2,1,0:T(8,128)S(1)}, u32[]{:S(2)}, u32[]{:S(2)}) collective-permute-start(f32[2,27,128]{2,1,0:T(8,128)S(1)} %add.79), channel_id=1, source_target_pairs={{0,4},{1,5},{2,6},{3,7},{4,0},{5,1},{6,2},{7,3},{8,12},{9,13},{10,... | collective-permute-start | bytes 82952 | tf_op jit(solution)/shard_map/ppermute | solution.py:328
  89.8 2.0 %collective-permute-start.26 = (f32[1024,128]{1,0:T(8,128)S(1)}, f32[1024,128]{1,0:T(8,128)S(1)}, u32[]{:S(2)}, u32[]{:S(2)}) collective-permute-start(f32[1024,128]{1,0:T(8,128)S(1)} %convert_add_fusion.part_ref), channel_id=1, source_target_pairs={{0,8},{8,0},{16,24},{24,16},{1,9},{9,1},{17,25},{25,17},{2,10},{10... | collective-permute-start | bytes 1572872 | tf_op jit(solution)/shard_map/ppermute | solution.py:328
